TPU v7x, 128 devices: a whole 4x4x4 slice. The times are simulated.
128 devices in a mesh: fsdp: 128 (over x, y, z, core).
Axes of the slice: x: 4, y: 4, z: 4, core: 2. Of those that a mesh axis runs over, the one named last changes fastest.
Arguments:
- tokens: bfloat16 [49152, 768], P('fsdp'), may hold values from -6 to 6
- cotangent: bfloat16 [49152, 768], P('fsdp'), may hold values from -6 to 6
- segments: int32 [49152], P('fsdp'), may hold values from 0 to 47, as said below
- counts: int32 [128], P('fsdp'), may hold values from 96 to 384, as said below
- norm_gain: bfloat16 [2, 768], P(None, 'fsdp'), may hold values from 0.5 to 1.5
- in_weight: bfloat16 [2, 768, 3352], P(None, 'fsdp'), may hold values from -0.21875 to 0.21875
- conv_weight: bfloat16 [2, 1792, 4], P(None, 'fsdp'), may hold values from -3 to 3
- conv_bias: bfloat16 [2, 1792], P(None, 'fsdp'), may hold values from -2 to 2
- a_log: float32 [2, 24], replicated, may hold values from 0 to 2.77
- dt_bias: float32 [2, 24], replicated, may hold values from -4 to -1
- skip: float32 [2, 24], replicated, may hold values from 0.5 to 2
- gate_gain: bfloat16 [2, 1536], P(None, 'fsdp'), may hold values from 0.5 to 1.5
- out_weight: bfloat16 [2, 1536, 768], P(None, None, 'fsdp'), may hold values from -0.15625 to 0.15625
Outputs:
- output: bfloat16 [49152, 768], P('fsdp')
- tokens_grad: bfloat16 [49152, 768], P('fsdp')
- norm_gain_grad: float32 [2, 768], P(None, 'fsdp')
- in_weight_grad: float32 [2, 768, 3352], P(None, 'fsdp')
- conv_weight_grad: float32 [2, 1792, 4], P(None, 'fsdp')
- conv_bias_grad: float32 [2, 1792], P(None, 'fsdp')
- a_log_grad: float32 [2, 24], replicated
- dt_bias_grad: float32 [2, 24], replicated
- skip_grad: float32 [2, 24], replicated
- gate_gain_grad: float32 [2, 1536], P(None, 'fsdp')
- out_weight_grad: float32 [2, 1536, 768], P(None, None, 'fsdp')
Inputs may be any that keep to these rules, and one draw needn't show every extreme that they name: `segments`: within each pack of 384 slots the numbers start at 0 and never fall; in every draw some pack holds one single sequence over all its 384 slots, and that pack is wholly live. `counts`: between a quarter and three quarters of a pack's slots are live, except that one or more packs are wholly live in every draw.
All inputs are finite; a program needn't handle non-finite values.
Results may differ from a plain program's by a relative error of at most 0.011.
Values may be sent and summed in bfloat16 or wider, within the bound.
A program may use at most 192 MiB of HBM per device.

v0:
```python
from functools import partial

import jax
import jax.numpy as jnp
from jax import lax
from jax.sharding import PartitionSpec as P

HEADS = 24
HEAD_DIM = 64
STATE = 128
KERNEL = 4
INNER = 1536
CONV_DIM = 1792


epsilon = 1e-05
highest = lax.Precision.HIGHEST


def rms_norm(values, gain):
    return values * lax.rsqrt(jnp.mean(values * values, axis=-1, keepdims=True) + epsilon) * gain


def mixer(segment_ids, projected, params):
    conv_taps, conv_offset, decay_log, step_bias, direct, gated_gain = params
    length = projected.shape[0]
    gate_part = projected[:, :INNER]
    conv_input = projected[:, INNER : INNER + CONV_DIM]
    step_raw = projected[:, INNER + CONV_DIM :]
    convolved = conv_offset + conv_input * conv_taps[:, KERNEL - 1]
    for offset in range(1, KERNEL):
        earlier = jnp.concatenate(
            [jnp.zeros((offset, CONV_DIM), jnp.float32), conv_input[: length - offset]], axis=0
        )
        earlier_ids = jnp.concatenate(
            [jnp.full((offset,), -1, jnp.int32), segment_ids[: length - offset]]
        )
        convolved = (
            convolved
            + jnp.where((earlier_ids == segment_ids)[:, None], earlier, 0.0)
            * conv_taps[:, KERNEL - 1 - offset]
        )
    activated = jax.nn.silu(convolved)
    head_values = activated[:, :INNER].reshape(length, HEADS, HEAD_DIM)
    inputs_b = activated[:, INNER : INNER + STATE]
    outputs_c = activated[:, INNER + STATE :]
    step_size = jax.nn.softplus(step_raw + step_bias)
    log_decay = jnp.cumsum(step_size * -jnp.exp(decay_log), axis=0)
    positions = jnp.arange(length, dtype=jnp.int32)
    linked = (segment_ids[:, None] == segment_ids[None, :]) & (
        positions[:, None] >= positions[None, :]
    )
    decay = jnp.exp(
        jnp.where(linked[:, :, None], log_decay[:, None, :] - log_decay[None, :, :], -10000.0)
    )
    scores = jnp.dot(outputs_c, inputs_b.T, precision=highest)
    weighting = scores[:, :, None] * decay * step_size[None, :, :]
    mixed = (
        jnp.einsum("tsh,shp->thp", weighting, head_values, precision=highest)
        + direct[None, :, None] * head_values
    )
    gated = mixed.reshape(length, INNER) * jax.nn.silu(gate_part)
    return rms_norm(gated, gated_gain)


def contract_rows(left, right):
    return lax.dot_general(
        left, right, (((0,), (0,)), ((), ())), preferred_element_type=jnp.float32
    )


def against_columns(left, right):
    return lax.dot_general(
        left, right, (((1,), (1,)), ((), ())), preferred_element_type=jnp.float32
    )


def local(
    tokens,
    cotangent,
    segments,
    counts,
    norm_gain,
    in_weight,
    conv_weight,
    conv_bias,
    a_log,
    dt_bias,
    skip,
    gate_gain,
    out_weight,
):
    layers = in_weight.shape[0]
    positions = jnp.arange(tokens.shape[0], dtype=jnp.int32)
    live_rows = (positions < counts[0]).astype(jnp.float32)[:, None]
    stream = tokens.astype(jnp.float32)
    stored = []
    for layer_index in range(layers):
        gathered = (
            lax.all_gather(norm_gain[layer_index], "fsdp", axis=0, tiled=True),
            lax.all_gather(in_weight[layer_index], "fsdp", axis=0, tiled=True),
            lax.all_gather(conv_weight[layer_index], "fsdp", axis=0, tiled=True),
            lax.all_gather(conv_bias[layer_index], "fsdp", axis=0, tiled=True),
            lax.all_gather(gate_gain[layer_index], "fsdp", axis=0, tiled=True),
            lax.all_gather(out_weight[layer_index], "fsdp", axis=1, tiled=True),
        )
        first_gain, proj_in, conv_taps, conv_offset, gated_gain, proj_out = gathered
        normed, norm_pull = jax.vjp(rms_norm, stream, first_gain.astype(jnp.float32))
        normed_low = normed.astype(jnp.bfloat16)
        projected = jnp.dot(normed_low, proj_in, preferred_element_type=jnp.float32)
        small = (
            conv_taps.astype(jnp.float32),
            conv_offset.astype(jnp.float32),
            a_log[layer_index],
            dt_bias[layer_index],
            skip[layer_index],
            gated_gain.astype(jnp.float32),
        )
        mixed, mix_pull = jax.vjp(partial(mixer, segments), projected, small)
        mixed_low = mixed.astype(jnp.bfloat16)
        stream = stream + jnp.dot(mixed_low, proj_out, preferred_element_type=jnp.float32)
        stored.append((norm_pull, normed_low, mix_pull, mixed_low, gathered))
    output = (stream * live_rows).astype(jnp.bfloat16)
    gradient = cotangent.astype(jnp.float32) * live_rows
    layer_grads = []
    head_terms = []
    for layer_index in reversed(range(layers)):
        norm_pull, normed_low, mix_pull, mixed_low, gathered = stored[layer_index]
        gathered = (
            lax.all_gather(norm_gain[layer_index], "fsdp", axis=0, tiled=True),
            lax.all_gather(in_weight[layer_index], "fsdp", axis=0, tiled=True),
            lax.all_gather(conv_weight[layer_index], "fsdp", axis=0, tiled=True),
            lax.all_gather(conv_bias[layer_index], "fsdp", axis=0, tiled=True),
            lax.all_gather(gate_gain[layer_index], "fsdp", axis=0, tiled=True),
            lax.all_gather(out_weight[layer_index], "fsdp", axis=1, tiled=True),
        )
        first_gain, proj_in, conv_taps, conv_offset, gated_gain, proj_out = gathered
        grad_low = gradient.astype(jnp.bfloat16)
        out_partial = contract_rows(mixed_low, grad_low)
        mixed_grad = against_columns(grad_low, proj_out)
        projected_grad, small_grads = mix_pull(mixed_grad)
        projected_low = projected_grad.astype(jnp.bfloat16)
        in_partial = contract_rows(normed_low, projected_low)
        normed_grad = against_columns(projected_low, proj_in)
        stream_grad, first_gain_grad = norm_pull(normed_grad)
        gradient = gradient + stream_grad
        taps_grad, offset_grad, decay_grad, step_grad, direct_grad, gated_grad = small_grads
        partials = (first_gain_grad, in_partial, taps_grad, offset_grad, gated_grad, out_partial)
        partials = (
            lax.psum_scatter(first_gain_grad, "fsdp", scatter_dimension=0, tiled=True),
            lax.psum_scatter(in_partial, "fsdp", scatter_dimension=0, tiled=True),
            lax.psum_scatter(taps_grad, "fsdp", scatter_dimension=0, tiled=True),
            lax.psum_scatter(offset_grad, "fsdp", scatter_dimension=0, tiled=True),
            lax.psum_scatter(gated_grad, "fsdp", scatter_dimension=0, tiled=True),
            lax.psum_scatter(out_partial, "fsdp", scatter_dimension=1, tiled=True),
        )
        layer_grads.insert(0, partials)
        head_terms.insert(0, (decay_grad, step_grad, direct_grad))
    stacked = [jnp.stack([entry[member] for entry in layer_grads]) for member in range(6)]
    heads_stacked = [jnp.stack([entry[member] for entry in head_terms]) for member in range(3)]
    decay_total, step_total, direct_total = lax.psum(
        (heads_stacked[0], heads_stacked[1], heads_stacked[2]), "fsdp"
    )
    tokens_grad = gradient.astype(jnp.bfloat16)
    return (
        output,
        tokens_grad,
        stacked[0],
        stacked[1],
        stacked[2],
        stacked[3],
        decay_total,
        step_total,
        direct_total,
        stacked[4],
        stacked[5],
    )


def solution(mesh):
    return jax.shard_map(
        local,
        mesh=mesh,
        in_specs=(
            P("fsdp", None),
            P("fsdp", None),
            P("fsdp"),
            P("fsdp"),
            P(None, "fsdp"),
            P(None, "fsdp", None),
            P(None, "fsdp", None),
            P(None, "fsdp"),
            P(),
            P(),
            P(),
            P(None, "fsdp"),
            P(None, None, "fsdp"),
        ),
        out_specs=(
            P("fsdp", None),
            P("fsdp", None),
            P(None, "fsdp"),
            P(None, "fsdp", None),
            P(None, "fsdp", None),
            P(None, "fsdp"),
            P(),
            P(),
            P(),
            P(None, "fsdp"),
            P(None, None, "fsdp"),
        ),
        check_vma=False,
    )
```

profile of v0, /device:TPU:1, one launch (start us, length us, event | category | flops | bytes accessed | tf_op | source)
XLA Modules:
  0.0 1125.4 jit_solution(3741464324398971671)
XLA Ops:
  15.5 69.4 %all-reduce.56 = (bf16[768]{0:T(1024)(128)(2,1)S(1)}, bf16[1792]{0:T(1024)(128)(2,1)S(1)}, bf16[1536]{0:T(1024)(128)(2,1)S(1)}, bf16[768]{0:T(1024)(128)(2,1)S(1...) all-reduce(bf16[768]{0:T(1024)(128)(2,1)S(1)} %dynamic-update-slice, ...), channel_id=3, replica_groups=mesh['fsdp'=128] {'fsdp'}, use_global_device_ids=true, to_apply=%add.35 | all-reduce | flops 8192 | bytes 32768
  85.8 35.3 %all-gather.3 = bf16[1,1792,4]{2,0,1:T(2,128)(2,1)S(1)} all-gather(bf16[1,14,4]{2,0,1:T(2,128)(2,1)S(1)} %copy.118), channel_id=5, replica_groups=mesh['fsdp'=128] {'fsdp'}, dimensions={1}, use_global_device_ids=true | all-gather | bytes 14448 | tf_op jit(solution)/shard_map/all_gather | solution.py:102
  122.9 34.2 %all-gather.9 = bf16[1,1792,4]{2,0,1:T(2,128)(2,1)S(1)} all-gather(bf16[1,14,4]{2,0,1:T(2,128)(2,1)S(1)} %copy.119), channel_id=11, replica_groups=mesh['fsdp'=128] {'fsdp'}, dimensions={1}, use_global_device_ids=true | all-gather | bytes 14448 | tf_op jit(solution)/shard_map/all_gather | solution.py:102
  166.3 11.7 %copy.96 = bf16[1,1536,768]{2,1,0:T(8,128)(2,1)} copy(bf16[1,1536,768]{1,0,2:T(2,128)(2,1)} %all-gather.19.cloned.1.call-done) | data formatting | bytes 4718592 | tf_op jit(solution)/shard_map/all_gather | solution.py:105
  178.0 11.8 %copy.101 = bf16[1,1536,768]{2,1,0:T(8,128)(2,1)} copy(bf16[1,1536,768]{1,0,2:T(2,128)(2,1)} %all-gather.23.cloned.1.call-done) | data formatting | bytes 4718592 | tf_op jit(solution)/shard_map/all_gather | solution.py:105
  189.8 34.1 %all-gather.17.cloned.1.call-done = bf16[1,768,3352]{2,0,1:T(2,128)(2,1)} async-done(((bf16[1,6,3352]{2,0,1:T(2,128)(2,1)}), bf16[1,768,3352]{2,0,1:T(2,128)(2,1)}) %all-gather.17.cloned.1.call-update) | async-done | bytes 5148688 | tf_op jit(solution)/shard_map/all_gather | solution.py:101
  223.9 23.4 %copy.92 = bf16[1,768,3352]{1,2,0:T(8,128)(2,1)} copy(bf16[1,768,3352]{2,0,1:T(2,128)(2,1)} %all-gather.17.cloned.1.call-done) | data formatting | bytes 10297344 | tf_op jit(solution)/shard_map/all_gather | solution.py:101
  247.3 5.0 fusion.50
  256.4 4.8 fusion.63
  264.9 20.3 %bitcast_add_fusion.3 = f32[384,24,64]{0,2,1:T(8,128)S(1)} fusion(f32[384,24,64]{0,2,1:T(8,128)} %bitcast.279, f32[384,24]{0,1:T(8,128)S(1)} %get-tuple-element.150, f32[384,24]{0,1:T(8,128)S(1)} %bitcast_bitcast_fusion.3, f32[384,384]{1,0:T(8,128)S(1)} %fusion.125, pred[384,384]{1,0:T(8,128)(4,1)S(1)} %fusion.109, f32[24]{0:T(128)S(1)} %get-tuple-element.169), kind=kOutput, calls=%fused_computation.121 | convolution fusion | flops 2733244416 | bytes 5529696 | tf_op jit(solution)/shard_map/jvp(tsh,shp->thp)/dot_general | solution.py:59
  291.2 6.0 all-gather.21.cloned.1.call-done
  297.2 23.2 %copy.97 = bf16[1,768,3352]{1,2,0:T(8,128)(2,1)} copy(bf16[1,768,3352]{2,0,1:T(2,128)(2,1)} %all-gather.21.cloned.1.call-done) | data formatting | bytes 10297344 | tf_op jit(solution)/shard_map/all_gather | solution.py:101
  320.4 5.3 fusion.46
  329.7 5.3 fusion.62
  341.9 19.8 %bitcast_add_fusion.2 = f32[384,24,64]{0,2,1:T(8,128)S(1)} fusion(f32[384,24,64]{0,2,1:T(8,128)} %bitcast.281, f32[384,24]{0,1:T(8,128)} %get-tuple-element.144, f32[384,24]{0,1:T(8,128)S(1)} %bitcast_bitcast_fusion.2, f32[384,384]{1,0:T(8,128)} %fusion.118, pred[384,384]{1,0:T(8,128)(4,1)S(1)} %fusion.109, f32[24]{0:T(128)S(1)} %copy-done.163), kind=kOutput, calls=%fused_computation.114 | convolution fusion | flops 2733244416 | bytes 5529696 | tf_op jit(solution)/shard_map/jvp(tsh,shp->thp)/dot_general | solution.py:59
  366.1 4.0 multiply_reduce_fusion.12
  370.1 19.7 %fusion.17 = (f32[384,24]{0,1:T(8,128)S(1)}, f32[384,24]{0,1:T(8,128)S(1)}, f32[384,24]{0,1:T(8,128)}, f32[384,384]{1,0:T(8,128)S(1)}) fusion(f32[384,24]{0,1:T(8,128)S(1)} %copy-done.63, f32[384,24]{0,1:T(8,128)S(1)} %bitcast_bitcast_fusion.2, f32[384,384]{1,0:T(8,128)S(1)} %copy-done.52, pred[384,384]{1,0:T(8,128)(4,1)S(1)} %fusion.109, ...), kind=kOutput, calls=%fused_computation.21 | convolution fusion | flops 2763740160 | bytes 6230016 | tf_op jit(solution)/shard_map/transpose(jvp(tsh,shp->thp))/dot_general | solution.py:59
  391.2 12.7 %bitcast_add_fusion.1 = f32[384,24,64]{0,2,1:T(8,128)S(1)} fusion(f32[384,24,64]{0,2,1:T(8,128)S(1)} %bitcast.288, f32[24,64,384]{2,1,0:T(8,128)S(1)} %bitcast.289, f32[384,24]{0,1:T(8,128)S(1)} %copy-done.63, f32[384,24]{0,1:T(8,128)S(1)} %bitcast_bitcast_fusion.2, f32[384,384]{1,0:T(8,128)S(1)} %copy-done.52, pred[384,384]{1,0:T(8,128)(4,1)} %copy-done.58, ...), kind=kOutput, calls=%fused_computation.107 | convolution fusion | flops 2733244416 | bytes 7888992 | tf_op jit(solution)/shard_map/transpose(jvp(tsh,shp->thp))/dot_general | solution.py:59
  404.0 5.4 fusion.158
  417.2 4.2 reduce-window.34
  423.1 4.9 multiply_add_fusion.1
  437.4 3.9 multiply_reduce_fusion.13
  441.4 20.5 %fusion.19 = (f32[384,24]{0,1:T(8,128)S(1)}, f32[384,24]{0,1:T(8,128)S(1)}, f32[384,24]{0,1:T(8,128)S(1)}, f32[384,384]{1,0:T(8,128)S(1)}) fusion(f32[384,24]{0,1:T(8,128)S(1)} %copy-done.61, f32[384,24]{0,1:T(8,128)S(1)} %copy-done.112, f32[384,384]{1,0:T(8,128)S(1)} %copy-done.51, pred[384,384]{1,0:T(8,128)(4,1)S(1)} %copy-done.59, ...), kind=kOutput, calls=%fused_computation.23 | convolution fusion | flops 2763740160 | bytes 6230016 | tf_op jit(solution)/shard_map/transpose(jvp(tsh,shp->thp))/dot_general | solution.py:59
  463.3 12.5 %bitcast_add_fusion = f32[384,24,64]{0,2,1:T(8,128)S(1)} fusion(f32[384,24,64]{0,2,1:T(8,128)S(1)} %bitcast.285, f32[24,64,384]{2,1,0:T(8,128)S(1)} %bitcast.286, f32[384,24]{0,1:T(8,128)S(1)} %copy-done.61, f32[384,24]{0,1:T(8,128)S(1)} %copy-done.112, f32[384,384]{1,0:T(8,128)S(1)} %copy-done.51, pred[384,384]{1,0:T(8,128)(4,1)S(1)} %copy-done.59, ...), kind=kOutput, calls=%fused_computation.106 | convolution fusion | flops 2733244416 | bytes 7888992 | tf_op jit(solution)/shard_map/transpose(jvp(tsh,shp->thp))/dot_general | solution.py:59
  475.9 5.3 fusion.157
  489.0 6.9 fusion.156
  495.9 3.9 reduce-window.36
  503.3 4.1 multiply_add_fusion
  507.6 7.5 fusion.100
  516.4 8.9 fusion.130
  527.1 3.8 fusion.113
  530.9 3.7 fusion.110
  534.6 367.5 %fusion.159 = (f32[1536,8]{0,1:T(8,128)}, f32[1536,8]{0,1:T(8,128)}) fusion(f32[1536,768]{0,1:T(8,128)} %fusion.113, f32[1536,768]{0,1:T(8,128)} %fusion.110), kind=kCustom, calls=%all-reduce-scatter.2 | all-reduce-scatter fusion | flops 3145729 | bytes 9535488
  909.4 6.0 collective-permute-start.31
  916.1 3.9 fusion.96
  929.6 11.3 %collective-permute-start.54 = (f32[1536,8]{0,1:T(8,128)S(1)}, f32[1536,8]{0,1:T(8,128)S(1)}, u32[]{:S(2)}, u32[]{:S(2)}) collective-permute-start(f32[1536,8]{0,1:T(8,128)S(1)} %copy-done.54), channel_id=1, source_target_pairs={{0,23},{1,24},{2,25},{3,26},{4,27},{5,28},{6,29},{7,30},{8,31},{9,... | collective-permute-start | bytes 147464
  940.9 5.1 collective-permute-start.53
  946.0 3.5 collective-permute-start.52
  952.2 3.7 collective-permute-start.50
  966.4 3.6 collective-permute-start.44
  973.5 3.7 collective-permute-start.42
  986.2 3.5 collective-permute-start.37
  995.8 4.0 collective-permute-start.34
  1019.2 3.5 collective-permute-start.21
  1047.8 3.7 collective-permute-start.10
  1060.6 3.5 collective-permute-start.5
  1079.7 7.0 concatenate.40
  1086.8 26.3 %concatenate.39 = f32[1536,262]{0,1:T(8,128)S(1)} concatenate(f32[1536,6]{0,1:T(8,128)S(1)} %copy-done.84, f32[1536,8]{0,1:T(8,128)S(1)} %collective-permute-done.30, f32[1536,8]{0,1:T(8,128)S(1)} %collective-permute-done.29, f32[1536,8]{0,1:T(8,128)S(1)} %collective-permute-done.28, f32[1536,8]{0,1:T(8,128)} %copy-done.88, f32[1536,8]{0,1:T(8,128)} %copy-done.89, ...), dimensions={1} | concatenate | bytes 3219456
  (617 shorter events, 206.2 us)
Async XLA Ops:
  7.2 159.1 %all-gather.19.cloned.1.call-start = ((), (), s32[]{:S(2)}) async-start(), calls=%async_computation.1 | async-start | bytes 4755456 | tf_op jit(solution)/shard_map/all_gather | solution.py:105
  8.8 169.3 %all-gather.23.cloned.1.call-start = ((), (), s32[]{:S(2)}) async-start(), calls=%async_computation.3 | async-start | bytes 4755456 | tf_op jit(solution)/shard_map/all_gather | solution.py:105
  9.5 214.4 %all-gather.17.cloned.1.call-start = ((), (), s32[]{:S(2)}) async-start(), calls=%async_computation | async-start | bytes 10699776 | tf_op jit(solution)/shard_map/all_gather | solution.py:101
  11.4 285.8 %all-gather.21.cloned.1.call-start = ((), (), s32[]{:S(2)}) async-start(), calls=%async_computation.2 | async-start | bytes 10699776 | tf_op jit(solution)/shard_map/all_gather | solution.py:101
  12.0 915.6 %all-reduce.61.cloned.1.call-start = ((), (), s32[]{:S(2)}) async-start(), calls=%async_computation.4 | async-start | bytes 202752
  516.4 597.6 %all-reduce.63.cloned.1.call-start = ((), (), s32[]{:S(2)}) async-start(), calls=%async_computation.5 | async-start | bytes 42467328
  902.9 21.0 %collective-permute-start.62 = (f32[1536,8]{0,1:T(8,128)}, f32[1536,8]{0,1:T(8,128)S(1)}, u32[]{:S(2)}, u32[]{:S(2)}) collective-permute-start(f32[1536,8]{0,1:T(8,128)} %get-tuple-element.129), channel_id=1, source_target_pairs={{0,31},{1,32},{2,33},{3,34},{4,35},{5,36},{6,37},{7,38},{8,39},{9,... | collective-permute-start | bytes 147464
  904.1 21.3 %collective-permute-start.61 = (f32[1536,8]{0,1:T(8,128)}, f32[1536,8]{0,1:T(8,128)S(1)}, u32[]{:S(2)}, u32[]{:S(2)}) collective-permute-start(f32[1536,8]{0,1:T(8,128)} %get-tuple-element.129), channel_id=1, source_target_pairs={{0,30},{1,31},{2,32},{3,33},{4,34},{5,35},{6,36},{7,37},{8,38},{9,... | collective-permute-start | bytes 147464
  905.4 22.8 %collective-permute-start.60 = (f32[1536,8]{0,1:T(8,128)}, f32[1536,8]{0,1:T(8,128)}, u32[]{:S(2)}, u32[]{:S(2)}) collective-permute-start(f32[1536,8]{0,1:T(8,128)} %get-tuple-element.129), channel_id=1, source_target_pairs={{0,29},{1,30},{2,31},{3,32},{4,33},{5,34},{6,35},{7,36},{8,37},{9,... | collective-permute-start | bytes 147464
  907.4 13.9 %collective-permute-start.63 = (f32[1536,6]{0,1:T(8,128)S(1)}, f32[1536,6]{0,1:T(8,128)S(1)}, u32[]{:S(2)}, u32[]{:S(2)}) collective-permute-start(f32[1536,6]{0,1:T(8,128)S(1)} %slice.270), channel_id=1, source_target_pairs={{0,32},{1,33},{2,34},{3,35},{4,36},{5,37},{6,38},{7,39},{8,40},{9,... | collective-permute-start | bytes 110600
  909.4 13.1 %collective-permute-start.31 = (f32[1536,6]{0,1:T(8,128)S(1)}, f32[1536,6]{0,1:T(8,128)S(1)}, u32[]{:S(2)}, u32[]{:S(2)}) collective-permute-start(f32[1536,6]{0,1:T(8,128)S(1)} %slice.269), channel_id=1, source_target_pairs={{0,32},{1,33},{2,34},{3,35},{4,36},{5,37},{6,38},{7,39},{8,40},{9,... | collective-permute-start | bytes 110600
  922.6 18.3 %collective-permute-start.58 = (f32[1536,8]{0,1:T(8,128)S(1)}, f32[1536,8]{0,1:T(8,128)S(1)}, u32[]{:S(2)}, u32[]{:S(2)}) collective-permute-start(f32[1536,8]{0,1:T(8,128)S(1)} %copy-done.54), channel_id=1, source_target_pairs={{0,27},{1,28},{2,29},{3,30},{4,31},{5,32},{6,33},{7,34},{8,35},{9,... | collective-permute-start | bytes 147464
  923.9 22.1 %collective-permute-start.57 = (f32[1536,8]{0,1:T(8,128)S(1)}, f32[1536,8]{0,1:T(8,128)S(1)}, u32[]{:S(2)}, u32[]{:S(2)}) collective-permute-start(f32[1536,8]{0,1:T(8,128)S(1)} %copy-done.54), channel_id=1, source_target_pairs={{0,26},{1,27},{2,28},{3,29},{4,30},{5,31},{6,32},{7,33},{8,34},{9,... | collective-permute-start | bytes 147464
  926.1 23.4 %collective-permute-start.56 = (f32[1536,8]{0,1:T(8,128)S(1)}, f32[1536,8]{0,1:T(8,128)S(1)}, u32[]{:S(2)}, u32[]{:S(2)}) collective-permute-start(f32[1536,8]{0,1:T(8,128)S(1)} %copy-done.54), channel_id=1, source_target_pairs={{0,25},{1,26},{2,27},{3,28},{4,29},{5,30},{6,31},{7,32},{8,33},{9,... | collective-permute-start | bytes 147464
  928.3 23.9 %collective-permute-start.55 = (f32[1536,8]{0,1:T(8,128)S(1)}, f32[1536,8]{0,1:T(8,128)S(1)}, u32[]{:S(2)}, u32[]{:S(2)}) collective-permute-start(f32[1536,8]{0,1:T(8,128)S(1)} %copy-done.54), channel_id=1, source_target_pairs={{0,24},{1,25},{2,26},{3,27},{4,28},{5,29},{6,30},{7,31},{8,32},{9,... | collective-permute-start | bytes 147464
  929.6 26.3 %collective-permute-start.54 = (f32[1536,8]{0,1:T(8,128)S(1)}, f32[1536,8]{0,1:T(8,128)S(1)}, u32[]{:S(2)}, u32[]{:S(2)}) collective-permute-start(f32[1536,8]{0,1:T(8,128)S(1)} %copy-done.54), channel_id=1, source_target_pairs={{0,23},{1,24},{2,25},{3,26},{4,27},{5,28},{6,29},{7,30},{8,31},{9,... | collective-permute-start | bytes 147464
  940.9 16.3 %collective-permute-start.53 = (f32[1536,8]{0,1:T(8,128)S(1)}, f32[1536,8]{0,1:T(8,128)S(1)}, u32[]{:S(2)}, u32[]{:S(2)}) collective-permute-start(f32[1536,8]{0,1:T(8,128)S(1)} %copy-done.54), channel_id=1, source_target_pairs={{0,22},{1,23},{2,24},{3,25},{4,26},{5,27},{6,28},{7,29},{8,30},{9,... | collective-permute-start | bytes 147464
  946.0 14.3 %collective-permute-start.52 = (f32[1536,8]{0,1:T(8,128)S(1)}, f32[1536,8]{0,1:T(8,128)S(1)}, u32[]{:S(2)}, u32[]{:S(2)}) collective-permute-start(f32[1536,8]{0,1:T(8,128)S(1)} %copy-done.54), channel_id=1, source_target_pairs={{0,21},{1,22},{2,23},{3,24},{4,25},{5,26},{6,27},{7,28},{8,29},{9,... | collective-permute-start | bytes 147464
  949.5 12.7 %collective-permute-start.51 = (f32[1536,8]{0,1:T(8,128)S(1)}, f32[1536,8]{0,1:T(8,128)S(1)}, u32[]{:S(2)}, u32[]{:S(2)}) collective-permute-start(f32[1536,8]{0,1:T(8,128)S(1)} %copy-done.54), channel_id=1, source_target_pairs={{0,20},{1,21},{2,22},{3,23},{4,24},{5,25},{6,26},{7,27},{8,28},{9,... | collective-permute-start | bytes 147464
  957.2 12.9 %collective-permute-start.48 = (f32[1536,8]{0,1:T(8,128)S(1)}, f32[1536,8]{0,1:T(8,128)S(1)}, u32[]{:S(2)}, u32[]{:S(2)}) collective-permute-start(f32[1536,8]{0,1:T(8,128)S(1)} %copy-done.54), channel_id=1, source_target_pairs={{0,17},{1,18},{2,19},{3,20},{4,21},{5,22},{6,23},{7,24},{8,25},{9,... | collective-permute-start | bytes 147464
  960.3 13.2 %collective-permute-start.47 = (f32[1536,8]{0,1:T(8,128)S(1)}, f32[1536,8]{0,1:T(8,128)S(1)}, u32[]{:S(2)}, u32[]{:S(2)}) collective-permute-start(f32[1536,8]{0,1:T(8,128)S(1)} %copy-done.54), channel_id=1, source_target_pairs={{0,16},{1,17},{2,18},{3,19},{4,20},{5,21},{6,22},{7,23},{8,24},{9,... | collective-permute-start | bytes 147464
  962.2 15.0 %collective-permute-start.46 = (f32[1536,8]{0,1:T(8,128)S(1)}, f32[1536,8]{0,1:T(8,128)S(1)}, u32[]{:S(2)}, u32[]{:S(2)}) collective-permute-start(f32[1536,8]{0,1:T(8,128)S(1)} %copy-done.54), channel_id=1, source_target_pairs={{0,15},{1,16},{2,17},{3,18},{4,19},{5,20},{6,21},{7,22},{8,23},{9,... | collective-permute-start | bytes 147464
  964.5 14.8 %collective-permute-start.45 = (f32[1536,8]{0,1:T(8,128)S(1)}, f32[1536,8]{0,1:T(8,128)S(1)}, u32[]{:S(2)}, u32[]{:S(2)}) collective-permute-start(f32[1536,8]{0,1:T(8,128)S(1)} %copy-done.54), channel_id=1, source_target_pairs={{0,14},{1,15},{2,16},{3,17},{4,18},{5,19},{6,20},{7,21},{8,22},{9,... | collective-permute-start | bytes 147464
  966.4 14.8 %collective-permute-start.44 = (f32[1536,8]{0,1:T(8,128)S(1)}, f32[1536,8]{0,1:T(8,128)S(1)}, u32[]{:S(2)}, u32[]{:S(2)}) collective-permute-start(f32[1536,8]{0,1:T(8,128)S(1)} %copy-done.54), channel_id=1, source_target_pairs={{0,13},{1,14},{2,15},{3,16},{4,17},{5,18},{6,19},{7,20},{8,21},{9,... | collective-permute-start | bytes 147464
  970.1 13.4 %collective-permute-start.43 = (f32[1536,8]{0,1:T(8,128)S(1)}, f32[1536,8]{0,1:T(8,128)S(1)}, u32[]{:S(2)}, u32[]{:S(2)}) collective-permute-start(f32[1536,8]{0,1:T(8,128)S(1)} %copy-done.54), channel_id=1, source_target_pairs={{0,12},{1,13},{2,14},{3,15},{4,16},{5,17},{6,18},{7,19},{8,20},{9,... | collective-permute-start | bytes 147464
  973.5 12.7 %collective-permute-start.42 = (f32[1536,8]{0,1:T(8,128)S(1)}, f32[1536,8]{0,1:T(8,128)S(1)}, u32[]{:S(2)}, u32[]{:S(2)}) collective-permute-start(f32[1536,8]{0,1:T(8,128)S(1)} %copy-done.54), channel_id=1, source_target_pairs={{0,11},{1,12},{2,13},{3,14},{4,15},{5,16},{6,17},{7,18},{8,19},{9,... | collective-permute-start | bytes 147464
  979.3 13.9 %collective-permute-start.40 = (f32[1536,8]{0,1:T(8,128)S(1)}, f32[1536,8]{0,1:T(8,128)S(1)}, u32[]{:S(2)}, u32[]{:S(2)}) collective-permute-start(f32[1536,8]{0,1:T(8,128)S(1)} %copy-done.54), channel_id=1, source_target_pairs={{0,9},{1,10},{2,11},{3,12},{4,13},{5,14},{6,15},{7,16},{8,17},{9,1... | collective-permute-start | bytes 147464
  981.2 14.5 %collective-permute-start.39 = (f32[1536,8]{0,1:T(8,128)S(1)}, f32[1536,8]{0,1:T(8,128)S(1)}, u32[]{:S(2)}, u32[]{:S(2)}) collective-permute-start(f32[1536,8]{0,1:T(8,128)S(1)} %copy-done.54), channel_id=1, source_target_pairs={{0,8},{1,9},{2,10},{3,11},{4,12},{5,13},{6,14},{7,15},{8,16},{9,17... | collective-permute-start | bytes 147464
  983.4 16.4 %collective-permute-start.38 = (f32[1536,8]{0,1:T(8,128)S(1)}, f32[1536,8]{0,1:T(8,128)S(1)}, u32[]{:S(2)}, u32[]{:S(2)}) collective-permute-start(f32[1536,8]{0,1:T(8,128)S(1)} %copy-done.54), channel_id=1, source_target_pairs={{0,7},{1,8},{2,9},{3,10},{4,11},{5,12},{6,13},{7,14},{8,15},{9,16}... | collective-permute-start | bytes 147464
  986.2 15.8 %collective-permute-start.37 = (f32[1536,8]{0,1:T(8,128)S(1)}, f32[1536,8]{0,1:T(8,128)S(1)}, u32[]{:S(2)}, u32[]{:S(2)}) collective-permute-start(f32[1536,8]{0,1:T(8,128)S(1)} %copy-done.54), channel_id=1, source_target_pairs={{0,6},{1,7},{2,8},{3,9},{4,10},{5,11},{6,12},{7,13},{8,14},{9,15},... | collective-permute-start | bytes 147464
  989.7 15.0 %collective-permute-start.36 = (f32[1536,8]{0,1:T(8,128)S(1)}, f32[1536,8]{0,1:T(8,128)S(1)}, u32[]{:S(2)}, u32[]{:S(2)}) collective-permute-start(f32[1536,8]{0,1:T(8,128)S(1)} %copy-done.54), channel_id=1, source_target_pairs={{0,5},{1,6},{2,7},{3,8},{4,9},{5,10},{6,11},{7,12},{8,13},{9,14},{... | collective-permute-start | bytes 147464
  993.2 13.4 %collective-permute-start.35 = (f32[1536,8]{0,1:T(8,128)S(1)}, f32[1536,8]{0,1:T(8,128)S(1)}, u32[]{:S(2)}, u32[]{:S(2)}) collective-permute-start(f32[1536,8]{0,1:T(8,128)S(1)} %copy-done.54), channel_id=1, source_target_pairs={{0,4},{1,5},{2,6},{3,7},{4,8},{5,9},{6,10},{7,11},{8,12},{9,13},{1... | collective-permute-start | bytes 147464
  1016.1 12.8 %collective-permute-start.23 = (f32[1536,8]{0,1:T(8,128)S(1)}, f32[1536,8]{0,1:T(8,128)S(1)}, u32[]{:S(2)}, u32[]{:S(2)}) collective-permute-start(f32[1536,8]{0,1:T(8,128)S(1)} %copy-done.53), channel_id=1, source_target_pairs={{0,24},{1,25},{2,26},{3,27},{4,28},{5,29},{6,30},{7,31},{8,32},{9,... | collective-permute-start | bytes 147464
  1017.4 14.7 %collective-permute-start.22 = (f32[1536,8]{0,1:T(8,128)S(1)}, f32[1536,8]{0,1:T(8,128)S(1)}, u32[]{:S(2)}, u32[]{:S(2)}) collective-permute-start(f32[1536,8]{0,1:T(8,128)S(1)} %copy-done.53), channel_id=1, source_target_pairs={{0,23},{1,24},{2,25},{3,26},{4,27},{5,28},{6,29},{7,30},{8,31},{9,... | collective-permute-start | bytes 147464
  1019.2 14.9 %collective-permute-start.21 = (f32[1536,8]{0,1:T(8,128)S(1)}, f32[1536,8]{0,1:T(8,128)S(1)}, u32[]{:S(2)}, u32[]{:S(2)}) collective-permute-start(f32[1536,8]{0,1:T(8,128)S(1)} %copy-done.53), channel_id=1, source_target_pairs={{0,22},{1,23},{2,24},{3,25},{4,26},{5,27},{6,28},{7,29},{8,30},{9,... | collective-permute-start | bytes 147464
  1022.7 12.7 %collective-permute-start.20 = (f32[1536,8]{0,1:T(8,128)S(1)}, f32[1536,8]{0,1:T(8,128)S(1)}, u32[]{:S(2)}, u32[]{:S(2)}) collective-permute-start(f32[1536,8]{0,1:T(8,128)S(1)} %copy-done.53), channel_id=1, source_target_pairs={{0,21},{1,22},{2,23},{3,24},{4,25},{5,26},{6,27},{7,28},{8,29},{9,... | collective-permute-start | bytes 147464
  1037.7 14.6 %collective-permute-start.14 = (f32[1536,8]{0,1:T(8,128)S(1)}, f32[1536,8]{0,1:T(8,128)S(1)}, u32[]{:S(2)}, u32[]{:S(2)}) collective-permute-start(f32[1536,8]{0,1:T(8,128)S(1)} %copy-done.53), channel_id=1, source_target_pairs={{0,15},{1,16},{2,17},{3,18},{4,19},{5,20},{6,21},{7,22},{8,23},{9,... | collective-permute-start | bytes 147464
  1040.0 13.5 %collective-permute-start.13 = (f32[1536,8]{0,1:T(8,128)S(1)}, f32[1536,8]{0,1:T(8,128)S(1)}, u32[]{:S(2)}, u32[]{:S(2)}) collective-permute-start(f32[1536,8]{0,1:T(8,128)S(1)} %copy-done.53), channel_id=1, source_target_pairs={{0,14},{1,15},{2,16},{3,17},{4,18},{5,19},{6,20},{7,21},{8,22},{9,... | collective-permute-start | bytes 147464
  1041.9 14.4 %collective-permute-start.12 = (f32[1536,8]{0,1:T(8,128)S(1)}, f32[1536,8]{0,1:T(8,128)S(1)}, u32[]{:S(2)}, u32[]{:S(2)}) collective-permute-start(f32[1536,8]{0,1:T(8,128)S(1)} %copy-done.53), channel_id=1, source_target_pairs={{0,13},{1,14},{2,15},{3,16},{4,17},{5,18},{6,19},{7,20},{8,21},{9,... | collective-permute-start | bytes 147464
  1044.6 13.1 %collective-permute-start.11 = (f32[1536,8]{0,1:T(8,128)S(1)}, f32[1536,8]{0,1:T(8,128)S(1)}, u32[]{:S(2)}, u32[]{:S(2)}) collective-permute-start(f32[1536,8]{0,1:T(8,128)S(1)} %copy-done.53), channel_id=1, source_target_pairs={{0,12},{1,13},{2,14},{3,15},{4,16},{5,17},{6,18},{7,19},{8,20},{9,... | collective-permute-start | bytes 147464
  1047.8 12.7 %collective-permute-start.10 = (f32[1536,8]{0,1:T(8,128)S(1)}, f32[1536,8]{0,1:T(8,128)S(1)}, u32[]{:S(2)}, u32[]{:S(2)}) collective-permute-start(f32[1536,8]{0,1:T(8,128)S(1)} %copy-done.53), channel_id=1, source_target_pairs={{0,11},{1,12},{2,13},{3,14},{4,15},{5,16},{6,17},{7,18},{8,19},{9,... | collective-permute-start | bytes 147464
  1053.6 14.3 %collective-permute-start.8 = (f32[1536,8]{0,1:T(8,128)S(1)}, f32[1536,8]{0,1:T(8,128)S(1)}, u32[]{:S(2)}, u32[]{:S(2)}) collective-permute-start(f32[1536,8]{0,1:T(8,128)S(1)} %copy-done.53), channel_id=1, source_target_pairs={{0,9},{1,10},{2,11},{3,12},{4,13},{5,14},{6,15},{7,16},{8,17},{9,1... | collective-permute-start | bytes 147464
  1056.3 15.0 %collective-permute-start.7 = (f32[1536,8]{0,1:T(8,128)S(1)}, f32[1536,8]{0,1:T(8,128)S(1)}, u32[]{:S(2)}, u32[]{:S(2)}) collective-permute-start(f32[1536,8]{0,1:T(8,128)S(1)} %copy-done.53), channel_id=1, source_target_pairs={{0,8},{1,9},{2,10},{3,11},{4,12},{5,13},{6,14},{7,15},{8,16},{9,17... | collective-permute-start | bytes 147464
  1057.7 17.1 %collective-permute-start.6 = (f32[1536,8]{0,1:T(8,128)S(1)}, f32[1536,8]{0,1:T(8,128)S(1)}, u32[]{:S(2)}, u32[]{:S(2)}) collective-permute-start(f32[1536,8]{0,1:T(8,128)S(1)} %copy-done.53), channel_id=1, source_target_pairs={{0,7},{1,8},{2,9},{3,10},{4,11},{5,12},{6,13},{7,14},{8,15},{9,16}... | collective-permute-start | bytes 147464
  1060.6 16.4 %collective-permute-start.5 = (f32[1536,8]{0,1:T(8,128)S(1)}, f32[1536,8]{0,1:T(8,128)S(1)}, u32[]{:S(2)}, u32[]{:S(2)}) collective-permute-start(f32[1536,8]{0,1:T(8,128)S(1)} %copy-done.53), channel_id=1, source_target_pairs={{0,6},{1,7},{2,8},{3,9},{4,10},{5,11},{6,12},{7,13},{8,14},{9,15},... | collective-permute-start | bytes 147464
  1064.8 21.9 %collective-permute-start.4 = (f32[1536,8]{0,1:T(8,128)S(1)}, f32[1536,8]{0,1:T(8,128)}, u32[]{:S(2)}, u32[]{:S(2)}) collective-permute-start(f32[1536,8]{0,1:T(8,128)S(1)} %copy-done.53), channel_id=1, source_target_pairs={{0,5},{1,6},{2,7},{3,8},{4,9},{5,10},{6,11},{7,12},{8,13},{9,14},{... | collective-permute-start | bytes 147464
  1067.9 18.8 %collective-permute-start.3 = (f32[1536,8]{0,1:T(8,128)S(1)}, f32[1536,8]{0,1:T(8,128)}, u32[]{:S(2)}, u32[]{:S(2)}) collective-permute-start(f32[1536,8]{0,1:T(8,128)S(1)} %copy-done.53), channel_id=1, source_target_pairs={{0,4},{1,5},{2,6},{3,7},{4,8},{5,9},{6,10},{7,11},{8,12},{9,13},{1... | collective-permute-start | bytes 147464
  1071.3 15.4 %collective-permute-start.2 = (f32[1536,8]{0,1:T(8,128)S(1)}, f32[1536,8]{0,1:T(8,128)}, u32[]{:S(2)}, u32[]{:S(2)}) collective-permute-start(f32[1536,8]{0,1:T(8,128)S(1)} %copy-done.53), channel_id=1, source_target_pairs={{0,3},{1,4},{2,5},{3,6},{4,7},{5,8},{6,9},{7,10},{8,11},{9,12},{10... | collective-permute-start | bytes 147464
  (193 other events, 4549.4 us)
Sparse Core Ops, SparseCore 0:
  11.0 70.7 all-gather.18
  85.5 64.9 all-gather.22
  154.1 69.8 all-gather.16
  227.4 69.7 all-gather.20
  516.5 143.3 all-reduce.60
  665.4 232.6 all-reduce.62
where the time goes:
time: 1140 us; the launch traced here: 1130 us
  blocking collectives  506 us (44%)
  matrix products  166 us (15%)
  starting transfers between devices  160 us (14%)
  local copies, waits for them, and re-layouts  151 us (13%)
  other arithmetic  83.2 us (7%)
  waiting for transfers between devices  41.6 us (4%)
  between operations  18 us (2%)
    unnamed x2, blocking collectives  437 us
    unnamed x66, starting transfers between devices  160 us
    dot_general x6, matrix products, mixer(): jnp.einsum('tsh,shp->thp', weighting, head_values, precision=highest)  105 us
    all_gather x2, blocking collectives, local(): lax.all_gather(conv_weight[layer_index], 'fsdp', axis=0, tiled=True)  69.5 us
    unnamed x368, local copies, waits for them, and re-layouts  56.1 us
    all_gather x2, local copies, waits for them, and re-layouts, local(): lax.all_gather(in_weight[layer_index], 'fsdp', axis=0, tiled=True)  46.6 us
    all_gather x2, waiting for transfers between devices, local(): lax.all_gather(in_weight[layer_index], 'fsdp', axis=0, tiled=True)  40.1 us
    all_gather x2, local copies, waits for them, and re-layouts, local(): lax.all_gather(out_weight[layer_index], 'fsdp', axis=1, tiled=True)  23.5 us
  transfers between devices with their start and end apart: 70, of which 2 were waited for; matrix products, arithmetic and copies ran while one was open for 48% of the time, Pallas kernels for 0%

commit v1 on v0

v1 whole, which is shorter than its diff:
```python
from functools import partial

import jax
import jax.numpy as jnp
from jax import lax
from jax.experimental import pallas as pl
from jax.experimental.pallas import tpu as pltpu
from jax.sharding import PartitionSpec as P

D = 768
HEADS = 24
STATE = 128
INNER = 1536
CONV = 1792
T = 384
GC = 3328
OUT0 = 3328
STEP0 = 4864
WIDE = 4992
PROJW = 3456
EPS = 1e-05
F32 = jnp.float32
BF = jnp.bfloat16


def nn(a, b):
    return lax.dot_general(a, b, (((1,), (0,)), ((), ())), preferred_element_type=F32)


def nt(a, b):
    return lax.dot_general(a, b, (((1,), (1,)), ((), ())), preferred_element_type=F32)


def tn(a, b):
    return lax.dot_general(a, b, (((0,), (0,)), ((), ())), preferred_element_type=F32)


def iota(shape, dim):
    return lax.broadcasted_iota(jnp.int32, shape, dim)


def ones_where(cond):
    return jnp.where(cond, 1.0, 0.0)


def cols_at(start, width):
    if isinstance(start, int):
        return pl.ds(start, width)
    return pl.ds(pl.multiple_of(start, 128), width)


def sigmoid(v):
    return 1.0 / (1.0 + jnp.exp(-v))


def pack3(v):
    hi = v.astype(BF).astype(F32)
    rest = v - hi
    mid = rest.astype(BF).astype(F32)
    low = rest - mid
    return (hi + pltpu.roll(mid, 32, 1) + pltpu.roll(low, 64, 1)).astype(BF)


def unpack3(v):
    return v + pltpu.roll(v, 96, 1) + pltpu.roll(v, 64, 1)


def head_mask(shape=(T, 128)):
    return iota(shape, 1) < HEADS


def spread_matrix(j, width, shift):
    return ones_where((iota((128, width), 0) & 31) == 4 * j + (iota((128, width), 1) >> shift)).astype(BF)


def rms_normed(stream, gain):
    r = lax.rsqrt(jnp.mean(stream * stream, axis=-1, keepdims=True) + EPS)
    return stream * r * gain


def step_terms(raw, heads_ref):
    mask = head_mask()
    rate = -jnp.exp(heads_ref[0:1, :])
    x = raw + heads_ref[1:2, :]
    x = jnp.where(mask, x, 0.0)
    step = jnp.where(mask, jnp.maximum(x, 0.0) + jnp.log1p(jnp.exp(-jnp.abs(x))), 0.0)
    return rate, x, step


def prepare_scan(raw, heads_ref, step3, log3, log_t):
    rate, x, step = step_terms(raw, heads_ref)
    lower = ones_where(iota((T, T), 0) >= iota((T, T), 1)).astype(BF)
    total = unpack3(nn(lower, pack3(jnp.where(head_mask(), step * rate, 0.0))))
    total = jnp.where(head_mask(), total, 0.0)
    step3[...] = pack3(step)
    log3[...] = pack3(total)
    flipped = jnp.transpose(total)
    for h in range(HEADS):
        log_t[h] = flipped[h : h + 1]
    return rate, x, step


def conv_pass(proj_ref, rows_ref, cols_ref, act_ref):
    masks = [ones_where(cols_ref[:, k : k + 1] == cols_ref[:, 0:1]) for k in range(1, 4)]

    def body(c, carry):
        ci = proj_ref[:, cols_at(INNER + c * 128, 128)]
        here = cols_at(c * 128, 128)
        total = rows_ref[0:1, here] + ci * rows_ref[4:5, here]
        for k in range(1, 4):
            total = total + pltpu.roll(ci, k, 0) * masks[k - 1] * rows_ref[4 - k : 5 - k, here]
        act_ref[:, here] = total * sigmoid(total)
        return carry

    lax.fori_loop(0, 14, body, 0)


def score_pass(act_ref, cols_ref, seg_row_ref, scores, scores_low):
    b = act_ref[:, INNER : INNER + STATE]
    c = act_ref[:, INNER + STATE :]
    s = lax.dot_general(c, b, (((1,), (1,)), ((), ())), precision=lax.Precision.HIGHEST, preferred_element_type=F32)
    linked = (cols_ref[:, 0:1] == seg_row_ref[0:1, :]) & (iota((T, T), 0) >= iota((T, T), 1))
    s = jnp.where(linked, s, 0.0)
    scores[...] = s
    scores_low[...] = s.astype(BF)


def lane_heads(q):
    return (iota((128, 256), 1) >> 6) == q


def block_rows(i):
    return slice(128 * i, 128 * (i + 1))


def scan_chunk_terms(j, act_ref, step3, log3, heads_skip, scores):
    here = cols_at(j * 256, 256)
    x = act_ref[:, here]
    spread = spread_matrix(j, 256, 6)
    step_e = nn(step3[...], spread)
    log_e = nn(log3[...], spread)
    wide = nn(log3[...], spread_matrix(j, 512, 7))
    xd = x * step_e
    return x, step_e, log_e, wide, xd


def decays(i, j, wide, log_t):
    out = []
    for q in range(4):
        row = log_t[4 * j + q, :, block_rows(i)]
        out.append(jnp.exp(jnp.minimum(wide[block_rows(i), 128 * q : 128 * (q + 1)] - row, 0.0)))
    return out


def fwd_kernel(stream_ref, w_ref, rows_ref, heads_ref, skip_ref, cols_ref, seg_row_ref,
               next_ref, proj_ref, mixed_ref, normed_ref,
               act_ref, scores, scores_low, step3, log3, log_t, gated, square, yn):
    normed_ref[...] = rms_normed(stream_ref[...], rows_ref[6:7, 0:D]).astype(BF)

    def project(c, carry):
        here = cols_at(c * 256, 256)
        proj_ref[:, here] = nn(normed_ref[...], w_ref[:, here])
        return carry

    lax.fori_loop(0, 13, project, 0)
    proj_ref[:, GC:] = nn(normed_ref[...], w_ref[:, STEP0:])
    prepare_scan(proj_ref[:, GC:], heads_ref, step3, log3, log_t)
    conv_pass(proj_ref, rows_ref, cols_ref, act_ref)
    score_pass(act_ref, cols_ref, seg_row_ref, scores, scores_low)
    square[...] = jnp.zeros_like(square)

    def chunk(j, carry):
        here = cols_at(j * 256, 256)
        x, step_e, log_e, wide, xd = scan_chunk_terms(j, act_ref, step3, log3, None, scores)
        xd_low = xd.astype(BF)
        for i in range(3):
            rows = block_rows(i)
            sc = scores[rows, rows]
            left = jnp.concatenate([(sc * e).astype(BF) for e in decays(i, j, wide, log_t)], axis=1)
            part = xd_low[rows]
            right = jnp.concatenate([jnp.where(lane_heads(q), part, 0) for q in range(4)], axis=0)
            y = nn(left, right)
            if i:
                edge = log_e[128 * i - 1 : 128 * i, :]
                before = slice(0, 128 * i)
                carried = (xd[before] * jnp.exp(jnp.minimum(edge - log_e[before], 0.0))).astype(BF)
                y = y + jnp.exp(jnp.minimum(log_e[rows] - edge, 0.0)) * nn(scores_low[rows, before], carried)
            mixed = y + skip_ref[0:1, here] * x[rows]
            mixed_ref[rows, here] = mixed
            gate = proj_ref[rows, here]
            u = mixed * (gate * sigmoid(gate))
            gated[rows, here] = u
            uu = u * u
            square[rows, :] += uu[:, :128] + uu[:, 128:]
        return carry

    lax.fori_loop(0, 6, chunk, 0)
    r = lax.rsqrt(jnp.sum(square[...], axis=-1, keepdims=True) * (1.0 / INNER) + EPS)

    def gain(c, carry):
        here = cols_at(c * 256, 256)
        yn[:, here] = (gated[:, here] * r * rows_ref[5:6, here]).astype(BF)
        return carry

    lax.fori_loop(0, 6, gain, 0)
    for n in range(3):
        there = slice(256 * n, 256 * (n + 1))
        next_ref[:, there] = stream_ref[:, there] + nt(yn[...], w_ref[there, OUT0:STEP0])


def bwd_kernel(grad_ref, stream_ref, normed_ref, proj_ref, mixed_ref, w_ref, rows_ref, heads_ref, skip_ref, cols_ref, seg_row_ref,
               prev_ref, g_ref, small_ref,
               act_ref, scores, scores_low, step3, log3, log_t, dyn, dact, dproj, dscores, dlog, dstep, gl, gl_t, sum_u, sum_d, row_skip):
    gl[...] = grad_ref[...].astype(BF)
    gl_t[...] = jnp.transpose(gl[...])
    small_ref[...] = jnp.zeros_like(small_ref)
    sum_u[...] = jnp.zeros_like(sum_u)
    sum_d[...] = jnp.zeros_like(sum_d)
    dscores[...] = jnp.zeros_like(dscores)
    dlog[...] = jnp.zeros_like(dlog)
    dstep[...] = jnp.zeros_like(dstep)

    def first(c, carry):
        here = cols_at(c * 256, 256)
        dy = nn(gl[...], w_ref[:, cols_at(OUT0 + c * 256, 256)])
        dyn[:, here] = dy
        gate = proj_ref[:, here]
        u = mixed_ref[:, here] * (gate * sigmoid(gate))
        uu = u * u
        ud = u * dy * rows_ref[5:6, here]
        sum_u[...] += uu[:, :128] + uu[:, 128:]
        sum_d[...] += ud[:, :128] + ud[:, 128:]
        return carry

    lax.fori_loop(0, 6, first, 0)
    rate, xstep, step = prepare_scan(proj_ref[:, GC:], heads_ref, step3, log3, log_t)
    conv_pass(proj_ref, rows_ref, cols_ref, act_ref)
    score_pass(act_ref, cols_ref, seg_row_ref, scores, scores_low)
    r = lax.rsqrt(jnp.sum(sum_u[...], axis=-1, keepdims=True) * (1.0 / INNER) + EPS)
    pull = r * r * r * (jnp.sum(sum_d[...], axis=-1, keepdims=True) * (1.0 / INNER))
    sum_u[...] = jnp.broadcast_to(r, (T, 128))
    sum_d[...] = jnp.broadcast_to(pull, (T, 128))

    def chunk(j, carry):
        here = cols_at(j * 256, 256)
        r = sum_u[:, 0:1]
        pull = sum_d[:, 0:1]
        x, step_e, log_e, wide, xd = scan_chunk_terms(j, act_ref, step3, log3, None, scores)
        xd_low = xd.astype(BF)
        dy = dyn[:, here]
        gate = proj_ref[:, here]
        mixed = mixed_ref[:, here]
        sg = sigmoid(gate)
        silu = gate * sg
        gain = rows_ref[5:6, here]
        u = mixed * silu
        ur = u * r
        small_ref[5:6, here] = jnp.sum(dy * ur, axis=0, keepdims=True)
        yn = (ur * gain).astype(BF)
        g_ref[:, cols_at(OUT0 + j * 256, 256)] = nn(gl_t[...], yn).astype(BF)
        du = r * (gain * dy) - u * pull
        dproj[:, here] = (du * mixed * (sg * (1.0 + gate * (1.0 - sg)))).astype(BF)
        dm = du * silu
        row_skip[0:1, here] = jnp.sum(dm * x, axis=0, keepdims=True)
        dm_low = dm.astype(BF)
        v_parts, dxd_parts = [], []
        for i in range(3):
            rows = block_rows(i)
            sc = scores[rows, rows]
            es = decays(i, j, wide, log_t)
            ws = [(sc * e).astype(BF) for e in es]
            part, dpart = xd_low[rows], dm_low[rows]
            right = jnp.concatenate([jnp.where(lane_heads(q), part, 0) for q in range(4)], axis=0)
            dright = jnp.concatenate([jnp.where(lane_heads(q), dpart, 0) for q in range(4)], axis=0)
            y = nn(jnp.concatenate(ws, axis=1), right)
            dxd = tn(jnp.concatenate(ws, axis=0), dright)
            g = nt(dright, part)
            ds = g[0:128] * es[0]
            for q in range(1, 4):
                ds = ds + g[128 * q : 128 * (q + 1)] * es[q]
            dscores[rows, rows] += ds
            v_parts.append(dpart.astype(F32) * y - part.astype(F32) * dxd)
            dxd_parts.append(dxd)
        for i in range(1, 3):
            rows = block_rows(i)
            before = slice(0, 128 * i)
            edge = log_e[128 * i - 1 : 128 * i, :]
            fade = jnp.exp(jnp.minimum(edge - log_e[before], 0.0))
            carried = (xd[before] * fade).astype(BF)
            de = (dm[rows] * jnp.exp(jnp.minimum(log_e[rows] - edge, 0.0))).astype(BF)
            z = nn(scores_low[rows, before], carried)
            dz = tn(scores_low[rows, before], de)
            dscores[rows, before] += nt(de, carried)
            v_parts[i] = v_parts[i] + de.astype(F32) * z
            back = carried.astype(F32) * dz
            faded = fade * dz
            for k in range(i):
                v_parts[k] = v_parts[k] - back[block_rows(k)]
                dxd_parts[k] = dxd_parts[k] + faded[block_rows(k)]
        v = jnp.concatenate(v_parts, axis=0)
        dxd = jnp.concatenate(dxd_parts, axis=0)
        dact[:, here] = step_e * dxd + skip_ref[0:1, here] * dm
        gather = ones_where(4 * j + ((iota((512, 128), 0) & 255) >> 6) == iota((512, 128), 1)).astype(BF)

        def head_sums(a):
            hi = a.astype(BF)
            return nn(jnp.concatenate([hi, (a - hi.astype(F32)).astype(BF)], axis=1), gather)

        dlog[...] += head_sums(v)
        dstep[...] += head_sums(x * dxd)
        return carry

    lax.fori_loop(0, 6, chunk, 0)

    linked = (cols_ref[:, 0:1] == seg_row_ref[0:1, :]) & (iota((T, T), 0) >= iota((T, T), 1))
    ds = jnp.where(linked, dscores[...], 0.0).astype(BF)
    b = act_ref[:, INNER : INNER + STATE].astype(BF)
    c = act_ref[:, INNER + STATE :].astype(BF)
    dact[:, INNER : INNER + STATE] = tn(ds, c)
    dact[:, INNER + STATE :] = nn(ds, b)

    upper = ones_where(iota((T, T), 0) <= iota((T, T), 1)).astype(BF)
    dsum = unpack3(nn(upper, pack3(dlog[...])))
    dsum = jnp.where(head_mask(), dsum, 0.0)
    dx = (dstep[...] + rate * dsum) * sigmoid(xstep)
    dx = jnp.where(head_mask(), dx, 0.0)
    dproj[:, GC:] = dx.astype(BF)
    small_ref[7:8, 0:128] = jnp.sum(dsum * step, axis=0, keepdims=True) * jnp.where(head_mask((1, 128)), rate, 0.0)
    small_ref[7:8, 128:256] = jnp.sum(dx, axis=0, keepdims=True)
    which = ones_where((iota((INNER, 128), 0) >> 6) == iota((INNER, 128), 1))
    small_ref[7:8, 256:384] = lax.dot_general(jnp.broadcast_to(row_skip[0:1, :], (8, INNER)), which, (((1,), (0,)), ((), ())),
                                              precision=lax.Precision.HIGHEST, preferred_element_type=F32)[0:1]

    def conv_back(c, carry):
        ci = proj_ref[:, cols_at(INNER + c * 128, 128)]
        here = cols_at(c * 128, 128)
        taps = [rows_ref[4 - k : 5 - k, here] for k in range(4)]
        masks = [ones_where(cols_ref[:, k : k + 1] == cols_ref[:, 0:1]) for k in range(1, 7)]
        shifted = [ci] + [pltpu.roll(ci, k, 0) * masks[k - 1] for k in range(1, 4)]
        total = rows_ref[0:1, here] + ci * taps[0]
        for k in range(1, 4):
            total = total + shifted[k] * taps[k]
        sg = sigmoid(total)
        dc = dact[:, here] * (sg * (1.0 + total * (1.0 - sg)))
        small_ref[0:1, here] = jnp.sum(dc, axis=0, keepdims=True)
        dci = dc * taps[0]
        for k in range(4):
            small_ref[4 - k : 5 - k, here] = jnp.sum(dc * shifted[k], axis=0, keepdims=True)
            if k:
                dci = dci + pltpu.roll(dc, T - k, 0) * masks[k + 2] * taps[k]
        dproj[:, cols_at(INNER + c * 128, 128)] = dci.astype(BF)
        return carry

    lax.fori_loop(0, 14, conv_back, 0)

    gl_t[...] = jnp.transpose(normed_ref[...])

    def in_grad(c, carry):
        here = cols_at(c * 256, 256)
        g_ref[:, here] = nn(gl_t[...], dproj[:, here]).astype(BF)
        return carry

    lax.fori_loop(0, 13, in_grad, 0)
    g_ref[:, STEP0:] = nn(gl_t[...], dproj[:, GC:]).astype(BF)
    for n in range(3):
        there = slice(256 * n, 256 * (n + 1))
        dyn[:, there] = nt(dproj[:, :GC], w_ref[there, :GC]) + nt(dproj[:, GC:], w_ref[there, STEP0:])
    dn = dyn[:, 0:D]
    stream = stream_ref[...]
    gain = rows_ref[6:7, 0:D]
    r = lax.rsqrt(jnp.mean(stream * stream, axis=-1, keepdims=True) + EPS)
    small_ref[6:7, 0:D] = jnp.sum(dn * stream * r, axis=0, keepdims=True)
    gd = gain * dn
    prev_ref[...] = grad_ref[...] + r * gd - stream * (r * r * r * jnp.mean(stream * gd, axis=-1, keepdims=True))


def vm(count):
    return [pl.BlockSpec(memory_space=pltpu.VMEM)] * count


PARAMS = dict(vmem_limit_bytes=60 * 1024 * 1024)


def scan_scratch():
    return [
        pltpu.VMEM((T, CONV), F32),
        pltpu.VMEM((T, T), F32),
        pltpu.VMEM((T, T), BF),
        pltpu.VMEM((T, 128), BF),
        pltpu.VMEM((T, 128), BF),
        pltpu.VMEM((HEADS, 1, T), F32),
    ]


def layer_forward(stream, w, rows, heads, skip, cols, seg_row):
    return pl.pallas_call(
        fwd_kernel,
        out_shape=(
            jax.ShapeDtypeStruct((T, D), F32),
            jax.ShapeDtypeStruct((T, PROJW), F32),
            jax.ShapeDtypeStruct((T, INNER), F32),
            jax.ShapeDtypeStruct((T, D), BF),
        ),
        in_specs=vm(7),
        out_specs=tuple(vm(4)),
        scratch_shapes=scan_scratch()
        + [pltpu.VMEM((T, INNER), F32), pltpu.VMEM((T, 128), F32), pltpu.VMEM((T, INNER), BF)],
        compiler_params=pltpu.CompilerParams(**PARAMS),
        name="layer_forward",
    )(stream, w, rows, heads, skip, cols, seg_row)


def layer_backward(grad, stream, normed, proj, mixed, w, rows, heads, skip, cols, seg_row):
    return pl.pallas_call(
        bwd_kernel,
        out_shape=(
            jax.ShapeDtypeStruct((T, D), F32),
            jax.ShapeDtypeStruct((D, WIDE), BF),
            jax.ShapeDtypeStruct((8, CONV), F32),
        ),
        in_specs=vm(11),
        out_specs=tuple(vm(3)),
        scratch_shapes=scan_scratch()
        + [
            pltpu.VMEM((T, INNER), F32),
            pltpu.VMEM((T, CONV), F32),
            pltpu.VMEM((T, PROJW), BF),
            pltpu.VMEM((T, T), F32),
            pltpu.VMEM((T, 128), F32),
            pltpu.VMEM((T, 128), F32),
            pltpu.VMEM((T, D), BF),
            pltpu.VMEM((D, T), BF),
            pltpu.VMEM((T, 128), F32),
            pltpu.VMEM((T, 128), F32),
            pltpu.VMEM((8, INNER), F32),
        ],
        compiler_params=pltpu.CompilerParams(**PARAMS),
        name="layer_backward",
    )(grad, stream, normed, proj, mixed, w, rows, heads, skip, cols, seg_row)


def wide_shard(in_weight, out_weight):
    pad = jnp.zeros((in_weight.shape[0], WIDE - STEP0 - HEADS), BF)
    return jnp.concatenate([in_weight[:, :GC], out_weight.T, in_weight[:, GC:], pad], axis=1)


def local(tokens, cotangent, segments, counts, norm_gain, in_weight, conv_weight, conv_bias, a_log, dt_bias, skip, gate_gain, out_weight):
    layers = in_weight.shape[0]
    me = lax.axis_index("fsdp")
    seg = segments.astype(F32)
    ahead = [jnp.concatenate([jnp.full((k,), -1.0, F32), seg[: T - k]]) for k in range(1, 4)]
    after = [jnp.concatenate([seg[k:], jnp.full((k,), -1.0, F32)]) for k in range(1, 4)]
    live = (jnp.arange(T, dtype=jnp.int32) < counts[0]).astype(F32)
    cols = jnp.stack([seg] + ahead + after + [live], axis=1)
    seg_row = seg[None, :]
    small = jnp.concatenate([conv_bias[:, :, None], conv_weight], axis=2).reshape(layers, -1)
    small = lax.all_gather(jnp.concatenate([small, gate_gain, norm_gain], axis=1), "fsdp", axis=0)
    widths = (CONV // 128 * 5, INNER // 128, D // 128)
    stream = tokens.astype(F32)
    kept = []
    for l in range(layers):
        w = lax.all_gather(wide_shard(in_weight[l], out_weight[l]), "fsdp", axis=0, tiled=True)
        part = small[:, l, :].astype(F32)
        conv = part[:, : widths[0]].reshape(CONV, 5).T
        gate = part[:, widths[0] : widths[0] + widths[1]].reshape(1, INNER)
        norm = part[:, widths[0] + widths[1] :].reshape(1, D)
        rows = jnp.concatenate([conv, jnp.pad(gate, ((0, 0), (0, CONV - INNER))), jnp.pad(norm, ((0, 0), (0, CONV - D))), jnp.zeros((1, CONV), F32)])
        heads = jnp.pad(jnp.stack([a_log[l], dt_bias[l], skip[l]]), ((0, 5), (0, 128 - HEADS)))
        wide_skip = jnp.repeat(skip[l], 64)[None, :]
        shared = (w, rows, heads, wide_skip, cols, seg_row)
        following, proj, mixed, normed = layer_forward(stream, *shared)
        kept.append((stream, normed, proj, mixed) + shared)
        stream = following
    output = (stream * live[:, None]).astype(BF)
    gradient = cotangent.astype(F32) * live[:, None]
    wide_grads, small_grads = [None] * layers, [None] * layers
    for l in reversed(range(layers)):
        gradient, wide, small_grads[l] = layer_backward(gradient, *kept[l])
        wide_grads[l] = lax.psum_scatter(wide, "fsdp", scatter_dimension=0, tiled=True).astype(F32)
    total = lax.psum(jnp.stack(small_grads), "fsdp")
    wide = jnp.stack(wide_grads)
    conv = lax.dynamic_slice_in_dim(total[:, 0:5], me * 14, 14, axis=2)
    gate = lax.dynamic_slice_in_dim(total[:, 5], me * 12, 12, axis=1)
    norm = lax.dynamic_slice_in_dim(total[:, 6], me * 6, 6, axis=1)
    return (
        output,
        gradient.astype(BF),
        norm,
        jnp.concatenate([wide[:, :, :GC], wide[:, :, STEP0 : STEP0 + HEADS]], axis=2),
        jnp.transpose(conv[:, 1:5], (0, 2, 1)),
        conv[:, 0],
        total[:, 7, 0:HEADS],
        total[:, 7, 128 : 128 + HEADS],
        total[:, 7, 256 : 256 + HEADS],
        gate,
        jnp.transpose(wide[:, :, OUT0:STEP0], (0, 2, 1)),
    )


def solution(mesh):
    axis = P("fsdp")
    rows, second, third = P("fsdp", None), P(None, "fsdp"), P(None, None, "fsdp")
    middle = P(None, "fsdp", None)
    return jax.shard_map(
        local,
        mesh=mesh,
        in_specs=(rows, rows, axis, axis, second, middle, middle, second, P(), P(), P(), second, third),
        out_specs=(rows, rows, second, middle, middle, second, P(), P(), P(), second, third),
        check_vma=False,
    )
```

time: 1140 us -> 615 us (0.54); the launches traced: 1130 us -> 614 us
  blocking collectives: 506 us -> 34.4 us
  waiting for transfers between devices: 41.6 us -> 375 us
  matrix products: 166 us -> 0 us
  starting transfers between devices: 160 us -> 0.16 us
  Pallas kernels: 0 us -> 133 us
  local copies, waits for them, and re-layouts: 151 us -> 46.5 us
  other arithmetic: 83.2 us -> 9.75 us
    unnamed x2 -> x0, blocking collectives: 437 us -> none
    unnamed x72 -> x5, waiting for transfers between devices: 1.48 us -> 172 us
    dot_general x24 -> x0, matrix products: 166 us -> none  [the longest x6 105 us: mixer(): jnp.einsum('tsh,shp->thp', weighting, head_values, precision=highest)]
    unnamed x66 -> x1, starting transfers between devices: 160 us -> 0.04 us
    psum x0 -> x1, waiting for transfers between devices: none -> 135 us  [local(): total = lax.psum(jnp.stack(small_grads), 'fsdp')]
    pallas_call x0 -> x4, Pallas kernels: none -> 133 us  [the longest x2 91.1 us: layer_backward(): pl.pallas_call(bwd_kernel, out_shape=(jax.ShapeDtypeStruct((T, D), F32),...]
    all_gather x4 -> x0, local copies, waits for them, and re-layouts: 70.2 us -> none  [the longest x2 46.6 us: local(): lax.all_gather(in_weight[layer_index], 'fsdp', axis=0, tiled=True)]
    all_gather x2 -> x1, blocking collectives: 69.5 us -> 34.4 us  [local(): lax.all_gather(jnp.concatenate([small, gate_gain, norm_gain], axis=1), 'f...]
  transfers between devices with their start and end apart: 70 -> 4, of which waited for: 2 -> 4; matrix products, arithmetic and copies ran while one was open for 48% -> 5% of each run, Pallas kernels for 0% -> 3%
where the time goes in v1:
time: 615 us; the launch traced here: 614 us
  waiting for transfers between devices  375 us (61%)
  Pallas kernels  133 us (22%)
  local copies, waits for them, and re-layouts  46.5 us (8%)
  blocking collectives  34.4 us (6%)
  between operations  14.7 us (2%)
  other arithmetic  9.75 us (2%)
    unnamed x5, waiting for transfers between devices  172 us
    psum x1, waiting for transfers between devices, local(): total = lax.psum(jnp.stack(small_grads), 'fsdp')  135 us
    pallas_call x2, Pallas kernels, layer_backward(): pl.pallas_call(bwd_kernel, out_shape=(jax.ShapeDtypeStruct((T, D), F32),...  91.1 us
    all_gather x2, waiting for transfers between devices, local(): lax.all_gather(wide_shard(in_weight[l], out_weight[l]), 'fsdp', axis=0, t...  67.6 us
    pallas_call x2, Pallas kernels, layer_forward(): pl.pallas_call(fwd_kernel, out_shape=(jax.ShapeDtypeStruct((T, D), F32),...  42.4 us
    all_gather x1, blocking collectives, local(): lax.all_gather(jnp.concatenate([small, gate_gain, norm_gain], axis=1), 'f...  34.4 us
    unnamed x20, local copies, waits for them, and re-layouts  28.5 us
  transfers between devices with their start and end apart: 4, of which 4 were waited for; matrix products, arithmetic and copies ran while one was open for 5% of the time, Pallas kernels for 3%

profile of v1, /device:TPU:1, one launch (start us, length us, event | category | flops | bytes accessed | tf_op | source)
XLA Modules:
  0.0 614.0 jit_solution(12110109944902609068)
XLA Ops:
  7.2 1.1 fusion.7
  8.4 0.9 fusion.8
  9.4 0.7 concatenate.39
  10.2 0.7 concatenate.49
  11.0 0.7 copy.46
  11.7 0.7 pad_maximum_fusion.2
  12.6 0.8 maximum_bitcast_fusion
  13.3 34.4 %all-gather.2 = bf16[128,2,88]{2,1,0:T(2,128)(2,1)S(1)} all-gather(bf16[1,2,88]{2,1,0:T(2,128)(2,1)S(1)} %maximum_bitcast_fusion), channel_id=2, replica_groups=mesh['fsdp'=128] {'fsdp'}, dimensions={0}, use_global_device_ids=true | all-gather | bytes 45408 | tf_op jit(solution)/shard_map/all_gather | solution.py:457
  48.1 0.6 broadcast_in_dim.16.seg_row_ref
  49.4 1.1 convert_element_type.51.stream_ref
  50.5 0.1 reshape.66
  50.6 0.1 reshape.65
  50.7 0.3 reshape.64
  51.0 0.3 copy.52
  51.3 0.2 reshape.63
  51.6 0.3 reshape.61
  51.9 0.3 copy.48
  52.3 0.7 broadcast_in_dim_reshape.6.skip_ref
  53.5 0.8 copy.49.cols_ref
  54.4 0.7 broadcast_in_dim_reshape.7.skip_ref
  55.2 0.6 select_maximum_fusion.6.heads_ref
  55.8 0.6 select_maximum_fusion.4.heads_ref
  56.4 0.7 fusion
  57.1 29.3 %all-gather.7.cloned.1.call-done = bf16[128,6,4992]{2,1,0:T(8,128)(2,1)} async-done(((bf16[1,6,4992]{2,1,0:T(8,128)(2,1)}), bf16[128,6,4992]{2,1,0:T(8,128)(2,1)}) %all-gather.7.cloned.1.call-update) | async-done | bytes 7667728 | tf_op jit(solution)/shard_map/all_gather | solution.py:462
  86.4 13.1 %reshape.71.w_ref = bf16[768,4992]{1,0:T(8,128)(2,1)} reshape(bf16[128,6,4992]{2,1,0:T(8,128)(2,1)} %all-gather.7.cloned.1.call-done) | data formatting | bytes 15335424
  99.6 21.2 %layer_forward.2 = (f32[384,768]{1,0:T(8,128)}, f32[384,3456]{1,0:T(8,128)}, f32[384,1536]{1,0:T(8,128)}, bf16[384,768]{1,0:T(8,128)(2,1)}) custom-call(f32[384,768]{1,0:T(8,128)} %convert_element_type.51.stream_ref, bf16[768,4992]{1,0:T(8,128)(2,1)} %reshape.71.w_ref, f32[8,1792]{1,0:T(8,128)} %get-tuple-element.102.rows_ref, ...), custom_call_target="tpu_custom_call" | custom-call | tf_op jit(solution)/shard_map/layer_forward/pallas_call | solution.py:396
  120.8 38.2 %all-gather.9.cloned.1.call-done = bf16[128,6,4992]{2,1,0:T(8,128)(2,1)} async-done(((bf16[1,6,4992]{2,1,0:T(8,128)(2,1)}), bf16[128,6,4992]{2,1,0:T(8,128)(2,1)}) %all-gather.9.cloned.1.call-update) | async-done | bytes 7667728 | tf_op jit(solution)/shard_map/all_gather | solution.py:462
  159.1 13.1 %reshape.75.w_ref = bf16[768,4992]{1,0:T(8,128)(2,1)} reshape(bf16[128,6,4992]{2,1,0:T(8,128)(2,1)} %all-gather.9.cloned.1.call-done) | data formatting | bytes 15335424
  172.2 21.2 %layer_forward.3 = (f32[384,768]{1,0:T(8,128)}, f32[384,3456]{1,0:T(8,128)}, f32[384,1536]{1,0:T(8,128)}, bf16[384,768]{1,0:T(8,128)(2,1)}) custom-call(f32[384,768]{1,0:T(8,128)} %get-tuple-element.25.stream_ref, bf16[768,4992]{1,0:T(8,128)(2,1)} %reshape.75.w_ref, f32[8,1792]{1,0:T(8,128)} %get-tuple-element.101.rows_ref, ...), custom_call_target="tpu_custom_call" | custom-call | tf_op jit(solution)/shard_map/layer_forward/pallas_call | solution.py:396
  193.3 2.7 convert_multiply_fusion
  196.0 45.5 %layer_backward.2 = (f32[384,768]{1,0:T(8,128)}, bf16[768,4992]{1,0:T(8,128)(2,1)}, f32[8,1792]{1,0:T(8,128)}) custom-call(f32[384,768]{1,0:T(8,128)} %get-tuple-element.85.grad_ref, f32[384,768]{1,0:T(8,128)} %get-tuple-element.25.stream_ref, bf16[384,768]{1,0:T(8,128)(2,1)} %get-tuple-element.27.normed_ref, f32[384,3456]{1,0:T(8,128)} %get-tuple-element.28.proj_ref, ...), custom_call_target="tpu_custom_call" | custom-call | tf_op jit(solution)/shard_map/layer_backward/pallas_call | solution.py:414
  241.5 45.6 %layer_backward.3 = (f32[384,768]{1,0:T(8,128)}, bf16[768,4992]{1,0:T(8,128)(2,1)}, f32[8,1792]{1,0:T(8,128)}) custom-call(f32[384,768]{1,0:T(8,128)} %get-tuple-element.30.grad_ref, f32[384,768]{1,0:T(8,128)} %convert_element_type.51.stream_ref, bf16[384,768]{1,0:T(8,128)(2,1)} %get-tuple-element.31.normed_ref, f32[384,3456]{1,0:T(8,128)} %get-tuple-element.32.proj_ref, ...), custom_call_target="tpu_custom_call" | custom-call | tf_op jit(solution)/shard_map/layer_backward/pallas_call | solution.py:414
  287.1 1.5 pad_maximum_fusion.1
  288.7 0.5 all-reduce.18.cloned.1.call-update
  289.2 0.7 copy-done
  289.9 0.9 convert_element_type.61
  290.8 135.0 %all-reduce.16.cloned.1.call-done = f32[2,8,1792]{2,1,0:T(8,128)} async-done(((f32[2,8,1792]{2,1,0:T(8,128)}), f32[2,8,1792]{2,1,0:T(8,128)}) %all-reduce.16.cloned.1.call-update) | async-done | bytes 114704 | tf_op jit(solution)/shard_map/psum | solution.py:480
  425.8 1.0 fusion.5
  426.8 0.6 constant_dynamic-slice_fusion.2
  427.4 1.4 constant_dynamic-slice_fusion.1
  428.8 0.6 constant_dynamic-slice_fusion
  429.4 1.4 dynamic-slice_bitcast_fusion.2
  430.8 1.3 fusion.6
  432.1 171.9 %all-reduce.18.cloned.1.call-done = (bf16[768,4992]{1,0:T(8,128)(2,1)}, bf16[768,4992]{1,0:T(8,128)(2,1)}) async-done(((bf16[768,4992]{1,0:T(8,128)(2,1)}, bf16[768,4992]{1,0:T(8,128)(2,1)}), (bf16[768,4992]{1,0:T(8,128)(2,1)}, bf16[768,4992]{1,0:T(8,128)(2,1)})) %all-reduce.18.cloned.1.call-update) | async-done | bytes 15335440
  604.0 0.9 dynamic-slice_bitcast_fusion
  605.0 1.0 dynamic-slice_bitcast_fusion.1
  606.1 0.8 copy.56
  606.8 0.7 copy.57
  (66 shorter events, 1.9 us)
Async XLA Ops:
  7.2 40.9 %copy-start.4 = (s32[384]{0:T(512)S(1)}, s32[384]{0:T(512)}, u32[]{:S(2)}) copy-start(s32[384]{0:T(512)} %param.15) | copy-start | bytes 4612
  7.2 42.2 %copy-start.1 = (bf16[384,768]{1,0:T(8,128)(2,1)S(1)}, bf16[384,768]{1,0:T(8,128)(2,1)}, u32[]{:S(2)}) copy-start(bf16[384,768]{1,0:T(8,128)(2,1)} %param.13) | copy-start | bytes 1769476
  7.2 79.2 %all-gather.7.cloned.1.call-start = ((), (), s32[]{:S(2)}) async-start(), calls=%async_computation.1 | async-start | bytes 10303488 | tf_op jit(solution)/shard_map/all_gather | solution.py:462
  10.1 148.9 %all-gather.9.cloned.1.call-start = ((), (), s32[]{:S(2)}) async-start(), calls=%async_computation.2 | async-start | bytes 10303488 | tf_op jit(solution)/shard_map/all_gather | solution.py:462
  10.9 414.8 %all-reduce.16.cloned.1.call-start = ((), (), s32[]{:S(2)}) async-start(), calls=%async_computation | async-start | bytes 229376 | tf_op jit(solution)/shard_map/psum | solution.py:480
  50.5 1.7 copy-start.5
  50.5 1.7 copy-start.6
  50.5 4.7 copy-start.7
  172.2 21.2 %copy-start.2 = (bf16[384,768]{1,0:T(8,128)(2,1)S(1)}, bf16[384,768]{1,0:T(8,128)(2,1)}, u32[]{:S(2)}) copy-start(bf16[384,768]{1,0:T(8,128)(2,1)} %param.14) | copy-start | bytes 1769476
  241.5 45.6 %copy-start.3 = (f32[8,1792]{1,0:T(8,128)S(1)}, f32[8,1792]{1,0:T(8,128)}, u32[]{:S(2)}) copy-start(f32[8,1792]{1,0:T(8,128)} %get-tuple-element.36) | copy-start | bytes 172036
  288.6 315.4 %all-reduce.18.cloned.1.call-start = ((), (), s32[]{:S(2)}) async-start(), calls=%async_computation.3 | async-start | bytes 30670848
  288.7 1.3 copy-start
Sparse Core Ops, SparseCore 0:
  11.5 74.9 all-gather.6
  89.9 69.1 all-gather.8
  288.7 137.0 all-reduce.15
  431.6 172.3 all-reduce.17

commit v2 on v0

v2 whole, which is shorter than its diff:
```python
from functools import partial

import jax
import jax.numpy as jnp
from jax import lax
from jax.experimental import pallas as pl
from jax.experimental.pallas import tpu as pltpu
from jax.sharding import PartitionSpec as P

D = 768
HEADS = 24
STATE = 128
INNER = 1536
CONV = 1792
T = 384
STEP = 1792
USED = 1920
SMALL = 1920
REST = 2048
EPS = 1e-05
F32 = jnp.float32
BF = jnp.bfloat16
HIGHEST = lax.Precision.HIGHEST
MESH = pl.DeviceIdType.MESH


def nn(a, b):
    return lax.dot_general(a, b, (((1,), (0,)), ((), ())), preferred_element_type=F32)


def nt(a, b):
    return lax.dot_general(a, b, (((1,), (1,)), ((), ())), preferred_element_type=F32)


def tn(a, b):
    return lax.dot_general(a, b, (((0,), (0,)), ((), ())), preferred_element_type=F32)


def exact(a, b):
    return lax.dot_general(a, b, (((1,), (0,)), ((), ())), precision=HIGHEST, preferred_element_type=F32)


def iota(shape, dim):
    return lax.broadcasted_iota(jnp.int32, shape, dim)


def ones_where(cond):
    return jnp.where(cond, 1.0, 0.0)


def tiles(start, width):
    if isinstance(start, int):
        return pl.ds(start, width)
    return pl.ds(pl.multiple_of(start, 128), width)


def sigmoid(v):
    return 1.0 / (1.0 + jnp.exp(-v))


def weight(w, cols):
    v = w[:, :, :, cols]
    return v.reshape(D, v.shape[-1])


def put_rows(g, cols, v):
    g[:, :, :, cols] = v.astype(BF).reshape(4, 4, 48, v.shape[-1])


def pack3(v):
    hi = v.astype(BF).astype(F32)
    rest = v - hi
    mid = rest.astype(BF).astype(F32)
    low = rest - mid
    return (hi + pltpu.roll(mid, 32, 1) + pltpu.roll(low, 64, 1)).astype(BF)


def unpack3(v):
    return v + pltpu.roll(v, 96, 1) + pltpu.roll(v, 64, 1)


def head_mask(shape=(T, 128)):
    return iota(shape, 1) < HEADS


def spread_matrix(j, width, shift):
    return ones_where((iota((128, width), 0) & 31) == 4 * j + (iota((128, width), 1) >> shift)).astype(BF)


UNITS = ((14, 4682), (12, 5462), (6, 10923))


def small_rows(w_rest, heads, rows, skip):
    pick = ones_where(iota((128, D), 1) == 6 * iota((128, D), 0)).astype(BF)
    held = nn(pick, weight(w_rest, tiles(SMALL, 128))).astype(BF)

    def row(entries, magic, offset, width):
        c = iota((128, width), 1)
        unit = (c * magic) >> 16
        spread = ones_where(iota((128, width), 0) == offset + c - unit * entries).astype(BF)
        return jnp.sum(jnp.where(unit == iota((128, width), 0), nn(held, spread), 0.0), axis=0, keepdims=True)

    for n in range(5):
        rows[n : n + 1, :] = row(*UNITS[0], 14 * n, CONV)
    rows[5:6, 0:INNER] = row(*UNITS[1], 70, INNER)
    rows[6:7, 0:D] = row(*UNITS[2], 82, D)
    which = ones_where((iota((128, INNER), 1) >> 6) == iota((128, INNER), 0))
    skip[...] = exact(heads[...], which)


def rms_normed(stream, gain):
    r = lax.rsqrt(jnp.mean(stream * stream, axis=-1, keepdims=True) + EPS)
    return stream * r * gain


def step_terms(raw, heads):
    mask = head_mask()
    rate = -jnp.exp(heads[0:1, :])
    x = jnp.where(mask, raw + heads[1:2, :], 0.0)
    step = jnp.where(mask, jnp.maximum(x, 0.0) + jnp.log1p(jnp.exp(-jnp.abs(x))), 0.0)
    return rate, x, step


def prepare_scan(raw, heads, step3, log3, log_t):
    rate, x, step = step_terms(raw, heads)
    lower = ones_where(iota((T, T), 0) >= iota((T, T), 1)).astype(BF)
    total = unpack3(nn(lower, pack3(jnp.where(head_mask(), step * rate, 0.0))))
    total = jnp.where(head_mask(), total, 0.0)
    step3[...] = pack3(step)
    log3[...] = pack3(total)
    flipped = jnp.transpose(total)
    for h in range(HEADS):
        log_t[h] = flipped[h : h + 1]


def conv_pass(rest, rows, cols, act):
    masks = [ones_where(cols[:, k : k + 1] == cols[:, 0:1]) for k in range(1, 4)]

    def body(c, carry):
        here = tiles(c * 128, 128)
        ci = rest[:, here]
        total = rows[0:1, here] + ci * rows[4:5, here]
        for k in range(1, 4):
            total = total + pltpu.roll(ci, k, 0) * masks[k - 1] * rows[4 - k : 5 - k, here]
        act[:, here] = total * sigmoid(total)
        return carry

    lax.fori_loop(0, 14, body, 0)


def linked_pairs(cols, seg_row):
    return (cols[:, 0:1] == seg_row[0:1, :]) & (iota((T, T), 0) >= iota((T, T), 1))


def score_pass(act, cols, seg_row, scores, scores_low):
    b = act[:, INNER : INNER + STATE]
    c = act[:, INNER + STATE :]
    s = lax.dot_general(c, b, (((1,), (1,)), ((), ())), precision=HIGHEST, preferred_element_type=F32)
    s = jnp.where(linked_pairs(cols, seg_row), s, 0.0)
    scores[...] = s
    scores_low[...] = s.astype(BF)


def lane_heads(q):
    return (iota((128, 256), 1) >> 6) == q


def block_rows(i):
    return slice(128 * i, 128 * (i + 1))


def chunk_terms(j, act, step3, log3):
    x = act[:, tiles(j * 256, 256)]
    spread = spread_matrix(j, 256, 6)
    step_e = nn(step3[...], spread)
    log_e = nn(log3[...], spread)
    wide = nn(log3[...], spread_matrix(j, 512, 7))
    return x, step_e, log_e, wide, x * step_e


def decays(i, j, wide, log_t):
    out = []
    for q in range(4):
        row = log_t[4 * j + q, :, block_rows(i)]
        out.append(jnp.exp(jnp.minimum(wide[block_rows(i), 128 * q : 128 * (q + 1)] - row, 0.0)))
    return out


def project(c, normed, w, proj):
    here = tiles(c * 256, 256)
    proj[:, here] = nn(normed[...], weight(w, here))


def forward_chunk(j, rows, skip, gate_ref, act, scores, scores_low, step3, log3, log_t, mixed_ref, gated, square):
    here = tiles(j * 256, 256)
    x, step_e, log_e, wide, xd = chunk_terms(j, act, step3, log3)
    xd_low = xd.astype(BF)
    for i in range(3):
        at = block_rows(i)
        sc = scores[at, at]
        left = jnp.concatenate([(sc * e).astype(BF) for e in decays(i, j, wide, log_t)], axis=1)
        part = xd_low[at]
        right = jnp.concatenate([jnp.where(lane_heads(q), part, 0) for q in range(4)], axis=0)
        y = nn(left, right)
        if i:
            edge = log_e[128 * i - 1 : 128 * i, :]
            before = slice(0, 128 * i)
            carried = (xd[before] * jnp.exp(jnp.minimum(edge - log_e[before], 0.0))).astype(BF)
            y = y + jnp.exp(jnp.minimum(log_e[at] - edge, 0.0)) * nn(scores_low[at, before], carried)
        mixed = y + skip[2:3, here] * x[at]
        mixed_ref[at, here] = mixed
        gate = gate_ref[at, here]
        u = mixed * (gate * sigmoid(gate))
        gated[at, here] = u
        uu = u * u
        square[at, :] += uu[:, :128] + uu[:, 128:]


def gate_norm(rows, gated, square, yn):
    r = lax.rsqrt(jnp.sum(square[...], axis=-1, keepdims=True) * (1.0 / INNER) + EPS)

    def gain(c, carry):
        here = tiles(c * 256, 256)
        yn[:, here] = (gated[:, here] * r * rows[5:6, here]).astype(BF)
        return carry

    lax.fori_loop(0, 6, gain, 0)


def first_backward(c, gl, w_out, rows, gate_ref, mixed_ref, dyn, sum_u, sum_d):
    here = tiles(c * 256, 256)
    dy = nn(gl[...], weight(w_out, here))
    dyn[:, here] = dy
    gate = gate_ref[:, here]
    u = mixed_ref[:, here] * (gate * sigmoid(gate))
    uu = u * u
    ud = u * dy * rows[5:6, here]
    sum_u[...] += uu[:, :128] + uu[:, 128:]
    sum_d[...] += ud[:, :128] + ud[:, 128:]


def norm_pull(sum_u, sum_d):
    r = lax.rsqrt(jnp.sum(sum_u[...], axis=-1, keepdims=True) * (1.0 / INNER) + EPS)
    pull = r * r * r * (jnp.sum(sum_d[...], axis=-1, keepdims=True) * (1.0 / INNER))
    sum_u[...] = jnp.broadcast_to(r, (T, 128))
    sum_d[...] = jnp.broadcast_to(pull, (T, 128))


def backward_chunk(j, rows, skip, gate_ref, act, scores, scores_low, step3, log3, log_t, mixed_ref, dyn, sum_u, sum_d,
                   gl_t, norm_t, g_out, g_gate, small, dgate, dact, dscores, dlog, dstep, row_skip):
    here = tiles(j * 256, 256)
    r = sum_u[:, 0:1]
    pull = sum_d[:, 0:1]
    x, step_e, log_e, wide, xd = chunk_terms(j, act, step3, log3)
    xd_low = xd.astype(BF)
    dy = dyn[:, here]
    gate = gate_ref[:, here]
    mixed = mixed_ref[:, here]
    sg = sigmoid(gate)
    silu = gate * sg
    gain = rows[5:6, here]
    u = mixed * silu
    ur = u * r
    small[5:6, here] = jnp.sum(dy * ur, axis=0, keepdims=True)
    put_rows(g_out, here, nn(gl_t[...], (ur * gain).astype(BF)))
    du = r * (gain * dy) - u * pull
    dg = (du * mixed * (sg * (1.0 + gate * (1.0 - sg)))).astype(BF)
    dgate[:, here] = dg
    put_rows(g_gate, here, nn(norm_t[...], dg))
    dm = du * silu
    row_skip[0:1, here] = jnp.sum(dm * x, axis=0, keepdims=True)
    dm_low = dm.astype(BF)
    v_parts, dxd_parts = [], []
    for i in range(3):
        at = block_rows(i)
        sc = scores[at, at]
        es = decays(i, j, wide, log_t)
        ws = [(sc * e).astype(BF) for e in es]
        part, dpart = xd_low[at], dm_low[at]
        right = jnp.concatenate([jnp.where(lane_heads(q), part, 0) for q in range(4)], axis=0)
        dright = jnp.concatenate([jnp.where(lane_heads(q), dpart, 0) for q in range(4)], axis=0)
        y = nn(jnp.concatenate(ws, axis=1), right)
        dxd = tn(jnp.concatenate(ws, axis=0), dright)
        g = nt(dright, part)
        ds = g[0:128] * es[0]
        for q in range(1, 4):
            ds = ds + g[128 * q : 128 * (q + 1)] * es[q]
        dscores[at, at] += ds
        v_parts.append(dpart.astype(F32) * y - part.astype(F32) * dxd)
        dxd_parts.append(dxd)
    for i in range(1, 3):
        at = block_rows(i)
        before = slice(0, 128 * i)
        edge = log_e[128 * i - 1 : 128 * i, :]
        fade = jnp.exp(jnp.minimum(edge - log_e[before], 0.0))
        carried = (xd[before] * fade).astype(BF)
        de = (dm[at] * jnp.exp(jnp.minimum(log_e[at] - edge, 0.0))).astype(BF)
        z = nn(scores_low[at, before], carried)
        dz = tn(scores_low[at, before], de)
        dscores[at, before] += nt(de, carried)
        v_parts[i] = v_parts[i] + de.astype(F32) * z
        back = carried.astype(F32) * dz
        faded = fade * dz
        for k in range(i):
            v_parts[k] = v_parts[k] - back[block_rows(k)]
            dxd_parts[k] = dxd_parts[k] + faded[block_rows(k)]
    v = jnp.concatenate(v_parts, axis=0)
    dxd = jnp.concatenate(dxd_parts, axis=0)
    dact[:, here] = step_e * dxd + skip[2:3, here] * dm
    gather = ones_where(4 * j + ((iota((512, 128), 0) & 255) >> 6) == iota((512, 128), 1)).astype(BF)

    def head_sums(a):
        hi = a.astype(BF)
        return nn(jnp.concatenate([hi, (a - hi.astype(F32)).astype(BF)], axis=1), gather)

    dlog[...] += head_sums(v)
    dstep[...] += head_sums(x * dxd)


def scores_backward(act, cols, seg_row, dscores, dact):
    ds = jnp.where(linked_pairs(cols, seg_row), dscores[...], 0.0).astype(BF)
    b = act[:, INNER : INNER + STATE].astype(BF)
    c = act[:, INNER + STATE :].astype(BF)
    dact[:, INNER : INNER + STATE] = tn(ds, c)
    dact[:, INNER + STATE :] = nn(ds, b)


def steps_backward(raw, heads, dlog, dstep, drest, small, row_skip):
    rate, x, step = step_terms(raw, heads)
    upper = ones_where(iota((T, T), 0) <= iota((T, T), 1)).astype(BF)
    dsum = unpack3(nn(upper, pack3(dlog[...])))
    dsum = jnp.where(head_mask(), dsum, 0.0)
    dx = jnp.where(head_mask(), (dstep[...] + rate * dsum) * sigmoid(x), 0.0)
    drest[:, STEP:USED] = dx.astype(BF)
    rates = jnp.sum(dsum * step, axis=0, keepdims=True) * jnp.where(head_mask((1, 128)), rate, 0.0)
    biases = jnp.sum(dx, axis=0, keepdims=True)
    which = ones_where((iota((INNER, 128), 0) >> 6) == iota((INNER, 128), 1))
    skips = exact(row_skip[...], which)[0:1]
    small[7:8, 0:128] = rates + pltpu.roll(biases, 32, 1) + pltpu.roll(skips, 64, 1)


def conv_backward(c, rest, rows, cols, dact, small, drest):
    here = tiles(c * 128, 128)
    ci = rest[:, here]
    taps = [rows[4 - k : 5 - k, here] for k in range(4)]
    masks = [ones_where(cols[:, k : k + 1] == cols[:, 0:1]) for k in range(1, 7)]
    shifted = [ci] + [pltpu.roll(ci, k, 0) * masks[k - 1] for k in range(1, 4)]
    total = rows[0:1, here] + ci * taps[0]
    for k in range(1, 4):
        total = total + shifted[k] * taps[k]
    sg = sigmoid(total)
    dc = dact[:, here] * (sg * (1.0 + total * (1.0 - sg)))
    small[0:1, here] = jnp.sum(dc, axis=0, keepdims=True)
    dci = dc * taps[0]
    for k in range(4):
        small[4 - k : 5 - k, here] = jnp.sum(dc * shifted[k], axis=0, keepdims=True)
        if k:
            dci = dci + pltpu.roll(dc, T - k, 0) * masks[k + 2] * taps[k]
    drest[:, here] = dci.astype(BF)


def rest_grad(norm_t, drest, g_rest):
    def body(c, carry):
        here = tiles(c * 256, 256)
        put_rows(g_rest, here, nn(norm_t[...], drest[:, here]))
        return carry

    lax.fori_loop(0, 7, body, 0)
    put_rows(g_rest, pl.ds(STEP, 128), nn(norm_t[...], drest[:, STEP:USED]))
    g_rest[:, :, :, SMALL:] = jnp.zeros((4, 4, 48, 128), BF)


def normed_backward(dgate, drest, w_gate, w_rest, dn):
    for n in range(2):
        gate = w_gate[2 * n : 2 * n + 2].reshape(T, INNER)
        rest = w_rest[2 * n : 2 * n + 2, :, :, 0:USED].reshape(T, USED)
        dn[:, T * n : T * (n + 1)] = nt(dgate[...], gate) + nt(drest[...], rest)


def stream_backward(dn, stream, gain, grad, small):
    r = lax.rsqrt(jnp.mean(stream * stream, axis=-1, keepdims=True) + EPS)
    small[6:7, 0:D] = jnp.sum(dn * stream * r, axis=0, keepdims=True)
    gd = gain * dn
    return grad + r * gd - stream * (r * r * r * jnp.mean(stream * gd, axis=-1, keepdims=True))


class Place:
    def __init__(self):
        me = lax.axis_index("fsdp")
        self.me = me
        self.x = lax.div(me, 32)
        self.y = lax.rem(lax.div(me, 8), 4)
        self.z = lax.rem(lax.div(me, 2), 4)
        self.c = lax.rem(me, 2)

    def at(self, dx=0, dy=0, dz=0, dc=0):
        x = lax.rem(self.x + dx, 4)
        y = lax.rem(self.y + dy, 4)
        z = lax.rem(self.z + dz, 4)
        c = lax.rem(self.c + dc, 2)
        return ((x * 4 + y) * 4 + z) * 2 + c

    def along(self, axis, step):
        return self.at(dx=step) if axis == 0 else self.at(dy=step)

    def half(self, core, size, color=0, colors=1):
        return pl.ds(pl.multiple_of(core * size + color * (size // 2), 128), size // colors)


def greet(places):
    barrier = pltpu.get_barrier_semaphore()
    for place in places:
        pl.semaphore_signal(barrier, inc=1, device_id=(place,), device_id_type=MESH)
    pl.semaphore_wait(barrier, len(places))


class Semaphores:
    def __init__(self, send, recv):
        self.send, self.recv, self.count = send, recv, 0

    def next(self):
        self.count += 1
        return self.send.at[self.count - 1], self.recv.at[self.count - 1]


class Copies:
    def __init__(self, semaphores):
        self.semaphores, self.made, self.over = semaphores, {}, set()

    def make(self, name, src, dst, device):
        send, recv = self.semaphores.next()
        self.made[name] = pltpu.make_async_remote_copy(
            src_ref=src, dst_ref=dst, send_sem=send, recv_sem=recv, device_id=(device,), device_id_type=MESH
        )

    def start(self, *name):
        self.made[name].start()

    def got(self, *name):
        self.made[name].wait_recv()

    def sent(self, *name):
        self.made[name].wait_send()
        self.over.add(name)

    def finish(self):
        for name in self.made:
            if name not in self.over:
                self.sent(*name)


STEPS = (1, 3, 2)
OFFSETS = (0, 3, 1, 2)
GROUP = [(dz, dc) for dz in (1, 3, 2, 0) for dc in (0, 1) if (dz, dc) != (0, 0)]


class GatherGroup:
    def __init__(self, at, shard, slots, semaphores):
        self.at, self.shard, self.slots, self.size = at, shard, slots, slots.shape[2]
        self.mine = at.z * 2 + at.c
        self.copies = Copies(semaphores)
        for dz, dc in GROUP:
            core = lax.rem(at.c + dc, 2)
            self.copies.make((dz, dc), shard.at[:, at.half(core, self.size)], slots.at[self.mine], at.at(dz=dz, dc=dc))

    def begin(self):
        for name in GROUP:
            self.copies.start(*name)
        self.slots[self.mine] = self.shard[:, self.at.half(self.at.c, self.size)]

    def end(self, first, second):
        for name in GROUP:
            self.copies.got(*name)
        row, k = iota((96, 128), 0), iota((96, 128), 1)
        within = k & 15
        block = jnp.where(within >= 6, 1, 0)
        aim = block * 48 + (k >> 4) * 6 + within - 6 * block
        select = ones_where((row == aim) & (within < 12)).astype(BF)
        got = nn(select, self.slots[...].reshape(128, self.size)).astype(BF)
        at = self.at
        first[at.x, at.y, :, at.half(at.c, self.size)] = got[:48]
        second[at.x, at.y, :, at.half(at.c, self.size)] = got[48:]


class GatherPlane:
    def __init__(self, at, w, semaphores):
        self.copies = c = Copies(semaphores)
        size = w.shape[3] // 2

        def block(color, first, second):
            dx, dy = (first, second) if color == 0 else (second, first)
            return w.at[lax.rem(at.x + dx, 4), lax.rem(at.y + dy, 4), :, at.half(at.c, size, color, 2)]

        for color in range(2):
            near, far = color, 1 - color
            for step in STEPS:
                own = block(color, 0, 0)
                c.make(("a", color, step), own, own, at.along(near, step))
                for o in OFFSETS:
                    there = block(color, o, 0)
                    c.make(("c", color, o, step), there, there, at.along(far, step))
            for o in OFFSETS:
                cols = at.half(at.c, size, color, 2)
                there = w.at[:, lax.rem(at.y + o, 4), :, cols] if color == 0 else w.at[lax.rem(at.x + o, 4), :, :, cols]
                c.make(("p", color, o), there, there, at.at(dc=1))

    def begin(self):
        for step in STEPS:
            for color in range(2):
                self.copies.start("a", color, step)
        for step in STEPS:
            for color in range(2):
                self.copies.start("c", color, 0, step)

    def near(self):
        for step in STEPS:
            for color in range(2):
                self.copies.got("a", color, step)
                for further in STEPS:
                    self.copies.start("c", color, 4 - step, further)
        for color in range(2):
            self.copies.start("p", color, 0)

    def far(self):
        for step in STEPS:
            for color in range(2):
                for o in OFFSETS:
                    self.copies.got("c", color, o, step)
                self.copies.start("p", color, 4 - step)

    def end(self):
        for o in OFFSETS:
            for color in range(2):
                self.copies.got("p", color, o)


def plus(a, b):
    return a.astype(F32) + b.astype(F32)


class Reduce:
    SENDS = 18

    def __init__(self, at, g, out, scratch, semaphores):
        self.h, self.rb, self.rb1, self.zs, self.zr, self.xs = scratch
        self.at, self.g, self.out = at, g, out
        self.size = g.shape[3] // 2
        self.copies = c = Copies(semaphores)
        other = lax.rem(at.c + 1, 2)
        for color in range(2):
            cols = self.here(color)
            c.make(("p", color), g.at[:, :, :, at.half(other, self.size, color, 2)], self.h.at[:, :, :, cols], at.at(dc=1))
            for step in STEPS:
                c.make(("a", color, step), self.rows(color, step), self.rb.at[color, step - 1], at.along(color, step))
                c.make(("d", color, step), self.block(color, step), self.rb1.at[color, step - 1], at.along(1 - color, step))
        for dz in STEPS:
            c.make(("z", dz), self.zs.at[lax.rem(at.z + dz, 4)], self.zr.at[at.z], at.at(dz=dz))
        c.make(("x",), self.xs, out.at[:, at.half(at.c, self.size)], at.at(dc=1))

    def here(self, color):
        return pl.ds(color * (self.size // 2), self.size // 2)

    def rows(self, color, o):
        if color == 0:
            return self.h.at[lax.rem(self.at.x + o, 4), :, :, self.here(color)]
        return self.h.at[:, lax.rem(self.at.y + o, 4), :, self.here(color)]

    def block(self, color, o):
        dx, dy = (0, o) if color == 0 else (o, 0)
        return self.h.at[lax.rem(self.at.x + dx, 4), lax.rem(self.at.y + dy, 4), :, self.here(color)]

    def begin(self):
        for color in range(2):
            self.copies.start("p", color)

    def pair(self, color):
        at = self.at
        self.copies.got("p", color)
        cols = self.here(color)

        def add(n, carry):
            x, y = lax.div(n, 4), lax.rem(n, 4)
            own = self.g[x, y, :, at.half(at.c, self.size, color, 2)]
            self.h[x, y, :, cols] = plus(own, self.h[x, y, :, cols]).astype(BF)
            return carry

        lax.fori_loop(0, 16, add, 0)
        for step in STEPS:
            self.copies.start("a", color, step)

    def near(self, color):
        for step in STEPS:
            self.copies.got("a", color, step)
        cols = self.here(color)

        def add(n, carry):
            x, y = (self.at.x, n) if color == 0 else (n, self.at.y)
            there = (x, y, slice(None), cols)
            self.h[there] = (plus(self.h[there], self.rb[color, 0, n]) + plus(self.rb[color, 1, n], self.rb[color, 2, n])).astype(BF)
            return carry

        lax.fori_loop(0, 4, add, 0)
        for step in STEPS:
            self.copies.start("d", color, step)

    def far(self, color):
        for step in STEPS:
            self.copies.got("d", color, step)
        there = self.block(color, 0)
        there[...] = (plus(there[...], self.rb1[color, 0]) + plus(self.rb1[color, 1], self.rb1[color, 2])).astype(BF)

    def along_z(self):
        at = self.at
        row, k = iota((64, 48), 0), iota((64, 48), 1)
        select = ones_where(((row & 15) < 12) & (k == 12 * (row >> 4) + (row & 15))).astype(BF)
        self.zs[...] = nn(select, self.h[at.x, at.y]).astype(BF).reshape(4, 16, self.size)
        for dz in STEPS:
            self.copies.start("z", dz)
        self.zr[at.z] = self.zs[at.z]

    def along_core(self):
        at = self.at
        for dz in STEPS:
            self.copies.got("z", dz)
        total = plus(self.zr[0], self.zr[1]) + plus(self.zr[2], self.zr[3])
        low, high = total[0:8], jnp.concatenate([total[6:12], total[0:2]], axis=0)
        core = jnp.broadcast_to(at.c, (8, self.size))
        self.xs[...] = jnp.where(core == 0, high, low)
        for color in range(2):
            for step in STEPS:
                self.copies.sent("a", color, step)
                self.copies.sent("d", color, step)
        self.copies.start("x")
        self.out[:, at.half(at.c, self.size)] = jnp.where(core == 0, low, high)

    def end(self):
        self.copies.got("x")


class SmallReduce:
    SENDS = 10

    def __init__(self, at, small, out, scratch, semaphores):
        self.at, self.small, self.out = at, small, out
        self.sx, self.sy, self.sz, self.sc = scratch
        self.copies = c = Copies(semaphores)
        for d in STEPS:
            c.make(("sx", d), self.sx.at[at.x], self.sx.at[at.x], at.at(dx=d))
            c.make(("sy", d), self.sy.at[at.y], self.sy.at[at.y], at.at(dy=d))
            c.make(("sz", d), self.sz.at[at.z], self.sz.at[at.z], at.at(dz=d))
        c.make(("sc",), self.sc.at[at.c], self.sc.at[at.c], at.at(dc=1))

    def begin(self):
        self.sx[self.at.x] = self.small[...]
        for d in STEPS:
            self.copies.start("sx", d)

    def step(self, name, here, following, index):
        for d in STEPS:
            self.copies.got(name, d)
        following[index] = (here[0] + here[1]) + (here[2] + here[3])

    def along_y(self):
        self.step("sx", self.sx, self.sy, self.at.y)
        for d in STEPS:
            self.copies.start("sy", d)

    def along_z(self):
        self.step("sy", self.sy, self.sz, self.at.z)
        for d in STEPS:
            self.copies.start("sz", d)

    def along_core(self):
        self.step("sz", self.sz, self.sc, self.at.c)
        self.copies.start("sc")

    def end(self):
        self.copies.got("sc")
        total = self.sc[0] + self.sc[1]

        def own(entries, width):
            pick = ones_where(iota((width, 128), 0) == entries * self.at.me + iota((width, 128), 1))
            pick = jnp.where(iota((width, 128), 1) < entries, pick, 0.0)
            return exact(total[:, :width], pick)

        self.out[0:5, :] = own(14, CONV)[0:5]
        self.out[5:6, :] = own(12, INNER)[5:6]
        self.out[6:7, :] = own(6, D)[6:7]
        self.out[7:8, :] = total[7:8, 0:128]


def dma_pair(count):
    return [pltpu.SemaphoreType.DMA((count,)), pltpu.SemaphoreType.DMA((count,))]


def wide_scratch(width):
    size = width // 2
    return [
        pltpu.VMEM((4, 4, 48, size), BF),
        pltpu.VMEM((2, 3, 4, 48, size // 2), BF),
        pltpu.VMEM((2, 3, 48, size // 2), BF),
    ]


def narrow_scratch(width):
    size = width // 2
    return [
        pltpu.VMEM((4, 16, size), BF),
        pltpu.VMEM((4, 16, size), BF),
        pltpu.VMEM((8, size), F32),
    ]


def small_scratch():
    return [pltpu.VMEM((4, 8, CONV), F32)] * 3 + [pltpu.VMEM((2, 8, CONV), F32)]


WIDTHS = (REST, INNER, INNER)


def vm(count):
    return [pl.BlockSpec(memory_space=pltpu.VMEM)] * count


def shape(*dims, dtype=F32):
    return jax.ShapeDtypeStruct(dims, dtype)


def whole(width):
    return shape(4, 4, 48, width, dtype=BF)


LIMIT = 62 * 1024 * 1024


def scan_scratch():
    return [
        pltpu.VMEM((T, CONV), F32),
        pltpu.VMEM((T, T), F32),
        pltpu.VMEM((T, T), BF),
        pltpu.VMEM((T, 128), BF),
        pltpu.VMEM((T, 128), BF),
        pltpu.VMEM((HEADS, 1, T), F32),
    ]


def forward_scratch():
    return [
        pltpu.VMEM((T, D), BF),
        pltpu.VMEM((T, INNER), F32),
        pltpu.VMEM((T, 128), F32),
        pltpu.VMEM((T, INNER), BF),
    ]


def backward_scratch():
    return [
        pltpu.VMEM((T, 128), F32),
        pltpu.VMEM((T, 128), F32),
        pltpu.VMEM((T, D), BF),
        pltpu.VMEM((D, T), BF),
        pltpu.VMEM((D, T), BF),
        pltpu.VMEM((T, INNER), BF),
        pltpu.VMEM((T, USED), BF),
        pltpu.VMEM((T, CONV), F32),
        pltpu.VMEM((T, T), F32),
        pltpu.VMEM((T, 128), F32),
        pltpu.VMEM((T, 128), F32),
        pltpu.VMEM((8, INNER), F32),
    ]


def nothing(name):
    return None


def run_forward(stream, w, heads, cols, seg_row, rows, skip, rest, gate, mixed, following, scan, scratch, then=nothing):
    w_rest, w_gate, w_out = w
    act, scores, scores_low, step3, log3, log_t = scan
    normed, gated, square, yn = scratch
    small_rows(w_rest, heads, rows, skip)
    normed[...] = rms_normed(stream[...], rows[6:7, 0:D]).astype(BF)
    then("normed")

    def rest_part(c, carry):
        project(c, normed, w_rest, rest)
        return carry

    lax.fori_loop(0, 7, rest_part, 0)
    rest[:, STEP:USED] = nn(normed[...], weight(w_rest, pl.ds(STEP, 128)))
    then("rest")
    prepare_scan(rest[:, STEP:USED], heads, step3, log3, log_t)
    conv_pass(rest, rows, cols, act)
    then("conv")
    score_pass(act, cols, seg_row, scores, scores_low)
    then("scores")
    square[...] = jnp.zeros_like(square)

    def chunk(j, carry):
        project(j, normed, w_gate, gate)
        forward_chunk(j, rows, skip, gate, act, scores, scores_low, step3, log3, log_t, mixed, gated, square)
        for n in range(6):
            if then is not nothing:
                pl.when(j == n)(lambda: then("chunk%d" % n))
        return carry

    lax.fori_loop(0, 6, chunk, 0)
    gate_norm(rows, gated, square, yn)
    then("yn")
    for n in range(2):
        there = slice(T * n, T * (n + 1))
        following[:, there] = stream[:, there] + nt(yn[...], w_out[2 * n : 2 * n + 2].reshape(T, INNER))


def run_backward(grad, stream, normed, w, heads, cols, seg_row, rows, skip, rest, gate, mixed, g, small, finish, scan, scratch, ready, then=nothing):
    w_rest, w_gate, w_out = w
    g_rest, g_gate, g_out = g
    act, scores, scores_low, step3, log3, log_t = scan
    sum_u, sum_d, gl, gl_t, norm_t, dgate, drest, dact, dscores, dlog, dstep, row_skip = scratch
    dyn = dact
    gl[...] = grad[...].astype(BF)
    gl_t[...] = jnp.transpose(gl[...])
    norm_t[...] = jnp.transpose(normed[...])
    for ref in (small, sum_u, sum_d, dscores, dlog, dstep, row_skip):
        ref[...] = jnp.zeros_like(ref)

    def first(c, carry):
        first_backward(c, gl, w_out, rows, gate, mixed, dyn, sum_u, sum_d)
        return carry

    lax.fori_loop(0, 6, first, 0)
    then("first")
    if not ready:
        prepare_scan(rest[:, STEP:USED], heads, step3, log3, log_t)
        conv_pass(rest, rows, cols, act)
        then("conv")
        score_pass(act, cols, seg_row, scores, scores_low)
        then("scores")
    norm_pull(sum_u, sum_d)

    def chunk(j, carry):
        backward_chunk(j, rows, skip, gate, act, scores, scores_low, step3, log3, log_t, mixed, dyn, sum_u, sum_d,
                       gl_t, norm_t, g_out, g_gate, small, dgate, dact, dscores, dlog, dstep, row_skip)
        for n in range(6):
            if then is not nothing:
                pl.when(j == n)(lambda: then("chunk%d" % n))
        return carry

    lax.fori_loop(0, 6, chunk, 0)
    then("chunks")
    scores_backward(act, cols, seg_row, dscores, dact)
    steps_backward(rest[:, STEP:USED], heads, dlog, dstep, drest, small, row_skip)
    then("steps")

    def conv(c, carry):
        conv_backward(c, rest, rows, cols, dact, small, drest)
        return carry

    lax.fori_loop(0, 14, conv, 0)
    then("conv_back")
    rest_grad(norm_t, drest, g_rest)
    then("rest_grad")
    normed_backward(dgate, drest, w_gate, w_rest, dyn)
    then("normed_back")
    finish(stream_backward(dyn[:, 0:D], stream[...], rows[6:7, 0:D], grad[...], small))
    then("done")


def block0_kernel(shard_rest, shard_gate, shard_out, tokens, heads, cols, seg_row,
                  w0r, w0g, w0o, w1r, w1g, w1o, following, rest, gate, mixed, rows,
                  slots_r, slots_g, slots_o, skip, stream, *scratch):
    scan, forward, (send, recv) = scratch[:6], scratch[6:10], scratch[10:]
    at = Place()
    greet([at.at(dx=d) for d in STEPS] + [at.at(dy=d) for d in STEPS] + [at.at(dz=dz, dc=dc) for dz, dc in GROUP])
    semaphores = Semaphores(send, recv)
    a_rest, a_gate, a_out = [GatherGroup(at, s, t, semaphores) for s, t in ((shard_rest, slots_r), (shard_gate, slots_g), (shard_out, slots_o))]
    r0, g0, o0, r1, g1, o1 = planes = [GatherPlane(at, w, semaphores) for w in (w0r, w0g, w0o, w1r, w1g, w1o)]
    a_rest.begin()
    stream[...] = tokens[...].astype(F32)
    a_rest.end(w0r, w1r)
    r0.begin()
    a_gate.begin()
    a_out.begin()
    a_gate.end(w0g, w1g)
    a_out.end(w0o, w1o)
    r0.near()
    g0.begin()
    r0.far()
    r0.end()

    plan = {
        "normed": [g0.near],
        "rest": [o0.begin, g0.far],
        "conv": [o0.near, r1.begin],
        "scores": [g0.end, o0.far],
        "chunk0": [r1.near, g1.begin],
        "chunk2": [r1.far, g1.near, o1.begin],
        "chunk4": [g1.far, o1.near],
        "yn": [o0.end, r1.end, g1.end, o1.far],
    }

    def then(name):
        for step in plan.get(name, ()):
            step()

    run_forward(stream, (w0r, w0g, w0o), heads, cols, seg_row, rows, skip, rest, gate, mixed, following, scan, forward, then)
    o1.end()
    for each in [a_rest, a_gate, a_out] + planes:
        each.copies.finish()


GATHERS = 3 * 7 + 6 * 38


def block0(shards, tokens, heads, cols, seg_row):
    weights = tuple(whole(w) for w in WIDTHS)
    return pl.pallas_call(
        block0_kernel,
        out_shape=weights + weights + (shape(T, D), shape(T, USED), shape(T, INNER), shape(T, INNER), shape(8, CONV)),
        in_specs=vm(7),
        out_specs=tuple(vm(11)),
        scratch_shapes=[pltpu.VMEM((8, 16, w // 2), BF) for w in WIDTHS]
        + [pltpu.VMEM((8, INNER), F32), pltpu.VMEM((T, D), F32)]
        + scan_scratch()
        + forward_scratch()
        + dma_pair(GATHERS),
        compiler_params=pltpu.CompilerParams(collective_id=0, has_side_effects=True, vmem_limit_bytes=LIMIT),
        name="gather_and_block0",
    )(*shards, tokens, heads, cols, seg_row)


def block1_kernel(stream, w_rest, w_gate, w_out, heads, cols, seg_row, cotangent,
                  output, prev, g_rest, g_gate, g_out, small,
                  skip, rows, rest, gate, mixed, following, grad, *scratch):
    scan, forward, backward = scratch[:6], scratch[6:10], scratch[10:]
    w = (w_rest, w_gate, w_out)
    live = cols[:, 7:8]
    run_forward(stream, w, heads, cols, seg_row, rows, skip, rest, gate, mixed, following, scan, forward)
    output[...] = (following[...] * live).astype(BF)
    grad[...] = cotangent[...].astype(F32) * live

    def finish(value):
        prev[...] = value

    run_backward(grad, stream, forward[0], w, heads, cols, seg_row, rows, skip, rest, gate, mixed,
                 (g_rest, g_gate, g_out), small, finish, scan, backward, True)


def block1(stream, weights, heads, cols, seg_row, cotangent):
    return pl.pallas_call(
        block1_kernel,
        out_shape=(shape(T, D, dtype=BF), shape(T, D)) + tuple(whole(w) for w in WIDTHS) + (shape(8, CONV),),
        in_specs=vm(8),
        out_specs=tuple(vm(6)),
        scratch_shapes=[
            pltpu.VMEM((8, INNER), F32),
            pltpu.VMEM((8, CONV), F32),
            pltpu.VMEM((T, USED), F32),
            pltpu.VMEM((T, INNER), F32),
            pltpu.VMEM((T, INNER), F32),
            pltpu.VMEM((T, D), F32),
            pltpu.VMEM((T, D), F32),
        ]
        + scan_scratch()
        + forward_scratch()
        + backward_scratch(),
        compiler_params=pltpu.CompilerParams(vmem_limit_bytes=LIMIT),
        name="block1",
    )(stream, *weights, heads, cols, seg_row, cotangent)


def back0_kernel(grad, tokens, w_rest, w_gate, w_out, rows, heads, cols, seg_row, rest, gate, mixed, g1r, g1g, g1o, small1,
                 tokens_grad, o0r, o0g, o0o, s0, o1r, o1g, o1o, s1,
                 g0r, g0g, g0o, small0, stream, normed, skip, *scratch):
    scan, backward = scratch[:6], scratch[6:18]
    places = iter(scratch[18:])
    take = lambda n: [next(places) for _ in range(n)]
    r, g, o = [take(3) for _ in range(3)]
    buffers = [wide + take(3) for wide in (r, g, o, r, o, g)]
    small_buffers = [take(4) for _ in range(2)]
    semaphores = Semaphores(*take(2))
    at = Place()
    greet([at.at(dx=d) for d in STEPS] + [at.at(dy=d) for d in STEPS] + [at.at(dz=d) for d in STEPS] + [at.at(dc=1)])
    outs = ((g1r, o1r), (g1g, o1g), (g1o, o1o), (g0r, o0r), (g0g, o0g), (g0o, o0o))
    r1, g1, o1, r0, g0, o0 = sums = [Reduce(at, g, out, buffer, semaphores) for (g, out), buffer in zip(outs, buffers)]
    t1, t0 = smalls = [SmallReduce(at, *v, semaphores) for v in ((small1, s1, small_buffers[0]), (small0, s0, small_buffers[1]))]

    def two(step):
        return [partial(step, 0), partial(step, 1)]

    plan = {
        "begin": [r1.begin, g1.begin, o1.begin, t1.begin],
        "first": two(r1.pair) + [t1.along_y],
        "conv": two(r1.near) + two(g1.pair) + [t1.along_z],
        "scores": two(r1.far) + [t1.along_core],
        "chunk0": two(g1.near) + two(o1.pair) + [r1.along_z],
        "chunk1": two(g1.far) + [t1.end, r1.along_core],
        "chunk2": two(o1.near) + [g1.along_z, r1.end],
        "chunk3": two(o1.far) + [g1.along_core],
        "chunk4": [o1.along_z, g1.end],
        "chunk5": [o1.along_core],
        "chunks": [o1.end, o0.begin, g0.begin],
        "steps": two(o0.pair),
        "conv_back": two(o0.near) + two(g0.pair),
        "rest_grad": [r0.begin] + two(o0.far) + two(g0.near),
        "normed_back": two(r0.pair) + [o0.along_z] + two(g0.far),
        "done": [t0.begin, g0.along_z, o0.along_core]
        + two(r0.near)
        + [t0.along_y, g0.along_core]
        + two(r0.far)
        + [r0.along_z, t0.along_z, r0.along_core, t0.along_core, o0.end, g0.end, r0.end, t0.end],
    }

    def then(name):
        for step in plan.get(name, ()):
            step()

    then("begin")
    stream[...] = tokens[...].astype(F32)
    normed[...] = rms_normed(stream[...], rows[6:7, 0:D]).astype(BF)
    which = ones_where((iota((128, INNER), 1) >> 6) == iota((128, INNER), 0))
    skip[...] = exact(heads[...], which)

    def finish(value):
        tokens_grad[...] = value.astype(BF)

    run_backward(grad, stream, normed, (w_rest, w_gate, w_out), heads, cols, seg_row, rows, skip, rest, gate, mixed,
                 (g0r, g0g, g0o), small0, finish, scan, backward, False, then)
    for each in sums + smalls:
        each.copies.finish()


def back0(grad, tokens, weights, rows, heads, cols, seg_row, rest, gate, mixed, grads1, small1):
    outs = tuple(shape(8, w) for w in WIDTHS) + (shape(8, 128),)
    buffers = []
    for width in WIDTHS:
        buffers += wide_scratch(width)
    for width in WIDTHS * 2:
        buffers += narrow_scratch(width)
    return pl.pallas_call(
        back0_kernel,
        out_shape=(shape(T, D, dtype=BF),) + outs + outs,
        in_specs=vm(16),
        out_specs=tuple(vm(9)),
        scratch_shapes=[pltpu.VMEM((4, 4, 48, w), BF) for w in WIDTHS]
        + [pltpu.VMEM((8, CONV), F32), pltpu.VMEM((T, D), F32), pltpu.VMEM((T, D), BF), pltpu.VMEM((8, INNER), F32)]
        + scan_scratch()
        + backward_scratch()
        + buffers
        + small_scratch() * 2
        + dma_pair(6 * Reduce.SENDS + 2 * SmallReduce.SENDS),
        compiler_params=pltpu.CompilerParams(collective_id=1, has_side_effects=True, vmem_limit_bytes=LIMIT),
        name="back0_and_reduce",
    )(grad, tokens, *weights, rows, heads, cols, seg_row, rest, gate, mixed, *grads1, small1)


def shards_of(norm_gain, in_weight, conv_weight, conv_bias, gate_gain, out_weight):
    taps = jnp.transpose(conv_weight, (0, 2, 1)).reshape(2, 56)
    small = jnp.concatenate([conv_bias, taps, gate_gain, norm_gain, jnp.zeros((2, 40), BF)], axis=1)
    tile = jnp.concatenate([small[:, None, :], jnp.zeros((2, 5, 128), BF)], axis=1)
    rest = jnp.concatenate([in_weight[:, :, INNER:], jnp.zeros((2, 6, SMALL - CONV - HEADS), BF), tile], axis=2)

    def stacked(v):
        return jnp.concatenate([v.reshape(12, -1), jnp.zeros((4, v.shape[2]), BF)], axis=0)

    return stacked(rest), stacked(in_weight[:, :, :INNER]), stacked(jnp.transpose(out_weight, (0, 2, 1)))


def local(tokens, cotangent, segments, counts, norm_gain, in_weight, conv_weight, conv_bias, a_log, dt_bias, skip, gate_gain, out_weight):
    seg = segments.astype(F32)
    ahead = [jnp.concatenate([jnp.full((k,), -1.0, F32), seg[: T - k]]) for k in range(1, 4)]
    after = [jnp.concatenate([seg[k:], jnp.full((k,), -1.0, F32)]) for k in range(1, 4)]
    live = (jnp.arange(T, dtype=jnp.int32) < counts[0]).astype(F32)
    cols = jnp.stack([seg] + ahead + after + [live], axis=1)
    seg_row = seg[None, :]
    heads = jnp.pad(jnp.stack([a_log, dt_bias, skip], axis=1), ((0, 0), (0, 5), (0, 128 - HEADS)))
    shards = shards_of(norm_gain, in_weight, conv_weight, conv_bias, gate_gain, out_weight)
    done = block0(shards, tokens, heads[0], cols, seg_row)
    weights0, weights1, (stream, rest, gate, mixed, rows) = done[0:3], done[3:6], done[6:]
    output, gradient, *grads1, small1 = block1(stream, weights1, heads[1], cols, seg_row, cotangent)
    tokens_grad, *sums = back0(gradient, tokens, weights0, rows, heads[0], cols, seg_row, rest, gate, mixed, grads1, small1)
    rest_sum, gate_sum, out_sum, small = [jnp.stack([sums[n], sums[n + 4]]) for n in range(4)]
    return (
        output,
        tokens_grad,
        small[:, 6, 0:6],
        jnp.concatenate([gate_sum[:, 0:6], rest_sum[:, 0:6, 0 : CONV + HEADS]], axis=2),
        jnp.transpose(small[:, 1:5, 0:14], (0, 2, 1)),
        small[:, 0, 0:14],
        small[:, 7, 0:24],
        small[:, 7, 32:56],
        small[:, 7, 64:88],
        small[:, 5, 0:12],
        jnp.transpose(out_sum[:, 0:6], (0, 2, 1)),
    )


def solution(mesh):
    axis = P("fsdp")
    rows, second, third = P("fsdp", None), P(None, "fsdp"), P(None, None, "fsdp")
    middle = P(None, "fsdp", None)
    return jax.shard_map(
        local,
        mesh=mesh,
        in_specs=(rows, rows, axis, axis, second, middle, middle, second, P(), P(), P(), second, third),
        out_specs=(rows, rows, second, middle, middle, second, P(), P(), P(), second, third),
        check_vma=False,
    )
```

time: 1140 us -> 291 us (0.26)
  blocking collectives: 506 us -> 0 us
  Pallas kernels: 0 us -> 264 us
  matrix products: 166 us -> 0 us
  starting transfers between devices: 160 us -> 0 us
  local copies, waits for them, and re-layouts: 151 us -> 11.9 us
  other arithmetic: 83.2 us -> 9.77 us
  waiting for transfers between devices: 41.6 us -> 0 us
  between operations: 18 us -> 1.82 us
    unnamed x2 -> x0, blocking collectives: 437 us -> none
    pallas_call x0 -> x3, Pallas kernels: none -> 264 us  [the longest x1 113 us: back0(): pl.pallas_call(back0_kernel, out_shape=(shape(T, D, dtype=BF),) + outs +...]
    dot_general x24 -> x0, matrix products: 166 us -> none  [the longest x6 105 us: mixer(): jnp.einsum('tsh,shp->thp', weighting, head_values, precision=highest)]
    unnamed x66 -> x0, starting transfers between devices: 160 us -> none
    all_gather x4 -> x0, local copies, waits for them, and re-layouts: 70.2 us -> none  [the longest x2 46.6 us: local(): lax.all_gather(in_weight[layer_index], 'fsdp', axis=0, tiled=True)]
    all_gather x2 -> x0, blocking collectives: 69.5 us -> none  [local(): lax.all_gather(conv_weight[layer_index], 'fsdp', axis=0, tiled=True)]
    unnamed x368 -> x3, local copies, waits for them, and re-layouts: 56.1 us -> 3.36 us
    all_gather x4 -> x0, waiting for transfers between devices: 40.1 us -> none  [the longest x2 40.1 us: local(): lax.all_gather(in_weight[layer_index], 'fsdp', axis=0, tiled=True)]
  transfers between devices with their start and end apart: 70 -> 0, of which waited for: 2 -> 0; matrix products, arithmetic and copies ran while one was open for 48% -> 0% of each run, Pallas kernels for 0% -> 0%
where the time goes in v2:
time: 291 us; the launch traced here: 287 us
  Pallas kernels  264 us (91%)
  local copies, waits for them, and re-layouts  11.9 us (4%)
  other arithmetic  9.77 us (3%)
    pallas_call x1, Pallas kernels, back0(): pl.pallas_call(back0_kernel, out_shape=(shape(T, D, dtype=BF),) + outs +...  113 us
    pallas_call x1, Pallas kernels, block0(): pl.pallas_call(block0_kernel, out_shape=weights + weights + (shape(T, D),...  95.9 us
    pallas_call x1, Pallas kernels, block1(): pl.pallas_call(block1_kernel, out_shape=(shape(T, D, dtype=BF), shape(T,...  55.2 us

profile of v2, /device:TPU:1, one launch (start us, length us, event | category | flops | bytes accessed | tf_op | source)
XLA Modules:
  0.0 287.0 jit_solution(11520230773722262204)
XLA Ops:
  1.3 0.8 reshape.44
  2.1 0.8 concatenate.39
  2.8 0.7 convert_element_type.15
  3.5 0.6 broadcast_in_dim.17.seg_row
  4.1 0.1 fusion.10
  4.2 0.1 pad_maximum_fusion.3
  4.3 0.1 fusion.8
  4.4 0.1 concatenate.47
  4.5 0.1 fusion.9
  4.5 0.1 concatenate.46
  4.7 0.7 select_maximum_fusion
  5.4 0.6 slice_bitcast_fusion
  6.0 0.8 slice.62
  6.8 0.6 concatenate.43.shard_gate
  7.5 0.8 slice.61
  8.3 0.1 concatenate.41
  8.5 0.6 concatenate.42.shard_rest
  9.1 0.8 copy.49
  9.9 0.6 concatenate.44.shard_out
  10.5 0.8 copy.53.cols
  11.3 95.9 %gather_and_block0.1 = (bf16[4,4,48,2048]{3,2,1,0:T(8,128)(2,1)}, bf16[4,4,48,1536]{3,2,1,0:T(8,128)(2,1)}, bf16[4,4,48,1536]{3,2,1,0:T(8,128)(2,1)}, bf16[4,4,4...) custom-call(bf16[16,2048]{1,0:T(8,128)(2,1)} %concatenate.42.shard_r, ...), custom_call_target="tpu_custom_call" | custom-call | tf_op jit(solution)/shard_map/gather_and_block0/pallas_call | solution.py:917
  107.2 55.2 %block1.1 = (bf16[384,768]{1,0:T(8,128)(2,1)}, f32[384,768]{1,0:T(8,128)}, bf16[4,4,48,2048]{3,2,1,0:T(8,128)(2,1)}, bf16[4,4,48,1536]{3,2,1,0:T(8,128)(2,1)}, b...) custom-call(f32[384,768]{1,0:T(8,128)} %get-tuple-element.37.stream, ...), custom_call_target="tpu_custom_call" | custom-call | tf_op jit(solution)/shard_map/block1/pallas_call | solution.py:950
  162.4 112.5 %back0_and_reduce.1 = (bf16[384,768]{1,0:T(8,128)(2,1)}, f32[8,2048]{1,0:T(8,128)}, f32[8,1536]{1,0:T(8,128)}, f32[8,1536]{1,0:T(8,128)}, f32[8,128]{1,0:T(8,128...) custom-call(f32[384,768]{1,0:T(8,128)} %get-tuple-element.42.grad, ...), custom_call_target="tpu_custom_call" | custom-call | tf_op jit(solution)/shard_map/back0_and_reduce/pallas_call | solution.py:1040
  274.9 1.3 fusion.5
  276.2 1.3 pad_maximum_fusion.5
  277.4 1.3 pad_maximum_fusion.6
  278.7 1.5 fusion.4
  280.2 1.3 fusion.3
  281.5 0.8 fusion.1
  282.3 0.7 copy.57
  283.0 0.9 fusion
  283.9 0.8 copy.56
  284.6 1.9 copy.60
  (19 shorter events, 0.2 us)

commit v3 on v2

v3 whole, which is shorter than its diff:
```python
from functools import partial

import jax
import jax.numpy as jnp
from jax import lax
from jax.experimental import pallas as pl
from jax.experimental.pallas import tpu as pltpu
from jax.sharding import PartitionSpec as P

D = 768
HEADS = 24
STATE = 128
INNER = 1536
CONV = 1792
T = 384
PART = 512
Q = 1536
STEP = 256
USED = 384
SMALL = 384
B = 512
EPS = 1e-05
F32 = jnp.float32
BF = jnp.bfloat16
HIGHEST = lax.Precision.HIGHEST
MESH = pl.DeviceIdType.MESH


def nn(a, b):
    return lax.dot_general(a, b, (((1,), (0,)), ((), ())), preferred_element_type=F32)


def nt(a, b):
    return lax.dot_general(a, b, (((1,), (1,)), ((), ())), preferred_element_type=F32)


def tn(a, b):
    return lax.dot_general(a, b, (((0,), (0,)), ((), ())), preferred_element_type=F32)


def exact(a, b):
    return lax.dot_general(a, b, (((1,), (0,)), ((), ())), precision=HIGHEST, preferred_element_type=F32)


def iota(shape, dim):
    return lax.broadcasted_iota(jnp.int32, shape, dim)


def ones_where(cond):
    return jnp.where(cond, 1.0, 0.0)


def tiles(start, width):
    if isinstance(start, int):
        return pl.ds(start, width)
    return pl.ds(pl.multiple_of(start, 128), width)


def sigmoid(v):
    return 1.0 / (1.0 + jnp.exp(-v))


def weight(w, cols):
    v = w[:, :, :, cols]
    return v.reshape(D, v.shape[-1])


def part_of(j, kind):
    return lax.div(j, 2), tiles(PART * kind + 256 * lax.rem(j, 2), 256)


def weight_chunk(wq, j, kind):
    n, cols = part_of(j, kind)
    return wq[n, :, :, :, cols].reshape(D, 256)


def put_product(g, cols, left, right):
    for n in range(2):
        v = nn(left[T * n : T * (n + 1), :], right)
        g[2 * n : 2 * n + 2, :, :, cols] = v.astype(BF).reshape(2, 4, 48, v.shape[-1])


def put_chunk(gq, j, kind, left, right):
    n, cols = part_of(j, kind)
    put_product(gq.at[n], cols, left, right)


def pack3(v):
    hi = v.astype(BF).astype(F32)
    rest = v - hi
    mid = rest.astype(BF).astype(F32)
    low = rest - mid
    return (hi + pltpu.roll(mid, 32, 1) + pltpu.roll(low, 64, 1)).astype(BF)


def unpack3(v):
    return v + pltpu.roll(v, 96, 1) + pltpu.roll(v, 64, 1)


def head_mask(shape=(T, 128)):
    return iota(shape, 1) < HEADS


def spread_matrix(j, width, shift):
    return ones_where((iota((128, width), 0) & 31) == 4 * j + (iota((128, width), 1) >> shift)).astype(BF)


UNITS = ((14, 4682), (12, 5462), (6, 10923))


def small_rows(wb, heads, rows, skip):
    pick = ones_where(iota((128, D), 1) == 6 * iota((128, D), 0)).astype(BF)
    held = nn(pick, weight(wb, tiles(SMALL, 128))).astype(BF)

    kinds = [UNITS[0] + (14 * n,) for n in range(5)] + [UNITS[1] + (70,), UNITS[2] + (82,)]

    def body(c, carry):
        channel = iota((128, 128), 1) + 128 * c
        units = [(channel * magic) >> 16 for _, magic in UNITS]
        spreads = []
        for n, (entries, _, offset) in enumerate(kinds):
            unit = units[max(n - 4, 0)]
            spreads.append(ones_where(iota((128, 128), 0) == offset + channel - unit * entries).astype(BF))
        got = nn(held, jnp.concatenate(spreads, axis=1))
        for n in range(7):
            mine = jnp.where(units[max(n - 4, 0)] == iota((128, 128), 0), got[:, 128 * n : 128 * (n + 1)], 0.0)
            rows[n : n + 1, tiles(128 * c, 128)] = jnp.sum(mine, axis=0, keepdims=True)
        return carry

    lax.fori_loop(0, 14, body, 0)
    which = ones_where((iota((128, INNER), 1) >> 6) == iota((128, INNER), 0))
    skip[...] = exact(heads[...], which)


def by_rows(body, count=12):
    size = T // count

    def step(n, carry):
        body(pl.ds(pl.multiple_of(n * size, size), size))
        return carry

    lax.fori_loop(0, count, step, 0)


def rms_normed(stream, gain, normed):
    def body(at):
        v = stream[at, :].astype(F32)
        r = lax.rsqrt(jnp.mean(v * v, axis=-1, keepdims=True) + EPS)
        normed[at, :] = (v * r * gain).astype(BF)

    by_rows(body)


def step_terms(raw, heads):
    mask = head_mask()
    rate = -jnp.exp(heads[0:1, :])
    x = jnp.where(mask, raw + heads[1:2, :], 0.0)
    step = jnp.where(mask, jnp.maximum(x, 0.0) + jnp.log1p(jnp.exp(-jnp.abs(x))), 0.0)
    return rate, x, step


def prepare_scan(raw, heads, step3, log3, log_t):
    rate, x, step = step_terms(raw, heads)
    lower = ones_where(iota((T, T), 0) >= iota((T, T), 1)).astype(BF)
    total = unpack3(nn(lower, pack3(jnp.where(head_mask(), step * rate, 0.0))))
    total = jnp.where(head_mask(), total, 0.0)
    step3[...] = pack3(step)
    log3[...] = pack3(total)
    flipped = jnp.transpose(total)
    for h in range(HEADS):
        log_t[h] = flipped[h : h + 1]


def conv_masks(cols, masks):
    for k in range(1, 7):
        masks[k - 1] = jnp.broadcast_to(ones_where(cols[:, k : k + 1] == cols[:, 0:1]), (T, 128))


def taken(src, masks, i, here):
    at = block_rows(i)
    if i == 0:
        ci = src[at, here]
        return [ci] + [pltpu.roll(ci, k, 0) * masks[k - 1, at, :] for k in range(1, 4)]
    slab = src[128 * i - 8 : 128 * (i + 1), here]
    return [slab[8:]] + [pltpu.roll(slab, k, 0)[8:] * masks[k - 1, at, :] for k in range(1, 4)]


def conv_forward(src, here, rows, channels, masks, out, there, slope=None):
    for i in range(3):
        ci = taken(src, masks, i, here)
        total = rows[0:1, channels] + ci[0] * rows[4:5, channels]
        for k in range(1, 4):
            total = total + ci[k] * rows[4 - k : 5 - k, channels]
        sg = sigmoid(total)
        out[block_rows(i), there] = total * sg
        if slope is not None:
            slope[block_rows(i), there] = sg * (1.0 + total * (1.0 - sg))


def conv_backward(src, here, rows, channels, masks, dact, slope, there, small, out, padded):
    sums = [0.0] * 5
    for i in range(3):
        ci = taken(src, masks, i, here)
        dc = dact[block_rows(i), there] * slope[block_rows(i), there]
        padded[block_rows(i), :] = dc
        for n, v in enumerate([dc] + [dc * ci[3 - m] for m in range(4)]):
            sums[n] = sums[n] + jnp.sum(v.reshape(16, 8, 128), axis=0)
    for n in range(5):
        small[n : n + 1, channels] = jnp.sum(sums[n], axis=0, keepdims=True)
    for i in range(3):
        at = block_rows(i)
        slab = padded[128 * i : 128 * (i + 1) + 8, :]
        dci = slab[:128] * rows[4:5, channels]
        for k in range(1, 4):
            dci = dci + pltpu.roll(slab, 136 - k, 0)[:128] * masks[k + 2, at, :] * rows[4 - k : 5 - k, channels]
        out[at, here] = dci.astype(BF)


def linked_pairs(cols, seg_row):
    return (cols[:, 0:1] == seg_row[0:1, :]) & (iota((T, T), 0) >= iota((T, T), 1))


def score_pass(act, cols, seg_row, scores):
    b = act[:, 0:STATE]
    c = act[:, STATE:]
    s = lax.dot_general(c, b, (((1,), (1,)), ((), ())), precision=HIGHEST, preferred_element_type=F32)
    s = jnp.where(linked_pairs(cols, seg_row), s, 0.0)
    scores[...] = s


def lane_heads(q):
    return (iota((128, 256), 1) >> 6) == q


def block_rows(i):
    return slice(128 * i, 128 * (i + 1))


def decays(at, j, log3, log_t):
    wide = nn(log3[at, :], spread_matrix(j, 512, 7))
    out = []
    for q in range(4):
        out.append(jnp.exp(jnp.minimum(wide[:, 128 * q : 128 * (q + 1)] - log_t[4 * j + q, :, at], 0.0)))
    return out


def by_head(part):
    return jnp.concatenate([jnp.where(lane_heads(q), part, 0) for q in range(4)], axis=0)


def halves(v):
    return v[:, :128] + v[:, 128:]


def dynamic_block(i):
    return pl.ds(pl.multiple_of(128 * i, 128), 128)


def value_chunk(j, values, rows, masks, x, slope=None):
    for n in range(2):
        here = tiles(j * 256 + 128 * n, 128)
        conv_forward(values, here, rows, here, masks, x, slice(128 * n, 128 * (n + 1)), slope)


def forward_chunk(j, rows, skip, gate_ref, scores, step3, log3, log_t, mixed_ref, gated, square, work):
    here = tiles(j * 256, 256)
    log_e, xd_ref, xd_low, y_ref, act = work[0], work[5], work[3], work[2], work[7]

    def inside(i, carry):
        at = dynamic_block(i)
        spread = spread_matrix(j, 256, 6)
        log_e[at, :] = nn(log3[at, :], spread)
        xd = act[at, :] * nn(step3[at, :], spread)
        xd_ref[at, :] = xd
        sc = scores[at, at]
        left = jnp.concatenate([(sc * e).astype(BF) for e in decays(at, j, log3, log_t)], axis=1)
        y_ref[at, :] = nn(left, by_head(xd.astype(BF)))
        return carry

    lax.fori_loop(0, 3, inside, 0)
    for i in range(1, 3):
        at, before = block_rows(i), slice(0, 128 * i)
        edge = log_e[128 * i - 1 : 128 * i, :]
        for k in range(i):
            part = block_rows(k)
            xd_low[part, :] = (xd_ref[part, :] * jnp.exp(jnp.minimum(edge - log_e[part, :], 0.0))).astype(BF)
        y_ref[at, :] += jnp.exp(jnp.minimum(log_e[at, :] - edge, 0.0)) * nn(scores[at, before].astype(BF), xd_low[before, :])

    def gating(i, carry):
        at = dynamic_block(i)
        mixed = y_ref[at, :] + skip[2:3, here] * act[at, :]
        mixed_ref[at, here] = mixed
        gate = gate_ref[at, here]
        u = mixed * (gate * sigmoid(gate))
        gated[at, here] = u
        square[at, :] += halves(u * u)
        return carry

    lax.fori_loop(0, 3, gating, 0)


def gate_norm(rows, gated, square, yn):
    r = lax.rsqrt(jnp.sum(square[...], axis=-1, keepdims=True) * (1.0 / INNER) + EPS)

    def gain(c, carry):
        here = tiles(c * 256, 256)
        yn[:, here] = (gated[:, here] * r * rows[5:6, here]).astype(BF)
        return carry

    lax.fori_loop(0, 6, gain, 0)


def first_backward(c, gl, wq, rows, gate_ref, mixed_ref, dyn, sum_u, sum_d):
    here = tiles(c * 256, 256)
    dyn[:, here] = nn(gl[...], weight_chunk(wq, c, 0))

    def body(i, carry):
        at = dynamic_block(i)
        gate = gate_ref[at, here]
        u = mixed_ref[at, here] * (gate * sigmoid(gate))
        sum_u[at, :] += halves(u * u)
        sum_d[at, :] += halves(u * dyn[at, here] * rows[5:6, here])
        return carry

    lax.fori_loop(0, 3, body, 0)


def norm_pull(sum_u, sum_d):
    r = lax.rsqrt(jnp.sum(sum_u[...], axis=-1, keepdims=True) * (1.0 / INNER) + EPS)
    pull = r * r * r * (jnp.sum(sum_d[...], axis=-1, keepdims=True) * (1.0 / INNER))
    sum_u[...] = jnp.broadcast_to(r, (T, 128))
    sum_d[...] = jnp.broadcast_to(pull, (T, 128))


def backward_chunk(j, rows, skip, gate_ref, values, masks, padded, scores, step3, log3, log_t, mixed_ref, dyn, sum_u, sum_d,
                   gl_t, norm_t, gq, small, dgate, dvalues, dscores, dlog, dstep, skip_sum, work):
    here = tiles(j * 256, 256)
    log_e, dm_ref, v_ref, low, dxd_ref, step_e, yn, act, slope = work
    value_chunk(j, values, rows, masks, act, slope)
    skips = skip_sum.at[0:8, 0:256]
    skips[...] = jnp.zeros((8, 256), F32)
    small[5:6, here] = jnp.zeros((1, 256), F32)

    def inside(i, carry):
        at = dynamic_block(i)
        spread = spread_matrix(j, 256, 6)
        log_e[at, :] = nn(log3[at, :], spread)
        step_e[at, :] = nn(step3[at, :], spread)
        x = act[at, :]
        xd = x * step_e[at, :]
        r, pull = sum_u[at, 0:1], sum_d[at, 0:1]
        dy = dyn[at, here]
        gate = gate_ref[at, here]
        mixed = mixed_ref[at, here]
        sg = sigmoid(gate)
        silu = gate * sg
        gain = rows[5:6, here]
        u = mixed * silu
        ur = u * r
        small[5:6, here] += jnp.sum(dy * ur, axis=0, keepdims=True)
        yn[at, :] = (ur * gain).astype(BF)
        du = r * (gain * dy) - u * pull
        dgate[at, here] = (du * mixed * (sg * (1.0 + gate * (1.0 - sg)))).astype(BF)
        dm = du * silu
        dm_ref[at, :] = dm
        skips[...] += jnp.sum((dm * x).reshape(16, 8, 256), axis=0)
        sc = scores[at, at]
        es = decays(at, j, log3, log_t)
        ws = [(sc * e).astype(BF) for e in es]
        part, dpart = xd.astype(BF), dm.astype(BF)
        dright = by_head(dpart)
        y = nn(jnp.concatenate(ws, axis=1), by_head(part))
        dxd = tn(jnp.concatenate(ws, axis=0), dright)
        g = nt(dright, part)
        ds = g[0:128] * es[0]
        for q in range(1, 4):
            ds = ds + g[128 * q : 128 * (q + 1)] * es[q]
        dscores[at, at] += ds
        v_ref[at, :] = dpart.astype(F32) * y - part.astype(F32) * dxd
        dxd_ref[at, :] = dxd
        return carry

    lax.fori_loop(0, 3, inside, 0)
    put_chunk(gq, j, 0, gl_t, yn[...])
    put_chunk(gq, j, 1, norm_t, dgate[:, here])
    for i in range(1, 3):
        at, before = block_rows(i), slice(0, 128 * i)
        edge = log_e[128 * i - 1 : 128 * i, :]
        for k in range(i):
            part = block_rows(k)
            low[part, :] = (act[part, :] * step_e[part, :] * jnp.exp(jnp.minimum(edge - log_e[part, :], 0.0))).astype(BF)
        de = (dm_ref[at, :] * jnp.exp(jnp.minimum(log_e[at, :] - edge, 0.0))).astype(BF)
        linked = scores[at, before].astype(BF)
        z = nn(linked, low[before, :])
        dscores[at, before] += nt(de, low[before, :])
        v_ref[at, :] += de.astype(F32) * z
        for k in range(i):
            part = block_rows(k)
            dz = tn(linked[:, part], de)
            v_ref[part, :] -= low[part, :].astype(F32) * dz
            dxd_ref[part, :] += jnp.exp(jnp.minimum(edge - log_e[part, :], 0.0)) * dz

    def outside(i, carry):
        at = dynamic_block(i)
        dxd = dxd_ref[at, :]
        gather = ones_where(4 * j + ((iota((512, 128), 0) & 255) >> 6) == iota((512, 128), 1)).astype(BF)

        def head_sums(a):
            hi = a.astype(BF)
            return nn(jnp.concatenate([hi, (a - hi.astype(F32)).astype(BF)], axis=1), gather)

        dlog[at, :] += head_sums(v_ref[at, :])
        dstep[at, :] += head_sums(act[at, :] * dxd)
        dxd_ref[at, :] = step_e[at, :] * dxd + skip[2:3, here] * dm_ref[at, :]
        return carry

    lax.fori_loop(0, 3, outside, 0)
    which = ones_where(4 * j + (iota((256, 128), 0) >> 6) == iota((256, 128), 1))
    skip_sum[8:16, 0:128] += exact(skips[...], which)
    for n in range(2):
        there = tiles(j * 256 + 128 * n, 128)
        conv_backward(values, there, rows, there, masks, dxd_ref, slope, slice(128 * n, 128 * (n + 1)), small, dvalues, padded)
    put_chunk(gq, j, 2, norm_t, dvalues[:, here])


def scores_backward(act, cols, seg_row, dscores, dact):
    ds = jnp.where(linked_pairs(cols, seg_row), dscores[...], 0.0).astype(BF)
    b = act[:, 0:STATE].astype(BF)
    c = act[:, STATE:].astype(BF)
    dact[:, 0:STATE] = tn(ds, c)
    dact[:, STATE:] = nn(ds, b)


def steps_backward(raw, heads, dlog, dstep, drest, small, skip_sum):
    rate, x, step = step_terms(raw, heads)
    upper = ones_where(iota((T, T), 0) <= iota((T, T), 1)).astype(BF)
    dsum = unpack3(nn(upper, pack3(dlog[...])))
    dsum = jnp.where(head_mask(), dsum, 0.0)
    dx = jnp.where(head_mask(), (dstep[...] + rate * dsum) * sigmoid(x), 0.0)
    drest[:, STEP:USED] = dx.astype(BF)
    rates = jnp.sum(dsum * step, axis=0, keepdims=True) * jnp.where(head_mask((1, 128)), rate, 0.0)
    biases = jnp.sum(dx, axis=0, keepdims=True)
    skips = jnp.sum(skip_sum[8:16, 0:128], axis=0, keepdims=True)
    small[7:8, 0:128] = rates + pltpu.roll(biases, 32, 1) + pltpu.roll(skips, 64, 1)


def normed_backward(dgate, dvalues, db, wq, wb, dn):
    for n in range(2):
        half = slice(2 * n, 2 * n + 2)
        total = nt(db[...], wb[half, :, :, 0:USED].reshape(T, USED))
        for s in range(3):
            cols = slice(PART * s, PART * (s + 1))
            total += nt(dgate[:, cols], wq[s, half, :, :, PART : 2 * PART].reshape(T, PART))
            total += nt(dvalues[:, cols], wq[s, half, :, :, 2 * PART :].reshape(T, PART))
        dn[:, T * n : T * (n + 1)] = total


def stream_backward(dn, stream, gain, grad, small, give):
    small[6:7, 0:D] = jnp.zeros((1, D), F32)

    def body(at):
        v, d = stream[at, :].astype(F32), dn[at, 0:D]
        r = lax.rsqrt(jnp.mean(v * v, axis=-1, keepdims=True) + EPS)
        small[6:7, 0:D] += jnp.sum(d * v * r, axis=0, keepdims=True)
        gd = gain * d
        give(at, grad[at, :] + r * gd - v * (r * r * r * jnp.mean(v * gd, axis=-1, keepdims=True)))

    by_rows(body)


class Place:
    def __init__(self):
        me = lax.axis_index("fsdp")
        self.me = me
        self.x = lax.div(me, 32)
        self.y = lax.rem(lax.div(me, 8), 4)
        self.z = lax.rem(lax.div(me, 2), 4)
        self.c = lax.rem(me, 2)

    def at(self, dx=0, dy=0, dz=0, dc=0):
        x = lax.rem(self.x + dx, 4)
        y = lax.rem(self.y + dy, 4)
        z = lax.rem(self.z + dz, 4)
        c = lax.rem(self.c + dc, 2)
        return ((x * 4 + y) * 4 + z) * 2 + c

    def along(self, axis, step):
        return self.at(dx=step) if axis == 0 else self.at(dy=step)

    def half(self, core, size, color=0, colors=1):
        return pl.ds(pl.multiple_of(core * size + color * (size // 2), 128), size // colors)


def greet(places):
    barrier = pltpu.get_barrier_semaphore()
    for place in places:
        pl.semaphore_signal(barrier, inc=1, device_id=(place,), device_id_type=MESH)
    pl.semaphore_wait(barrier, len(places))


class Semaphores:
    def __init__(self, send, recv):
        self.send, self.recv, self.count = send, recv, 0

    def next(self):
        self.count += 1
        return self.send.at[self.count - 1], self.recv.at[self.count - 1]


class Copies:
    def __init__(self, semaphores):
        self.semaphores, self.made, self.over = semaphores, {}, set()

    def make(self, name, src, dst, device):
        send, recv = self.semaphores.next()
        self.made[name] = pltpu.make_async_remote_copy(
            src_ref=src, dst_ref=dst, send_sem=send, recv_sem=recv, device_id=(device,), device_id_type=MESH
        )

    def start(self, *name):
        self.made[name].start()

    def got(self, *name):
        self.made[name].wait_recv()

    def sent(self, *name):
        self.made[name].wait_send()
        self.over.add(name)

    def finish(self):
        for name in self.made:
            if name not in self.over:
                self.sent(*name)


STEPS = (1, 3, 2)
OFFSETS = (0, 3, 1, 2)
GROUP = [(dz, dc) for dz in (1, 3, 2, 0) for dc in (0, 1) if (dz, dc) != (0, 0)]


class GatherGroup:
    def __init__(self, at, shard, room, semaphores):
        self.at, self.shard, self.size = at, shard, room.shape[3]
        self.slots = room.at[0:2, :, 0:16, :]
        self.mine = (lax.div(at.z, 2), lax.rem(at.z, 2) * 2 + at.c)
        self.copies = Copies(semaphores)
        for dz, dc in GROUP:
            core = lax.rem(at.c + dc, 2)
            self.copies.make((dz, dc), shard.at[:, at.half(core, self.size)], self.slots.at[self.mine], at.at(dz=dz, dc=dc))

    def begin(self):
        for name in GROUP:
            self.copies.start(*name)
        self.slots[self.mine] = self.shard[:, self.at.half(self.at.c, self.size)]

    def end(self, first, second):
        for name in GROUP:
            self.copies.got(*name)
        row, k = iota((96, 128), 0), iota((96, 128), 1)
        within = k & 15
        block = jnp.where(within >= 6, 1, 0)
        aim = block * 48 + (k >> 4) * 6 + within - 6 * block
        select = ones_where((row == aim) & (within < 12)).astype(BF)
        got = nn(select, self.slots[...].reshape(128, self.size)).astype(BF)
        at = self.at
        first[at.x, at.y, :, at.half(at.c, self.size)] = got[:48]
        second[at.x, at.y, :, at.half(at.c, self.size)] = got[48:]


class GatherPlane:
    SENDS = 20

    def __init__(self, at, w, semaphores):
        self.copies = c = Copies(semaphores)
        size = w.shape[3] // 2
        for color in range(2):
            cols = at.half(at.c, size, color, 2)
            own = w.at[at.x, at.y, :, cols]
            for step in STEPS:
                c.make(("a", color, step), own, own, at.along(color, step))
            for o in OFFSETS:
                line = w.at[:, lax.rem(at.y + o, 4), :, cols] if color == 0 else w.at[lax.rem(at.x + o, 4), :, :, cols]
                if o == 0:
                    for step in STEPS:
                        c.make(("c", color, step), line, line, at.along(1 - color, step))
                c.make(("p", color, o), line, line, at.at(dc=1))

    def begin(self):
        for step in STEPS:
            for color in range(2):
                self.copies.start("a", color, step)

    def near(self):
        for color in range(2):
            for step in STEPS:
                self.copies.got("a", color, step)
            for step in STEPS:
                self.copies.start("c", color, step)
            self.copies.start("p", color, 0)

    def far(self):
        for step in STEPS:
            for color in range(2):
                self.copies.got("c", color, step)
                self.copies.start("p", color, 4 - step)

    def end(self):
        for o in OFFSETS:
            for color in range(2):
                self.copies.got("p", color, o)


def plus(a, b):
    return a.astype(F32) + b.astype(F32)


class Reduce:
    SENDS = 18

    def __init__(self, at, g, out, scratch, semaphores):
        self.h, self.rb, self.rb1, self.zs, self.zr, self.xs = scratch
        self.at, self.g, self.out = at, g, out
        self.size = g.shape[3] // 2
        self.copies = c = Copies(semaphores)
        other = lax.rem(at.c + 1, 2)
        for color in range(2):
            cols = self.here(color)
            c.make(("p", color), g.at[:, :, :, at.half(other, self.size, color, 2)], self.h.at[:, :, :, cols], at.at(dc=1))
            for step in STEPS:
                c.make(("a", color, step), self.rows(color, step), self.rb.at[color, step - 1], at.along(color, step))
                c.make(("d", color, step), self.block(color, step), self.rb1.at[color, step - 1], at.along(1 - color, step))
        for dz in STEPS:
            c.make(("z", dz), self.zs.at[lax.rem(at.z + dz, 4)], self.zr.at[at.z], at.at(dz=dz))
        c.make(("x",), self.xs, out.at[:, at.half(at.c, self.size)], at.at(dc=1))

    def here(self, color):
        return pl.ds(color * (self.size // 2), self.size // 2)

    def rows(self, color, o):
        if color == 0:
            return self.h.at[lax.rem(self.at.x + o, 4), :, :, self.here(color)]
        return self.h.at[:, lax.rem(self.at.y + o, 4), :, self.here(color)]

    def block(self, color, o):
        dx, dy = (0, o) if color == 0 else (o, 0)
        return self.h.at[lax.rem(self.at.x + dx, 4), lax.rem(self.at.y + dy, 4), :, self.here(color)]

    def begin(self):
        for color in range(2):
            self.copies.start("p", color)

    def pair(self, color):
        at = self.at
        self.copies.got("p", color)
        cols = self.here(color)

        def add(n, carry):
            x, y = lax.div(n, 4), lax.rem(n, 4)
            own = self.g[x, y, :, at.half(at.c, self.size, color, 2)]
            self.h[x, y, :, cols] = plus(own, self.h[x, y, :, cols]).astype(BF)
            return carry

        lax.fori_loop(0, 16, add, 0)
        for step in STEPS:
            self.copies.start("a", color, step)

    def near(self, color):
        for step in STEPS:
            self.copies.got("a", color, step)
        cols = self.here(color)

        def add(n, carry):
            x, y = (self.at.x, n) if color == 0 else (n, self.at.y)
            there = (x, y, slice(None), cols)
            self.h[there] = (plus(self.h[there], self.rb[color, 0, n]) + plus(self.rb[color, 1, n], self.rb[color, 2, n])).astype(BF)
            return carry

        lax.fori_loop(0, 4, add, 0)
        for step in STEPS:
            self.copies.start("d", color, step)

    def far(self, color):
        for step in STEPS:
            self.copies.got("d", color, step)
        there = self.block(color, 0)
        there[...] = (plus(there[...], self.rb1[color, 0]) + plus(self.rb1[color, 1], self.rb1[color, 2])).astype(BF)

    def along_z(self):
        at = self.at
        row, k = iota((64, 48), 0), iota((64, 48), 1)
        select = ones_where(((row & 15) < 12) & (k == 12 * (row >> 4) + (row & 15))).astype(BF)
        self.zs[...] = nn(select, self.h[at.x, at.y]).astype(BF).reshape(4, 16, self.size)
        for dz in STEPS:
            self.copies.start("z", dz)
        self.zr[at.z] = self.zs[at.z]

    def along_core(self):
        at = self.at
        for dz in STEPS:
            self.copies.got("z", dz)
        total = plus(self.zr[0], self.zr[1]) + plus(self.zr[2], self.zr[3])
        low, high = total[0:8], jnp.concatenate([total[6:12], total[0:2]], axis=0)
        core = jnp.broadcast_to(at.c, (8, self.size))
        self.xs[...] = jnp.where(core == 0, high, low)
        for color in range(2):
            for step in STEPS:
                self.copies.sent("a", color, step)
                self.copies.sent("d", color, step)
        for dz in STEPS:
            self.copies.sent("z", dz)
        self.copies.start("x")
        self.out[:, at.half(at.c, self.size)] = jnp.where(core == 0, low, high)

    def end(self):
        self.copies.got("x")
        self.copies.sent("x")


class SmallReduce:
    SENDS = 10

    def __init__(self, at, small, out, scratch, semaphores):
        self.at, self.small, self.out = at, small, out
        self.sx, self.sy, self.sz, self.sc = scratch
        self.copies = c = Copies(semaphores)
        for d in STEPS:
            c.make(("sx", d), self.sx.at[at.x], self.sx.at[at.x], at.at(dx=d))
            c.make(("sy", d), self.sy.at[at.y], self.sy.at[at.y], at.at(dy=d))
            c.make(("sz", d), self.sz.at[at.z], self.sz.at[at.z], at.at(dz=d))
        c.make(("sc",), self.sc.at[at.c], self.sc.at[at.c], at.at(dc=1))

    def begin(self):
        self.sx[self.at.x] = self.small[...]
        for d in STEPS:
            self.copies.start("sx", d)

    def step(self, name, here, following, index):
        for d in STEPS:
            self.copies.got(name, d)
        following[index] = (here[0] + here[1]) + (here[2] + here[3])

    def along_y(self):
        self.step("sx", self.sx, self.sy, self.at.y)
        for d in STEPS:
            self.copies.start("sy", d)

    def along_z(self):
        self.step("sy", self.sy, self.sz, self.at.z)
        for d in STEPS:
            self.copies.start("sz", d)

    def along_core(self):
        self.step("sz", self.sz, self.sc, self.at.c)
        self.copies.start("sc")

    def end(self):
        self.copies.got("sc")
        for name in list(self.copies.made):
            self.copies.sent(*name)
        total = self.sc[0] + self.sc[1]

        self.sc[0] = total

        def own(entries, width):
            def part(n, sums):
                pick = (iota((128, 128), 0) + 128 * n == entries * self.at.me + iota((128, 128), 1)) & (iota((128, 128), 1) < entries)
                return sums + exact(self.sc[0, :, tiles(128 * n, 128)], ones_where(pick))

            return lax.fori_loop(0, width // 128, part, jnp.zeros((8, 128), F32))

        self.out[0:5, :] = own(14, CONV)[0:5]
        self.out[5:6, :] = own(12, INNER)[5:6]
        self.out[6:7, :] = own(6, D)[6:7]
        self.out[7:8, :] = total[7:8, 0:128]


def dma_pair(count):
    return [pltpu.SemaphoreType.DMA((count,)), pltpu.SemaphoreType.DMA((count,))]


def wide_scratch(width):
    size = width // 2
    return [
        pltpu.VMEM((4, 4, 48, size), BF),
        pltpu.VMEM((2, 3, 4, 48, size // 2), BF),
        pltpu.VMEM((2, 3, 48, size // 2), BF),
    ]


def narrow_scratch(width):
    size = width // 2
    return [
        pltpu.VMEM((4, 16, size), BF),
        pltpu.VMEM((4, 16, size), BF),
        pltpu.VMEM((8, size), F32),
    ]


def small_scratch():
    return [pltpu.VMEM((4, 8, CONV), F32)] * 3 + [pltpu.VMEM((2, 8, CONV), F32)]


WIDTHS = (Q, Q, Q, B)


def vm(count):
    return [pl.BlockSpec(memory_space=pltpu.VMEM)] * count


def shape(*dims, dtype=F32):
    return jax.ShapeDtypeStruct(dims, dtype)


def whole(width):
    return shape(4, 4, 48, width, dtype=BF)


LIMIT = 63 * 1024 * 1024


def scan_scratch():
    return [
        pltpu.VMEM((T, T), F32),
        pltpu.VMEM((T, 128), BF),
        pltpu.VMEM((T, 128), BF),
        pltpu.VMEM((HEADS, 1, T), F32),
        pltpu.VMEM((6, T, 128), F32),
        pltpu.VMEM((T + 8, 128), F32),
        pltpu.VMEM((T, 256), F32),
        pltpu.VMEM((T, 256), F32),
    ] + [pltpu.VMEM((T, 256), dtype) for dtype in (F32, F32, F32, BF, F32, F32, BF, F32, F32)]


def backward_scratch():
    return [
        pltpu.VMEM((T, 128), F32),
        pltpu.VMEM((T, 128), F32),
        pltpu.VMEM((D, T), BF),
        pltpu.VMEM((D, T), BF),
        pltpu.VMEM((T, INNER), BF),
        pltpu.VMEM((T, INNER), BF),
        pltpu.VMEM((T, USED), BF),
        pltpu.VMEM((T, INNER), F32),
        pltpu.VMEM((T, T), F32),
        pltpu.VMEM((T, 128), F32),
        pltpu.VMEM((T, 128), F32),
        pltpu.VMEM((16, 256), F32),
    ]


class Plan:
    def __init__(self, prefix, steps):
        self.prefix, self.steps = prefix, steps

    def __call__(self, name):
        for step in self.steps.get(self.prefix + name, ()):
            step()

    def at_chunk(self, j):
        for n in range(6):
            if self.prefix + "chunk%d" % n in self.steps:
                pl.when(j == n)(partial(self, "chunk%d" % n))


def first_terms(rb, heads, rows, cols, seg_row, scan, then):
    scores, step3, log3, log_t, masks, padded, act, slope, *work = scan
    prepare_scan(rb[:, STEP:USED], heads, step3, log3, log_t)
    for n in range(2):
        here = slice(128 * n, 128 * (n + 1))
        conv_forward(rb, here, rows, slice(INNER + 128 * n, INNER + 128 * (n + 1)), masks, act, here, slope)
    score_pass(act, cols, seg_row, scores)
    then("scores")


def run_forward(stream, wq, wb, heads, cols, seg_row, rows, skip, rb, values, gate, mixed, following, scan, scratch, then):
    scores, step3, log3, log_t, masks, padded, act, slope, *work = scan
    normed, gated, square, yn = scratch
    small_rows(wb, heads, rows, skip)
    then("rows")
    rms_normed(stream, rows[6:7, 0:D], normed)
    rb[...] = nn(normed[...], weight(wb, pl.ds(0, USED)))
    then("normed")
    first_terms(rb, heads, rows, cols, seg_row, scan, then)
    square[...] = jnp.zeros_like(square)

    def chunk(j, carry):
        here = tiles(j * 256, 256)
        values[:, here] = nn(normed[...], weight_chunk(wq, j, 2))
        gate[:, here] = nn(normed[...], weight_chunk(wq, j, 1))
        value_chunk(j, values, rows, masks, work[7])
        forward_chunk(j, rows, skip, gate, scores, step3, log3, log_t, mixed, gated, square, work)
        then.at_chunk(j)
        return carry

    lax.fori_loop(0, 6, chunk, 0)
    gate_norm(rows, gated, square, yn)
    then("yn")
    for n in range(2):
        there = slice(T * n, T * (n + 1))
        total = stream[:, there].astype(F32)
        for s in range(3):
            total += nt(yn[:, PART * s : PART * (s + 1)], wq[s, 2 * n : 2 * n + 2, :, :, 0:PART].reshape(T, PART))
        following[:, there] = total


def run_backward(grad, stream, normed, wq, wb, heads, cols, seg_row, rows, skip, rb, values, gate, mixed, gq, gb, small, finish, scan, scratch, ready, then):
    scores, step3, log3, log_t, masks, padded, act, slope, *work = scan
    sum_u, sum_d, gl_t, norm_t, dgate, dvalues, db, dyn, dscores, dlog, dstep, skip_sum = scratch

    def lower(at):
        gl[at, :] = grad[at, :].astype(BF)

    norm_t[...] = jnp.transpose(normed[...])
    gl = normed
    by_rows(lower)
    gl_t[...] = jnp.transpose(gl[...])
    for ref in (small, sum_u, sum_d, dscores, dlog, dstep, skip_sum):
        ref[...] = jnp.zeros_like(ref)

    def first(c, carry):
        first_backward(c, gl, wq, rows, gate, mixed, dyn, sum_u, sum_d)
        return carry

    lax.fori_loop(0, 6, first, 0)
    then("first")
    if not ready:
        first_terms(rb, heads, rows, cols, seg_row, scan, then)
    norm_pull(sum_u, sum_d)

    def chunk(j, carry):
        backward_chunk(j, rows, skip, gate, values, masks, padded, scores, step3, log3, log_t, mixed, dyn, sum_u, sum_d,
                       gl_t, norm_t, gq, small, dgate, dvalues, dscores, dlog, dstep, skip_sum, work)
        then.at_chunk(j)
        return carry

    lax.fori_loop(0, 6, chunk, 0)
    then("chunks")
    dact = work[0]
    scores_backward(act, cols, seg_row, dscores, dact)
    steps_backward(rb[:, STEP:USED], heads, dlog, dstep, db, small, skip_sum)
    then("steps")
    for n in range(2):
        here = slice(128 * n, 128 * (n + 1))
        conv_backward(rb, here, rows, slice(INNER + 128 * n, INNER + 128 * (n + 1)), masks, dact, slope, here, small, db, padded)
    put_product(gb, pl.ds(0, USED), norm_t, db[...])
    gb[:, :, :, USED:] = jnp.zeros((4, 4, 48, 128), BF)
    then("b_grad")
    normed_backward(dgate, dvalues, db, wq, wb, dyn)
    then("normed_back")
    stream_backward(dyn, stream, rows[6:7, 0:D], grad, small, finish)
    then("done")


def whole_kernel(shard_b, shard_q, tokens, cotangent, heads, cols, seg_row,
                 output, tokens_grad, ob0, oq0, s0, ob1, oq1, s1, far_rb, far_values, far_gate, far_mixed,
                 wb0, wq0, wb1, wq1, gb1, gq1,
                 second, grad, rb, values, gate, mixed, rows0, rows1, skip0, skip1, small0, small1, normed, square, local_sem, *scratch):
    places = iter(scratch)
    take = lambda n: [next(places) for _ in range(n)]
    scan, backward = take(17), take(12)
    dgate, dyn = backward[4], backward[7]
    forward = (normed, dyn, square, dgate)
    wide = [take(3) for _ in range(4)]
    narrow = [take(3) for _ in range(4)]
    sums_by_axis = take(4)
    semaphores = Semaphores(*take(2))
    at = Place()
    greet([at.at(dx=d) for d in STEPS] + [at.at(dy=d) for d in STEPS] + [at.at(dz=dz, dc=dc) for dz, dc in GROUP])

    parts = range(3)
    ab, *aq = groups = [GatherGroup(at, s, t, semaphores) for s, t in [(shard_b, wide[3][0])] + [(shard_q.at[n], wide[n][0]) for n in parts]]
    b0, x0, y0, z0, b1, x1, y1, z1 = planes = [
        GatherPlane(at, w, semaphores) for wb, wq in ((wb0, wq0), (wb1, wq1)) for w in [wb] + [wq.at[n] for n in parts]
    ]
    def sums_of(gb, gq, ob, oq):
        pairs = [(gq.at[n], oq.at[n]) for n in parts] + [(gb, ob)]
        return [Reduce(at, g, o, wide[n] + narrow[n], semaphores) for n, (g, o) in enumerate(pairs)]

    X1, Y1, Z1, B1 = sums1 = sums_of(gb1, gq1, ob1, oq1)
    X0, Y0, Z0, B0 = sums0 = sums_of(wb1, wq1, ob0, oq0)
    S1, S0 = [SmallReduce(at, *v, semaphores) for v in ((small1, s1, sums_by_axis), (small0, s0, sums_by_axis))]

    def two(step):
        return [partial(step, 0), partial(step, 1)]

    away, back = [], []
    for n, (near, far) in enumerate(((rb, far_rb), (values, far_values), (gate, far_gate), (mixed, far_mixed))):
        away.append(pltpu.make_async_copy(near, far, local_sem.at[n]))
        back.append(pltpu.make_async_copy(far, near, local_sem.at[4 + n]))

    steps = {
        "f0.rows": [x0.near, y0.begin],
        "f0.normed": [z0.begin, y0.near],
        "f0.scores": [away[0].start, x0.far, z0.near, x0.end],
        "f0.chunk0": [b1.begin, x1.begin],
        "f0.chunk1": [y0.far, b1.near, y0.end],
        "f0.chunk2": [y1.begin, x1.near, b1.far],
        "f0.chunk3": [z0.far, z1.begin, z0.end],
        "f0.chunk4": [b1.end, y1.near],
        "f0.chunk5": [x1.far, z1.near],
        "f0.yn": [each.start for each in away[1:]],
        "f1.begin": [away[0].wait],
        "f1.scores": [each.wait for each in away[1:]] + [x1.end],
        "f1.chunk0": [y1.far],
        "f1.chunk1": [y1.end],
        "f1.chunk2": [z1.far],
        "f1.chunk3": [z1.end],
        "b1.first": [each.copies.finish for each in groups + planes],
        "b1.chunk1": [X1.begin],
        "b1.chunk2": two(X1.pair),
        "b1.chunk3": [Y1.begin] + two(X1.near),
        "b1.chunk4": two(Y1.pair) + two(X1.far),
        "b1.chunk5": [Z1.begin] + two(Y1.near) + [X1.along_z],
        "b1.chunks": [each.start for each in back[1:]],
        "b1.steps": two(Z1.pair) + [X1.along_core],
        "b1.b_grad": [back[0].start, B1.begin] + two(Y1.far),
        "b1.normed_back": two(B1.pair) + two(Z1.near) + [Y1.along_z, X1.end],
        "b1.done": [each.wait for each in back] + two(B1.near) + two(Z1.far) + [Y1.along_core, S1.begin],
        "b0.first": two(B1.far) + [Z1.along_z, Y1.end, S1.along_y],
        "b0.scores": [B1.along_z, Z1.along_core, S1.along_z],
        "b0.chunk0": [B1.along_core, Z1.end, S1.along_core],
        "b0.chunk1": [B1.end, S1.end, X0.begin],
        "b0.chunk2": two(X0.pair),
        "b0.chunk3": [Y0.begin] + two(X0.near),
        "b0.chunk4": two(Y0.pair) + two(X0.far),
        "b0.chunk5": [Z0.begin] + two(Y0.near) + [X0.along_z],
        "b0.steps": two(Z0.pair) + [X0.along_core],
        "b0.b_grad": [B0.begin] + two(Y0.far),
        "b0.normed_back": two(B0.pair) + two(Z0.near) + [Y0.along_z, X0.end],
        "b0.done": [S0.begin]
        + two(B0.near)
        + two(Z0.far)
        + [Y0.along_core, S0.along_y]
        + two(B0.far)
        + [Z0.along_z, S0.along_z, B0.along_z, Y0.end, Z0.along_core, S0.along_core, B0.along_core, Z0.end, B0.end, S0.end],
    }

    ab.begin()
    for each in aq:
        each.begin()
    conv_masks(cols, scan[4])
    scan[5][T:, :] = jnp.zeros((8, 128), F32)
    ab.end(wb0, wb1)
    b0.begin()
    aq[0].end(wq0.at[0], wq1.at[0])
    x0.begin()
    b0.near()
    for n in (1, 2):
        aq[n].end(wq0.at[n], wq1.at[n])
    b0.far()
    b0.end()

    head0, head1 = heads.at[0], heads.at[1]
    run_forward(tokens, wq0, wb0, head0, cols, seg_row, rows0, skip0, rb, values, gate, mixed, second, scan, forward, Plan("f0.", steps))
    Plan("f1.", steps)("begin")
    run_forward(second, wq1, wb1, head1, cols, seg_row, rows1, skip1, rb, values, gate, mixed, grad, scan, forward, Plan("f1.", steps))

    def turn(at):
        live = cols[at, 7:8]
        output[at, :] = (grad[at, :] * live).astype(BF)
        grad[at, :] = cotangent[at, :].astype(F32) * live

    by_rows(turn)

    def keep(at, value):
        grad[at, :] = value

    run_backward(grad, second, normed, wq1, wb1, head1, cols, seg_row, rows1, skip1, rb, values, gate, mixed,
                 gq1, gb1, small1, keep, scan, backward, True, Plan("b1.", steps))
    rms_normed(tokens, rows0[6:7, 0:D], normed)

    def give(at, value):
        tokens_grad[at, :] = value.astype(BF)

    run_backward(grad, tokens, normed, wq0, wb0, head0, cols, seg_row, rows0, skip0, rb, values, gate, mixed,
                 wq1, wb1, small0, give, scan, backward, False, Plan("b0.", steps))
    for each in sums1 + sums0 + [S1, S0]:
        each.copies.finish()


SENDS = 4 * 7 + 8 * GatherPlane.SENDS + 8 * Reduce.SENDS + 2 * SmallReduce.SENDS


def two_blocks(shards, tokens, cotangent, heads, cols, seg_row):
    outs = (shape(8, B), shape(3, 8, Q), shape(8, 128))
    wb, wq = pltpu.VMEM((4, 4, 48, B), BF), pltpu.VMEM((3, 4, 4, 48, Q), BF)
    buffers = []
    for width in WIDTHS:
        buffers += wide_scratch(width)
    for width in WIDTHS:
        buffers += narrow_scratch(width)
    return pl.pallas_call(
        whole_kernel,
        out_shape=(shape(T, D, dtype=BF), shape(T, D, dtype=BF)) + outs + outs + (shape(T, USED),) + (shape(T, INNER),) * 3,
        in_specs=vm(7),
        out_specs=tuple(vm(8)) + (pl.BlockSpec(memory_space=pl.ANY),) * 4,
        scratch_shapes=[wb, wq] * 3
        + [pltpu.VMEM((T, D), F32)] * 2
        + [pltpu.VMEM((T, USED), F32)]
        + [pltpu.VMEM((T, INNER), F32)] * 3
        + [pltpu.VMEM((8, CONV), F32)] * 2
        + [pltpu.VMEM((8, INNER), F32)] * 2
        + [pltpu.VMEM((8, CONV), F32)] * 2
        + [pltpu.VMEM((T, D), BF), pltpu.VMEM((T, 128), F32), pltpu.SemaphoreType.DMA((8,))]
        + scan_scratch()
        + backward_scratch()
        + buffers
        + small_scratch()
        + dma_pair(SENDS),
        compiler_params=pltpu.CompilerParams(collective_id=0, has_side_effects=True, vmem_limit_bytes=LIMIT),
        name="two_blocks",
    )(*shards, tokens, cotangent, heads, cols, seg_row)


def shards_of(norm_gain, in_weight, conv_weight, conv_bias, gate_gain, out_weight):
    taps = jnp.transpose(conv_weight, (0, 2, 1)).reshape(2, 56)
    small = jnp.concatenate([conv_bias, taps, gate_gain, norm_gain, jnp.zeros((2, 40), BF)], axis=1)
    tile = jnp.concatenate([small[:, None, :], jnp.zeros((2, 5, 128), BF)], axis=1)
    wide = jnp.concatenate([in_weight[:, :, INNER + INNER :], jnp.zeros((2, 6, SMALL - STEP - HEADS), BF), tile], axis=2)
    kinds = [jnp.transpose(out_weight, (0, 2, 1)), in_weight[:, :, :INNER], in_weight[:, :, INNER : 2 * INNER]]
    q = jnp.stack([v.reshape(12, 3, PART) for v in kinds], axis=2).reshape(12, 3, Q).transpose(1, 0, 2)
    return jnp.pad(wide.reshape(12, B), ((0, 4), (0, 0))), jnp.pad(q, ((0, 0), (0, 4), (0, 0)))


def local(tokens, cotangent, segments, counts, norm_gain, in_weight, conv_weight, conv_bias, a_log, dt_bias, skip, gate_gain, out_weight):
    seg = segments.astype(F32)
    ahead = [jnp.concatenate([jnp.full((k,), -1.0, F32), seg[: T - k]]) for k in range(1, 4)]
    after = [jnp.concatenate([seg[k:], jnp.full((k,), -1.0, F32)]) for k in range(1, 4)]
    live = (jnp.arange(T, dtype=jnp.int32) < counts[0]).astype(F32)
    cols = jnp.stack([seg] + ahead + after + [live], axis=1)
    seg_row = seg[None, :]
    heads = jnp.pad(jnp.stack([a_log, dt_bias, skip], axis=1), ((0, 0), (0, 5), (0, 128 - HEADS)))
    shards = shards_of(norm_gain, in_weight, conv_weight, conv_bias, gate_gain, out_weight)
    output, tokens_grad, ob0, oq0, s0, ob1, oq1, s1, *_ = two_blocks(shards, tokens, cotangent, heads, cols, seg_row)
    small = jnp.stack([s0, s1])
    sums = jnp.stack([oq0, oq1])[:, :, 0:6].reshape(2, 3, 6, 3, PART).transpose(3, 0, 2, 1, 4).reshape(3, 2, 6, INNER)
    return (
        output,
        tokens_grad,
        small[:, 6, 0:6],
        jnp.concatenate([sums[1], sums[2], jnp.stack([ob0, ob1])[:, 0:6, 0 : STEP + HEADS]], axis=2),
        jnp.transpose(small[:, 1:5, 0:14], (0, 2, 1)),
        small[:, 0, 0:14],
        small[:, 7, 0:24],
        small[:, 7, 32:56],
        small[:, 7, 64:88],
        small[:, 5, 0:12],
        jnp.transpose(sums[0], (0, 2, 1)),
    )


def solution(mesh):
    axis = P("fsdp")
    rows, second, third = P("fsdp", None), P(None, "fsdp"), P(None, None, "fsdp")
    middle = P(None, "fsdp", None)
    return jax.shard_map(
        local,
        mesh=mesh,
        in_specs=(rows, rows, axis, axis, second, middle, middle, second, P(), P(), P(), second, third),
        out_specs=(rows, rows, second, middle, middle, second, P(), P(), P(), second, third),
        check_vma=False,
    )
```

time: 291 us -> 268 us (0.921); the launches traced: 287 us -> 268 us
  Pallas kernels: 264 us -> 244 us
    pallas_call x3 -> x1, Pallas kernels: 264 us -> 244 us  [two_blocks(): pl.pallas_call(whole_kernel, out_shape=(shape(T, D, dtype=BF), shape(T, D...]
    another operation x3 -> x6, other arithmetic: 4 us -> 5.9 us  [the longest x3 3.99 us: local(): small = jnp.stack([s0, s1])]
where the time goes in v3:
time: 268 us
  Pallas kernels  244 us (91%)
  other arithmetic  11.3 us (4%)
  local copies, waits for them, and re-layouts  10.7 us (4%)
    pallas_call x1, Pallas kernels, two_blocks(): pl.pallas_call(whole_kernel, out_shape=(shape(T, D, dtype=BF), shape(T, D...  244 us

profile of v3, /device:TPU:1, one launch (start us, length us, event | category | flops | bytes accessed | tf_op | source)
XLA Modules:
  0.0 267.7 jit_solution(8324795680806723180)
XLA Ops:
  1.3 0.8 reshape.51
  2.1 0.8 concatenate.30
  2.8 0.1 pad.40.clone
  2.9 0.7 convert_element_type.19
  3.6 0.6 broadcast_in_dim.16.seg_row
  4.2 0.1 fusion.11
  4.3 0.1 pad_maximum_fusion.4
  4.3 0.1 fusion.9
  4.4 0.1 concatenate.35
  4.5 0.1 fusion.10
  4.6 0.1 concatenate.34
  4.7 1.3 select_maximum_fusion.heads
  6.0 0.7 slice.66
  6.8 0.6 pad.17.shard_b
  7.4 0.8 copy.53
  8.2 0.8 fusion.8
  9.2 0.1 pad_maximum_fusion.2
  9.3 0.1 copy.56
  9.5 0.2 reshape.53
  9.6 0.7 pad.18.shard_q
  10.3 0.8 copy.60.cols
  11.1 244.3 %two_blocks.1 = (bf16[384,768]{1,0:T(8,128)(2,1)}, bf16[384,768]{1,0:T(8,128)(2,1)}, f32[8,512]{1,0:T(8,128)}, f32[3,8,1536]{2,1,0:T(8,128)}, f32[8,128]{1,0:T(8...) custom-call(bf16[16,512]{1,0:T(8,128)(2,1)} %pad.17.shard_b, ...), custom_call_target="tpu_custom_call" | custom-call | tf_op jit(solution)/shard_map/two_blocks/pallas_call | solution.py:1092
  255.4 0.0 copy-start.1
  255.4 1.3 fusion.4
  256.7 1.2 pad_maximum_fusion.6
  258.0 1.2 pad_maximum_fusion.7
  259.2 1.4 fusion.3
  260.7 1.3 fusion.2
  261.9 0.0 copy-start
  261.9 0.8 pad_maximum_fusion.3
  262.7 1.0 pad_maximum_fusion
  263.8 0.2 copy.61
  263.9 0.2 reshape.54
  264.2 0.2 fusion.7
  264.4 0.7 squeeze.39
  265.1 0.1 squeeze.33
  265.3 0.1 squeeze.32
  265.4 0.7 pad_maximum_fusion.1
  266.1 0.0 copy-done.1
  266.1 0.8 copy.69
  266.9 0.0 copy-done
  266.9 0.8 copy.70
  (25 shorter events, 0.4 us)
Async XLA Ops:
  255.4 10.7 %copy-start.1 = (bf16[384,768]{1,0:T(8,128)(2,1)S(1)}, bf16[384,768]{1,0:T(8,128)(2,1)}, u32[]{:S(2)}) copy-start(bf16[384,768]{1,0:T(8,128)(2,1)} %get-tuple-element.54) | copy-start | bytes 1769476
  261.9 5.0 %copy-start = (bf16[384,768]{1,0:T(8,128)(2,1)S(1)}, bf16[384,768]{1,0:T(8,128)(2,1)}, u32[]{:S(2)}) copy-start(bf16[384,768]{1,0:T(8,128)(2,1)} %get-tuple-element.55) | copy-start | bytes 1769476

commit v4 on v3

--- a/solution.py
+++ b/solution.py
@@ -169,6 +169,18 @@
     flipped = jnp.transpose(total)
     for h in range(HEADS):
         log_t[h] = flipped[h : h + 1]
+
+
+def slot_columns(segments, counts, cols, seg_row):
+    seg = jnp.broadcast_to(segments[...].astype(F32), (8, T))
+    slot, row = iota((8, T), 1), iota((8, T), 0)
+    seg_row[...] = seg
+    lines = seg
+    for k in range(1, 4):
+        lines = jnp.where(row == k, jnp.where(slot >= k, pltpu.roll(seg, k, 1), -1.0), lines)
+        lines = jnp.where(row == k + 3, jnp.where(slot < T - k, pltpu.roll(seg, T - k, 1), -1.0), lines)
+    lines = jnp.where(row == 7, ones_where(slot < counts[...]), lines)
+    cols[...] = jnp.transpose(jnp.concatenate([lines, jnp.zeros((120, T), F32)], axis=0))
 
 
 def conv_masks(cols, masks):
@@ -654,13 +666,11 @@
         self.copies.got("p", color)
         cols = self.here(color)
 
-        def add(n, carry):
-            x, y = lax.div(n, 4), lax.rem(n, 4)
-            own = self.g[x, y, :, at.half(at.c, self.size, color, 2)]
-            self.h[x, y, :, cols] = plus(own, self.h[x, y, :, cols]).astype(BF)
+        def add(x, carry):
+            self.h[x, :, :, cols] += self.g[x, :, :, at.half(at.c, self.size, color, 2)]
             return carry
 
-        lax.fori_loop(0, 16, add, 0)
+        lax.fori_loop(0, 4, add, 0)
         for step in STEPS:
             self.copies.start("a", color, step)
 
@@ -951,10 +961,10 @@
     then("done")
 
 
-def whole_kernel(shard_b, shard_q, tokens, cotangent, heads, cols, seg_row,
+def whole_kernel(shard_b, shard_q, tokens, cotangent, a_log, dt_bias, head_skip, segments, counts,
                  output, tokens_grad, ob0, oq0, s0, ob1, oq1, s1, far_rb, far_values, far_gate, far_mixed,
                  wb0, wq0, wb1, wq1, gb1, gq1,
-                 second, grad, rb, values, gate, mixed, rows0, rows1, skip0, skip1, small0, small1, normed, square, local_sem, *scratch):
+                 second, grad, rb, values, gate, mixed, rows0, rows1, skip0, skip1, small0, small1, normed, square, local_sem, heads, cols, seg_row, *scratch):
     places = iter(scratch)
     take = lambda n: [next(places) for _ in range(n)]
     scan, backward = take(17), take(12)
@@ -989,55 +999,58 @@
         back.append(pltpu.make_async_copy(far, near, local_sem.at[4 + n]))
 
     steps = {
-        "f0.rows": [x0.near, y0.begin],
-        "f0.normed": [z0.begin, y0.near],
-        "f0.scores": [away[0].start, x0.far, z0.near, x0.end],
-        "f0.chunk0": [b1.begin, x1.begin],
+        "f0.rows": [y0.begin],
+        "f0.normed": [z0.begin],
+        "f0.scores": [away[0].start, x0.far, y0.near, x0.end],
+        "f0.chunk0": [b1.begin, x1.begin, z0.near],
         "f0.chunk1": [y0.far, b1.near, y0.end],
         "f0.chunk2": [y1.begin, x1.near, b1.far],
         "f0.chunk3": [z0.far, z1.begin, z0.end],
         "f0.chunk4": [b1.end, y1.near],
-        "f0.chunk5": [x1.far, z1.near],
-        "f0.yn": [each.start for each in away[1:]],
+        "f0.chunk5": [x1.far],
+        "f0.yn": [each.start for each in away[1:]] + [z1.near],
         "f1.begin": [away[0].wait],
-        "f1.scores": [each.wait for each in away[1:]] + [x1.end],
-        "f1.chunk0": [y1.far],
-        "f1.chunk1": [y1.end],
-        "f1.chunk2": [z1.far],
+        "f1.rows": [y1.far],
+        "f1.scores": [each.wait for each in away[1:]] + [x1.end, y1.end],
+        "f1.chunk1": [z1.far],
         "f1.chunk3": [z1.end],
         "b1.first": [each.copies.finish for each in groups + planes],
         "b1.chunk1": [X1.begin],
         "b1.chunk2": two(X1.pair),
-        "b1.chunk3": [Y1.begin] + two(X1.near),
-        "b1.chunk4": two(Y1.pair) + two(X1.far),
-        "b1.chunk5": [Z1.begin] + two(Y1.near) + [X1.along_z],
+        "b1.chunk3": [Y1.begin],
+        "b1.chunk4": two(X1.near) + two(Y1.pair),
+        "b1.chunk5": [Z1.begin] + two(X1.far),
         "b1.chunks": [each.start for each in back[1:]],
-        "b1.steps": two(Z1.pair) + [X1.along_core],
-        "b1.b_grad": [back[0].start, B1.begin] + two(Y1.far),
-        "b1.normed_back": two(B1.pair) + two(Z1.near) + [Y1.along_z, X1.end],
-        "b1.done": [each.wait for each in back] + two(B1.near) + two(Z1.far) + [Y1.along_core, S1.begin],
-        "b0.first": two(B1.far) + [Z1.along_z, Y1.end, S1.along_y],
-        "b0.scores": [B1.along_z, Z1.along_core, S1.along_z],
-        "b0.chunk0": [B1.along_core, Z1.end, S1.along_core],
-        "b0.chunk1": [B1.end, S1.end, X0.begin],
-        "b0.chunk2": two(X0.pair),
-        "b0.chunk3": [Y0.begin] + two(X0.near),
-        "b0.chunk4": two(Y0.pair) + two(X0.far),
-        "b0.chunk5": [Z0.begin] + two(Y0.near) + [X0.along_z],
-        "b0.steps": two(Z0.pair) + [X0.along_core],
-        "b0.b_grad": [B0.begin] + two(Y0.far),
-        "b0.normed_back": two(B0.pair) + two(Z0.near) + [Y0.along_z, X0.end],
+        "b1.b_grad": [back[0].start, B1.begin],
+        "b1.normed_back": two(Y1.near) + two(Z1.pair) + [X1.along_z],
+        "b1.done": [each.wait for each in back] + two(Y1.far) + [X1.along_core, S1.begin],
+        "b0.first": two(Z1.near) + [S1.along_y] + two(B1.pair) + [Y1.along_z, X1.end],
+        "b0.chunk0": two(Z1.far) + two(B1.near) + [Y1.along_core, S1.along_z],
+        "b0.chunk1": [X0.begin] + two(B1.far) + [Z1.along_z, Y1.end, S1.along_core],
+        "b0.chunk2": two(X0.pair) + [Z1.along_core, B1.along_z, S1.end],
+        "b0.chunk3": [Y0.begin, Z1.end, B1.along_core],
+        "b0.chunk4": two(X0.near) + two(Y0.pair) + [B1.end],
+        "b0.chunk5": [Z0.begin] + two(X0.far) + two(Y0.near) + [X0.along_z],
+        "b0.b_grad": [B0.begin] + two(Z0.pair) + two(Y0.far),
+        "b0.normed_back": two(B0.pair) + [Y0.along_z, X0.along_core],
         "b0.done": [S0.begin]
+        + two(Z0.near)
         + two(B0.near)
+        + [Y0.along_core, S0.along_y, X0.end]
         + two(Z0.far)
-        + [Y0.along_core, S0.along_y]
+        + [Z0.along_z]
         + two(B0.far)
-        + [Z0.along_z, S0.along_z, B0.along_z, Y0.end, Z0.along_core, S0.along_core, B0.along_core, Z0.end, B0.end, S0.end],
+        + [B0.along_z, S0.along_z, Z0.along_core, B0.along_core, S0.along_core, Y0.end, Z0.end, B0.end, S0.end],
     }
 
     ab.begin()
     for each in aq:
         each.begin()
+    heads[...] = jnp.zeros_like(heads)
+    for l in range(2):
+        for n, source in enumerate((a_log, dt_bias, head_skip)):
+            heads[l, n : n + 1, 0:HEADS] = source[l : l + 1, :]
+    slot_columns(segments, counts, cols, seg_row)
     conv_masks(cols, scan[4])
     scan[5][T:, :] = jnp.zeros((8, 128), F32)
     ab.end(wb0, wb1)
@@ -1045,9 +1058,10 @@
     aq[0].end(wq0.at[0], wq1.at[0])
     x0.begin()
     b0.near()
+    x0.near()
+    b0.far()
     for n in (1, 2):
         aq[n].end(wq0.at[n], wq1.at[n])
-    b0.far()
     b0.end()
 
     head0, head1 = heads.at[0], heads.at[1]
@@ -1081,7 +1095,7 @@
 SENDS = 4 * 7 + 8 * GatherPlane.SENDS + 8 * Reduce.SENDS + 2 * SmallReduce.SENDS
 
 
-def two_blocks(shards, tokens, cotangent, heads, cols, seg_row):
+def two_blocks(shards, *rest):
     outs = (shape(8, B), shape(3, 8, Q), shape(8, 128))
     wb, wq = pltpu.VMEM((4, 4, 48, B), BF), pltpu.VMEM((3, 4, 4, 48, Q), BF)
     buffers = []
@@ -1092,7 +1106,7 @@
     return pl.pallas_call(
         whole_kernel,
         out_shape=(shape(T, D, dtype=BF), shape(T, D, dtype=BF)) + outs + outs + (shape(T, USED),) + (shape(T, INNER),) * 3,
-        in_specs=vm(7),
+        in_specs=vm(9),
         out_specs=tuple(vm(8)) + (pl.BlockSpec(memory_space=pl.ANY),) * 4,
         scratch_shapes=[wb, wq] * 3
         + [pltpu.VMEM((T, D), F32)] * 2
@@ -1102,6 +1116,7 @@
         + [pltpu.VMEM((8, INNER), F32)] * 2
         + [pltpu.VMEM((8, CONV), F32)] * 2
         + [pltpu.VMEM((T, D), BF), pltpu.VMEM((T, 128), F32), pltpu.SemaphoreType.DMA((8,))]
+        + [pltpu.VMEM((2, 8, 128), F32), pltpu.VMEM((T, 128), F32), pltpu.VMEM((8, T), F32)]
         + scan_scratch()
         + backward_scratch()
         + buffers
@@ -1109,7 +1124,7 @@
         + dma_pair(SENDS),
         compiler_params=pltpu.CompilerParams(collective_id=0, has_side_effects=True, vmem_limit_bytes=LIMIT),
         name="two_blocks",
-    )(*shards, tokens, cotangent, heads, cols, seg_row)
+    )(*shards, *rest)
 
 
 def shards_of(norm_gain, in_weight, conv_weight, conv_bias, gate_gain, out_weight):
@@ -1123,15 +1138,10 @@
 
 
 def local(tokens, cotangent, segments, counts, norm_gain, in_weight, conv_weight, conv_bias, a_log, dt_bias, skip, gate_gain, out_weight):
-    seg = segments.astype(F32)
-    ahead = [jnp.concatenate([jnp.full((k,), -1.0, F32), seg[: T - k]]) for k in range(1, 4)]
-    after = [jnp.concatenate([seg[k:], jnp.full((k,), -1.0, F32)]) for k in range(1, 4)]
-    live = (jnp.arange(T, dtype=jnp.int32) < counts[0]).astype(F32)
-    cols = jnp.stack([seg] + ahead + after + [live], axis=1)
-    seg_row = seg[None, :]
-    heads = jnp.pad(jnp.stack([a_log, dt_bias, skip], axis=1), ((0, 0), (0, 5), (0, 128 - HEADS)))
     shards = shards_of(norm_gain, in_weight, conv_weight, conv_bias, gate_gain, out_weight)
-    output, tokens_grad, ob0, oq0, s0, ob1, oq1, s1, *_ = two_blocks(shards, tokens, cotangent, heads, cols, seg_row)
+    output, tokens_grad, ob0, oq0, s0, ob1, oq1, s1, *_ = two_blocks(
+        shards, tokens, cotangent, a_log, dt_bias, skip, segments.reshape(1, T), counts.reshape(1, 1)
+    )
     small = jnp.stack([s0, s1])
     sums = jnp.stack([oq0, oq1])[:, :, 0:6].reshape(2, 3, 6, 3, PART).transpose(3, 0, 2, 1, 4).reshape(3, 2, 6, INNER)
     return (

time: 268 us -> 241 us (0.90)
  Pallas kernels: 244 us -> 220 us
    pallas_call x1, Pallas kernels: 244 us -> 220 us  [two_blocks(): pl.pallas_call(whole_kernel, out_shape=(shape(T, D, dtype=BF), shape(T, D...]
where the time goes in v4:
time: 241 us; the launch traced here: 240 us
  Pallas kernels  220 us (91%)
  local copies, waits for them, and re-layouts  10.2 us (4%)
  other arithmetic  9.17 us (4%)
    pallas_call x1, Pallas kernels, two_blocks(): pl.pallas_call(whole_kernel, out_shape=(shape(T, D, dtype=BF), shape(T, D...  220 us

profile of v4, /device:TPU:1, one launch (start us, length us, event | category | flops | bytes accessed | tf_op | source)
XLA Modules:
  0.0 240.5 jit_solution(13177712921009436954)
XLA Ops:
  1.3 0.8 reshape.47
  2.1 0.8 concatenate.12
  2.8 0.1 pad.24.clone
  2.9 1.2 reshape.50.segments
  4.2 0.7 slice.48
  4.9 0.6 pad.9.shard_b
  5.6 0.8 copy.30
  6.4 0.8 fusion.8
  7.3 0.1 pad_maximum_fusion.2
  7.5 0.1 copy.33
  7.6 0.2 reshape.49
  7.8 0.7 pad.10.shard_q
  8.4 219.7 %two_blocks.1 = (bf16[384,768]{1,0:T(8,128)(2,1)}, bf16[384,768]{1,0:T(8,128)(2,1)}, f32[8,512]{1,0:T(8,128)}, f32[3,8,1536]{2,1,0:T(8,128)}, f32[8,128]{1,0:T(8...) custom-call(bf16[16,512]{1,0:T(8,128)(2,1)} %pad.9.shard_b, ...), custom_call_target="tpu_custom_call" | custom-call | tf_op jit(solution)/shard_map/two_blocks/pallas_call | solution.py:1106
  228.1 0.0 copy-start.1
  228.2 1.3 fusion.4
  229.5 1.2 pad_maximum_fusion.4
  230.7 1.2 pad_maximum_fusion.5
  232.0 1.4 fusion.3
  233.4 1.3 fusion.2
  234.7 0.0 copy-start
  234.7 0.8 pad_maximum_fusion.3
  235.5 1.0 pad_maximum_fusion
  236.5 0.2 copy.34
  236.7 0.2 reshape.52
  236.9 0.2 fusion.7
  237.1 0.7 squeeze.35
  237.9 0.1 squeeze.29
  238.0 0.1 squeeze.28
  238.1 0.7 pad_maximum_fusion.1
  238.8 0.0 copy-done.1
  238.8 0.8 copy.42
  239.6 0.0 copy-done
  239.6 0.8 copy.43
  (14 shorter events, 0.3 us)
Async XLA Ops:
  228.1 10.7 %copy-start.1 = (bf16[384,768]{1,0:T(8,128)(2,1)S(1)}, bf16[384,768]{1,0:T(8,128)(2,1)}, u32[]{:S(2)}) copy-start(bf16[384,768]{1,0:T(8,128)(2,1)} %get-tuple-element.46) | copy-start | bytes 1769476
  234.7 5.0 %copy-start = (bf16[384,768]{1,0:T(8,128)(2,1)S(1)}, bf16[384,768]{1,0:T(8,128)(2,1)}, u32[]{:S(2)}) copy-start(bf16[384,768]{1,0:T(8,128)(2,1)} %get-tuple-element.47) | copy-start | bytes 1769476

commit v5 on v4

--- a/solution.py
+++ b/solution.py
@@ -127,7 +127,7 @@
             rows[n : n + 1, tiles(128 * c, 128)] = jnp.sum(mine, axis=0, keepdims=True)
         return carry
 
-    lax.fori_loop(0, 14, body, 0)
+    lax.fori_loop(0, 14, body, 0, unroll=2)
     which = ones_where((iota((128, INNER), 1) >> 6) == iota((128, INNER), 0))
     skip[...] = exact(heads[...], which)
 
@@ -139,7 +139,7 @@
         body(pl.ds(pl.multiple_of(n * size, size), size))
         return carry
 
-    lax.fori_loop(0, count, step, 0)
+    lax.fori_loop(0, count, step, 0, unroll=3)
 
 
 def rms_normed(stream, gain, normed):
@@ -289,7 +289,7 @@
         y_ref[at, :] = nn(left, by_head(xd.astype(BF)))
         return carry
 
-    lax.fori_loop(0, 3, inside, 0)
+    lax.fori_loop(0, 3, inside, 0, unroll=True)
     for i in range(1, 3):
         at, before = block_rows(i), slice(0, 128 * i)
         edge = log_e[128 * i - 1 : 128 * i, :]
@@ -308,7 +308,7 @@
         square[at, :] += halves(u * u)
         return carry
 
-    lax.fori_loop(0, 3, gating, 0)
+    lax.fori_loop(0, 3, gating, 0, unroll=True)
 
 
 def gate_norm(rows, gated, square, yn):
@@ -334,7 +334,7 @@
         sum_d[at, :] += halves(u * dyn[at, here] * rows[5:6, here])
         return carry
 
-    lax.fori_loop(0, 3, body, 0)
+    lax.fori_loop(0, 3, body, 0, unroll=True)
 
 
 def norm_pull(sum_u, sum_d):
@@ -392,7 +392,7 @@
         dxd_ref[at, :] = dxd
         return carry
 
-    lax.fori_loop(0, 3, inside, 0)
+    lax.fori_loop(0, 3, inside, 0, unroll=True)
     put_chunk(gq, j, 0, gl_t, yn[...])
     put_chunk(gq, j, 1, norm_t, dgate[:, here])
     for i in range(1, 3):
@@ -426,7 +426,7 @@
         dxd_ref[at, :] = step_e[at, :] * dxd + skip[2:3, here] * dm_ref[at, :]
         return carry
 
-    lax.fori_loop(0, 3, outside, 0)
+    lax.fori_loop(0, 3, outside, 0, unroll=True)
     which = ones_where(4 * j + (iota((256, 128), 0) >> 6) == iota((256, 128), 1))
     skip_sum[8:16, 0:128] += exact(skips[...], which)
     for n in range(2):
@@ -670,7 +670,7 @@
             self.h[x, :, :, cols] += self.g[x, :, :, at.half(at.c, self.size, color, 2)]
             return carry
 
-        lax.fori_loop(0, 4, add, 0)
+        lax.fori_loop(0, 4, add, 0, unroll=True)
         for step in STEPS:
             self.copies.start("a", color, step)
 
@@ -685,7 +685,7 @@
             self.h[there] = (plus(self.h[there], self.rb[color, 0, n]) + plus(self.rb[color, 1, n], self.rb[color, 2, n])).astype(BF)
             return carry
 
-        lax.fori_loop(0, 4, add, 0)
+        lax.fori_loop(0, 4, add, 0, unroll=True)
         for step in STEPS:
             self.copies.start("d", color, step)
 

time: 241 us -> 225 us (0.934)
  Pallas kernels: 220 us -> 201 us
    pallas_call x1, Pallas kernels: 220 us -> 201 us  [two_blocks(): pl.pallas_call(whole_kernel, out_shape=(shape(T, D, dtype=BF), shape(T, D...]
where the time goes in v5:
time: 225 us; the launch traced here: 222 us
  Pallas kernels  201 us (89%)
  local copies, waits for them, and re-layouts  10.2 us (5%)
  other arithmetic  9.17 us (4%)
    pallas_call x1, Pallas kernels, two_blocks(): pl.pallas_call(whole_kernel, out_shape=(shape(T, D, dtype=BF), shape(T, D...  201 us

profile of v5, /device:TPU:1, one launch (start us, length us, event | category | flops | bytes accessed | tf_op | source)
XLA Modules:
  0.0 222.4 jit_solution(16967357806356676382)
XLA Ops:
  1.3 0.8 reshape.47
  2.1 0.8 concatenate.12
  2.8 0.1 pad.24.clone
  2.9 1.2 reshape.50.segments
  4.2 0.7 slice.48
  4.9 0.6 pad.9.shard_b
  5.6 0.8 copy.30
  6.4 0.8 fusion.8
  7.3 0.1 pad_maximum_fusion.2
  7.5 0.1 copy.33
  7.6 0.2 reshape.49
  7.8 0.7 pad.10.shard_q
  8.4 201.4 %two_blocks.1 = (bf16[384,768]{1,0:T(8,128)(2,1)}, bf16[384,768]{1,0:T(8,128)(2,1)}, f32[8,512]{1,0:T(8,128)}, f32[3,8,1536]{2,1,0:T(8,128)}, f32[8,128]{1,0:T(8...) custom-call(bf16[16,512]{1,0:T(8,128)(2,1)} %pad.9.shard_b, ...), custom_call_target="tpu_custom_call" | custom-call | tf_op jit(solution)/shard_map/two_blocks/pallas_call | solution.py:1106
  209.8 0.0 copy-start.1
  209.8 1.3 fusion.4
  211.1 1.2 pad_maximum_fusion.4
  212.4 1.2 pad_maximum_fusion.5
  213.6 1.4 fusion.3
  215.1 1.3 fusion.2
  216.4 0.0 copy-start
  216.4 0.8 pad_maximum_fusion.3
  217.2 1.0 pad_maximum_fusion
  218.2 0.2 copy.34
  218.3 0.2 reshape.52
  218.6 0.2 fusion.7
  218.8 0.7 squeeze.35
  219.6 0.1 squeeze.29
  219.7 0.1 squeeze.28
  219.8 0.7 pad_maximum_fusion.1
  220.5 0.0 copy-done.1
  220.5 0.8 copy.42
  221.3 0.0 copy-done
  221.3 0.8 copy.43
  (14 shorter events, 0.3 us)
Async XLA Ops:
  209.8 10.7 %copy-start.1 = (bf16[384,768]{1,0:T(8,128)(2,1)S(1)}, bf16[384,768]{1,0:T(8,128)(2,1)}, u32[]{:S(2)}) copy-start(bf16[384,768]{1,0:T(8,128)(2,1)} %get-tuple-element.46) | copy-start | bytes 1769476
  216.4 5.0 %copy-start = (bf16[384,768]{1,0:T(8,128)(2,1)S(1)}, bf16[384,768]{1,0:T(8,128)(2,1)}, u32[]{:S(2)}) copy-start(bf16[384,768]{1,0:T(8,128)(2,1)} %get-tuple-element.47) | copy-start | bytes 1769476

commit v6 on v5

--- a/solution.py
+++ b/solution.py
@@ -962,9 +962,9 @@
 
 
 def whole_kernel(shard_b, shard_q, tokens, cotangent, a_log, dt_bias, head_skip, segments, counts,
-                 output, tokens_grad, ob0, oq0, s0, ob1, oq1, s1, far_rb, far_values, far_gate, far_mixed,
+                 output, tokens_grad, in_grad, ob0, oq0, s0, ob1, oq1, s1, far_rb, far_values, far_gate, far_mixed,
                  wb0, wq0, wb1, wq1, gb1, gq1,
-                 second, grad, rb, values, gate, mixed, rows0, rows1, skip0, skip1, small0, small1, normed, square, local_sem, heads, cols, seg_row, *scratch):
+                 second, grad, rb, values, gate, mixed, rows0, rows1, skip0, skip1, small, normed, square, local_sem, heads, cols, seg_row, *scratch):
     places = iter(scratch)
     take = lambda n: [next(places) for _ in range(n)]
     scan, backward = take(17), take(12)
@@ -988,7 +988,7 @@
 
     X1, Y1, Z1, B1 = sums1 = sums_of(gb1, gq1, ob1, oq1)
     X0, Y0, Z0, B0 = sums0 = sums_of(wb1, wq1, ob0, oq0)
-    S1, S0 = [SmallReduce(at, *v, semaphores) for v in ((small1, s1, sums_by_axis), (small0, s0, sums_by_axis))]
+    S1, S0 = [SmallReduce(at, *v, semaphores) for v in ((small, s1, sums_by_axis), (small, s0, sums_by_axis))]
 
     def two(step):
         return [partial(step, 0), partial(step, 1)]
@@ -1080,16 +1080,22 @@
         grad[at, :] = value
 
     run_backward(grad, second, normed, wq1, wb1, head1, cols, seg_row, rows1, skip1, rb, values, gate, mixed,
-                 gq1, gb1, small1, keep, scan, backward, True, Plan("b1.", steps))
+                 gq1, gb1, small, keep, scan, backward, True, Plan("b1.", steps))
     rms_normed(tokens, rows0[6:7, 0:D], normed)
 
     def give(at, value):
         tokens_grad[at, :] = value.astype(BF)
 
     run_backward(grad, tokens, normed, wq0, wb0, head0, cols, seg_row, rows0, skip0, rb, values, gate, mixed,
-                 wq1, wb1, small0, give, scan, backward, False, Plan("b0.", steps))
+                 wq1, wb1, small, give, scan, backward, False, Plan("b0.", steps))
     for each in sums1 + sums0 + [S1, S0]:
         each.copies.finish()
+    for l, (ob, oq) in enumerate(((ob0, oq0), (ob1, oq1))):
+        for n in parts:
+            for kind in (1, 2):
+                start = INNER * (kind - 1) + PART * n
+                in_grad[l, :, start : start + PART] = oq[n, 0:6, PART * kind : PART * (kind + 1)]
+        in_grad[l, :, 2 * INNER :] = ob[0:6, 0 : STEP + HEADS]
 
 
 SENDS = 4 * 7 + 8 * GatherPlane.SENDS + 8 * Reduce.SENDS + 2 * SmallReduce.SENDS
@@ -1105,16 +1111,16 @@
         buffers += narrow_scratch(width)
     return pl.pallas_call(
         whole_kernel,
-        out_shape=(shape(T, D, dtype=BF), shape(T, D, dtype=BF)) + outs + outs + (shape(T, USED),) + (shape(T, INNER),) * 3,
+        out_shape=(shape(T, D, dtype=BF), shape(T, D, dtype=BF), shape(2, 6, 2 * INNER + STEP + HEADS)) + outs + outs + (shape(T, USED),) + (shape(T, INNER),) * 3,
         in_specs=vm(9),
-        out_specs=tuple(vm(8)) + (pl.BlockSpec(memory_space=pl.ANY),) * 4,
+        out_specs=tuple(vm(9)) + (pl.BlockSpec(memory_space=pl.ANY),) * 4,
         scratch_shapes=[wb, wq] * 3
         + [pltpu.VMEM((T, D), F32)] * 2
         + [pltpu.VMEM((T, USED), F32)]
         + [pltpu.VMEM((T, INNER), F32)] * 3
         + [pltpu.VMEM((8, CONV), F32)] * 2
         + [pltpu.VMEM((8, INNER), F32)] * 2
-        + [pltpu.VMEM((8, CONV), F32)] * 2
+        + [pltpu.VMEM((8, CONV), F32)]
         + [pltpu.VMEM((T, D), BF), pltpu.VMEM((T, 128), F32), pltpu.SemaphoreType.DMA((8,))]
         + [pltpu.VMEM((2, 8, 128), F32), pltpu.VMEM((T, 128), F32), pltpu.VMEM((8, T), F32)]
         + scan_scratch()
@@ -1139,23 +1145,23 @@
 
 def local(tokens, cotangent, segments, counts, norm_gain, in_weight, conv_weight, conv_bias, a_log, dt_bias, skip, gate_gain, out_weight):
     shards = shards_of(norm_gain, in_weight, conv_weight, conv_bias, gate_gain, out_weight)
-    output, tokens_grad, ob0, oq0, s0, ob1, oq1, s1, *_ = two_blocks(
+    output, tokens_grad, in_grad, _, oq0, s0, _, oq1, s1, *_ = two_blocks(
         shards, tokens, cotangent, a_log, dt_bias, skip, segments.reshape(1, T), counts.reshape(1, 1)
     )
     small = jnp.stack([s0, s1])
-    sums = jnp.stack([oq0, oq1])[:, :, 0:6].reshape(2, 3, 6, 3, PART).transpose(3, 0, 2, 1, 4).reshape(3, 2, 6, INNER)
+    outs = jnp.stack([oq0, oq1])[:, :, 0:6, 0:PART]
     return (
         output,
         tokens_grad,
         small[:, 6, 0:6],
-        jnp.concatenate([sums[1], sums[2], jnp.stack([ob0, ob1])[:, 0:6, 0 : STEP + HEADS]], axis=2),
+        in_grad,
         jnp.transpose(small[:, 1:5, 0:14], (0, 2, 1)),
         small[:, 0, 0:14],
         small[:, 7, 0:24],
         small[:, 7, 32:56],
         small[:, 7, 64:88],
         small[:, 5, 0:12],
-        jnp.transpose(sums[0], (0, 2, 1)),
+        jnp.transpose(outs.transpose(0, 2, 1, 3).reshape(2, 6, INNER), (0, 2, 1)),
     )
 
 

time: 225 us -> 225 us (level)
    unnamed x6 -> x5, local copies, waits for them, and re-layouts: 1.64 us -> 4.42 us
where the time goes in v6:
time: 225 us; the launch traced here: 222 us
  Pallas kernels  201 us (89%)
  local copies, waits for them, and re-layouts  12.1 us (5%)
  other arithmetic  7.45 us (3%)
    pallas_call x1, Pallas kernels, two_blocks(): pl.pallas_call(whole_kernel, out_shape=(shape(T, D, dtype=BF), shape(T, D...  201 us

profile of v6, /device:TPU:1, one launch (start us, length us, event | category | flops | bytes accessed | tf_op | source)
XLA Modules:
  0.0 222.4 jit_solution(5024325115752989236)
XLA Ops:
  1.3 0.8 reshape.40
  2.1 0.8 concatenate.9
  2.8 0.1 pad.19.clone
  2.9 1.2 reshape.43.segments
  4.2 0.7 slice.33
  4.9 0.6 pad.9.shard_b
  5.5 0.8 copy.27
  6.4 0.8 fusion.8
  7.3 0.1 pad_maximum_fusion
  7.5 0.1 copy.30
  7.6 0.2 reshape.42
  7.7 0.7 pad.10.shard_q
  8.4 201.0 %two_blocks.1 = (bf16[384,768]{1,0:T(8,128)(2,1)}, bf16[384,768]{1,0:T(8,128)(2,1)}, f32[2,6,3352]{2,1,0:T(8,128)}, f32[8,512]{1,0:T(8,128)}, f32[3,8,1536]{2,1,...) custom-call(bf16[16,512]{1,0:T(8,128)(2,1)} %pad.9.shard_b, ...), custom_call_target="tpu_custom_call" | custom-call | tf_op jit(solution)/shard_map/two_blocks/pallas_call | solution.py:1112
  209.5 0.0 copy-start
  209.5 1.3 fusion.5
  210.8 1.2 pad_maximum_fusion.2
  212.0 1.2 pad_maximum_fusion.3
  213.3 1.4 fusion.4
  214.7 1.3 fusion.3
  216.0 0.8 fusion
  216.8 0.1 copy.31
  216.8 0.7 reshape.45
  217.5 1.7 copy.32
  219.2 1.9 copy.36
  221.2 0.0 copy-done
  221.2 0.8 copy.37
  (10 shorter events, 0.2 us)
Async XLA Ops:
  209.5 11.7 %copy-start = (bf16[384,768]{1,0:T(8,128)(2,1)S(1)}, bf16[384,768]{1,0:T(8,128)(2,1)}, u32[]{:S(2)}) copy-start(bf16[384,768]{1,0:T(8,128)(2,1)} %get-tuple-element.64) | copy-start | bytes 1769476
